TPU v7x, 32 devices: a whole 2x2x4 slice. The times are simulated.
32 devices in a mesh: rep: 2 (over y), ep: 4 (over z), dp: 4 (over x, core).
Axes of the slice: x: 2, y: 2, z: 4, core: 2. Of those that a mesh axis runs over, the one named last changes fastest.
Arguments:
- tokens: bfloat16 [256, 4096], P(('rep', 'ep', 'dp')), parts along dimension 0, may hold values from -6 to 6
- expert_ids: int32 [256, 8], P(('rep', 'ep', 'dp')), parts along dimension 0, may hold values from 0 to 63, all different within a row; in each aligned block of 8 rows (0 to 7, 8 to 15, ...) at most 2 rows name the same one
- gate_scores: float32 [256, 8], P(('rep', 'ep', 'dp')), parts along dimension 0, may hold values from 0.05 to 1
- gate_weight: bfloat16 [64, 4096, 768], P('ep', None, 'dp'), may hold values from -0.09375 to 0.09375
- up_weight: bfloat16 [64, 4096, 768], P('ep', None, 'dp'), may hold values from -0.09375 to 0.09375
- down_weight: bfloat16 [64, 768, 4096], P('ep', 'dp'), may hold values from -0.21875 to 0.21875
Outputs:
- moe_output: bfloat16 [256, 4096], P(('rep', 'ep', 'dp')), parts along dimension 0
There are 2 independent parts, one for each index of `rep`. A program takes and returns all parts, laid end to end along the dimension named above; an argument that names none is the same for every part. Nothing has to cross between parts.
Inputs may be any that keep to these rules, and one draw needn't show every extreme that they name: `expert_ids`: the 8 ids of a token are distinct. Among the 8 tokens of one device no expert is named by more than 2 tokens, and in every draw some device names some expert exactly 2 times.
All inputs are finite; a program needn't handle non-finite values.
Results may differ from a plain program's by a relative error of at most 0.011.
Values may be sent and summed in bfloat16 or wider, within the bound.
No kernel may reach another device: no remote copies, remote signals or barrier semaphores. Data moves between devices by JAX's collectives and lax.ppermute only.
A program may use at most 192 MiB of HBM per device.

v0:
```python
import jax
import jax.numpy as jnp
from jax import lax
from jax.sharding import PartitionSpec as P

CAP = 2


def local(tokens, expert_ids, gate_scores, gate_weight, up_weight, down_weight):
    token_count, model_width = tokens.shape
    top_count = expert_ids.shape[1]
    ep_count = lax.axis_size("ep")
    local_experts = gate_weight.shape[0]
    expert_total = local_experts * ep_count
    flat_ids = expert_ids.reshape(-1)
    one_hot = (flat_ids[:, None] == jnp.arange(expert_total, dtype=jnp.int32)[None, :]).astype(
        jnp.int32
    )
    slot_rank = jnp.sum(jnp.cumsum(one_hot, axis=0) * one_hot, axis=1) - 1
    slot_index = flat_ids * CAP + slot_rank
    assign_map = (
        slot_index[:, None] == jnp.arange(expert_total * CAP, dtype=jnp.int32)[None, :]
    ).astype(jnp.bfloat16)
    token_map = jnp.sum(
        assign_map.reshape(token_count, top_count, expert_total * CAP).astype(jnp.float32), axis=1
    )
    outgoing = jnp.dot(
        token_map.T.astype(jnp.bfloat16), tokens, preferred_element_type=jnp.float32
    ).astype(jnp.bfloat16)
    outgoing = outgoing.reshape(ep_count, local_experts, CAP, model_width)
    grouped = lax.all_gather(outgoing[None], "dp", axis=0, tiled=True)
    arrived = lax.all_to_all(grouped, "ep", split_axis=1, concat_axis=1, tiled=True)
    gate_acts = jnp.einsum(
        "gsecd,edf->gsecf", arrived, gate_weight, preferred_element_type=jnp.float32
    )
    up_acts = jnp.einsum("gsecd,edf->gsecf", arrived, up_weight, preferred_element_type=jnp.float32)
    hidden = (jax.nn.silu(gate_acts) * up_acts).astype(jnp.bfloat16)
    partial_value = jnp.einsum(
        "gsecf,efd->gsecd", hidden, down_weight, preferred_element_type=jnp.float32
    )
    partial_rounded = partial_value.astype(jnp.bfloat16)
    summed = lax.psum_scatter(partial_rounded, "dp", scatter_dimension=0, tiled=True).astype(
        jnp.float32
    )
    expert_out = lax.all_to_all(
        summed.astype(jnp.bfloat16), "ep", split_axis=1, concat_axis=1, tiled=True
    )
    expert_out = expert_out.reshape(expert_total * CAP, model_width)
    per_assign = jnp.dot(assign_map, expert_out, preferred_element_type=jnp.float32)
    weights = gate_scores / jnp.sum(gate_scores, axis=1, keepdims=True)
    combined = jnp.sum(
        per_assign.reshape(token_count, top_count, model_width) * weights[:, :, None], axis=1
    )
    return combined.astype(jnp.bfloat16)


def solution(mesh):
    in_specs = (
        P(("rep", "ep", "dp"), None),
        P(("rep", "ep", "dp"), None),
        P(("rep", "ep", "dp"), None),
        P("ep", None, "dp"),
        P("ep", None, "dp"),
        P("ep", "dp", None),
    )
    out_specs = P(("rep", "ep", "dp"), None)
    return jax.shard_map(local, mesh=mesh, in_specs=in_specs, out_specs=out_specs, check_vma=False)
```

profile of v0, /device:TPU:0, one launch (start us, length us, event | category | flops | bytes accessed | tf_op | source)
XLA Modules:
  0.0 283.0 jit_solution(1270929106040251512)
XLA Ops:
  6.5 0.0 copy-start
  6.5 0.0 all-gather.2.cloned.1.call-start
  6.5 0.8 eq.51
  7.3 0.1 fusion.20
  7.4 0.1 reduce_window_sum.11
  7.5 0.2 select_reduce_fusion
  7.7 0.1 sub.7
  7.8 0.7 multiply_add_fusion
  8.5 0.1 fusion.24
  8.6 0.0 copy-done
  8.6 0.5 convolution_convert_fusion
  9.1 1.5 broadcast_in_dim_reshape.4
  10.6 0.0 all-gather.2.cloned.1.call-update
  10.6 0.0 reduce-scatter.2.cloned.1.call-start
  10.7 37.3 %all-gather.2.cloned.1.call-done = bf16[4,4,16,2,4096]{4,3,0,2,1:T(2,128)(2,1)} async-done(((bf16[1,4,16,2,4096]{4,3,0,2,1:T(2,128)(2,1)}), bf16[4,4,16,2,4096]{4,3,0,2,1:T(2,128)(2,1)}) %all-gather.2.cloned.1.call-update) | async-done | bytes 4194320 | tf_op jit(solution)/shard_map/all_gather | solution.py:31
  47.9 99.5 %all_to_all.10 = bf16[4,4,16,2,4096]{4,3,0,2,1:T(2,128)(2,1)} all-to-all(bf16[4,4,16,2,4096]{4,3,0,2,1:T(2,128)(2,1)} %all-gather.2.cloned.1.call-done), channel_id=1, replica_groups=mesh['rep'=2,'ep'=4,'dp'=4] {'ep'}, dimensions={1} | all-to-all | bytes 8388608 | tf_op jit(solution)/shard_map/all_to_all | solution.py:32
  147.5 14.3 %fusion.2 = f32[16,4,4,2,192]{4,3,2,1,0:T(2,128)S(1)} fusion(bf16[16,4096,192]{1,2,0:T(8,128)(2,1)} %param.10, bf16[4,4,16,2,4096]{4,3,0,2,1:T(2,128)(2,1)} %all_to_all.10), kind=kOutput, calls=%fused_computation.2 | convolution fusion | flops 805306368 | bytes 29753344 | tf_op jit(solution)/shard_map/gsecd,edf->gsecf/dot_general | solution.py:36
  161.8 14.5 %fusion.4 = f32[16,4,4,2,192]{4,3,2,1,0:T(2,128)S(1)} fusion(bf16[16,4096,192]{1,2,0:T(8,128)(2,1)} %param.9, bf16[4,4,16,2,4096]{4,3,0,2,1:T(2,128)(2,1)} %all_to_all.10), kind=kOutput, calls=%fused_computation.4 | convolution fusion | flops 805306368 | bytes 29753344 | tf_op jit(solution)/shard_map/gsecd,edf->gsecf/dot_general | solution.py:33
  176.2 0.6 fusion.15
  176.9 14.9 %fusion.9 = bf16[4,4,16,2,4096]{4,1,3,0,2:T(4,128)(2,1)} fusion(bf16[16,192,4096]{2,1,0:T(8,128)(2,1)} %param.11, bf16[4,4,16,2,192]{4,2,3,1,0:T(8,128)(2,1)S(1)} %fusion.15), kind=kOutput, calls=%fused_computation.7 | convolution fusion | flops 807403520 | bytes 29556736 | tf_op jit(solution)/shard_map/gsecf,efd->gsecd/dot_general | solution.py:38
  191.7 6.4 %copy.27 = bf16[4,4,16,2,4096]{4,2,3,1,0:T(8,128)(2,1)} copy(bf16[4,4,16,2,4096]{4,1,3,0,2:T(4,128)(2,1)} %fusion.9) | data formatting | bytes 8388608 | tf_op jit(solution)/shard_map/convert_element_type | solution.py:41
  198.2 0.0 copy-start.2
  198.2 0.0 reduce-scatter.2.cloned.1.call-update
  198.2 0.0 copy-start.1
  198.2 42.8 %reduce-scatter.2.cloned.1.call-done = bf16[1,4,16,2,4096]{4,2,3,1,0:T(8,128)(2,1)} async-done(((bf16[4,4,16,2,4096]{4,2,3,1,0:T(8,128)(2,1)}), bf16[1,4,16,2,4096]{4,2,3,1,0:T(8,128)(2,1)}) %reduce-scatter.2.cloned.1.call-update) | async-done | bytes 1048592 | tf_op jit(solution)/shard_map/reduce_scatter | solution.py:42
  241.0 3.3 %copy.28 = bf16[1,4,16,2,4096]{4,3,0,2,1:T(2,128)(2,1)} copy(bf16[1,4,16,2,4096]{4,2,3,1,0:T(8,128)(2,1)} %reduce-scatter.2.cloned.1.call-done) | data formatting | bytes 2097152 | tf_op jit(solution)/shard_map/reduce_scatter | solution.py:42
  244.3 4.6 %all-to-all-start.1 = ((bf16[1,4,16,2,4096]{4,3,0,2,1:T(2,128)(2,1)}), bf16[1,4,16,2,4096]{4,3,0,2,1:T(2,128)(2,1)S(1)}, u32[]{:S(2)}, u32[]{:S(2)}) async-start(bf16[1,4,16,2,4096]{4,3,0,2,1:T(2,128)(2,1)} %copy.28), calls=%async_computation.2 | async-start | bytes 2097152 | tf_op jit(solution)/shard_map/all_to_all | solution.py:45
  248.9 0.0 copy-done.2
  248.9 0.1 reduce_sum.41
  249.0 0.1 broadcast_divide_fusion
  249.1 25.5 %all-to-all-done.1 = bf16[1,4,16,2,4096]{4,3,0,2,1:T(2,128)(2,1)S(1)} async-done(((bf16[1,4,16,2,4096]{4,3,0,2,1:T(2,128)(2,1)}), bf16[1,4,16,2,4096]{4,3,0,2,1:T(2,128)(2,1)S(1)}, u32[]{:S(2)}, u32[]{:S(2)}) %all-to-all-start.1) | async-done | bytes 1048608 | tf_op jit(solution)/shard_map/all_to_all | solution.py:45
  274.6 0.4 reshape.55
  275.1 1.1 fusion.14
  276.2 0.0 copy-done.1
  (1 shorter events, 0.0 us)
Async XLA Ops:
  6.5 2.0 copy-start
  6.5 41.4 %all-gather.2.cloned.1.call-start = ((), (), s32[]{:S(2)}) async-start(), calls=%async_computation.3 | async-start | bytes 5242880 | tf_op jit(solution)/shard_map/all_gather | solution.py:31
  10.6 230.4 %reduce-scatter.2.cloned.1.call-start = ((), (), s32[]{:S(2)}) async-start(), calls=%async_computation.4 | async-start | bytes 5242880 | tf_op jit(solution)/shard_map/reduce_scatter | solution.py:42
  198.2 50.7 %copy-start.2 = (f32[8,8]{1,0:T(8,128)S(1)}, f32[8,8]{1,0:T(8,128)}, u32[]{:S(2)}) copy-start(f32[8,8]{1,0:T(8,128)} %param.8) | copy-start | bytes 772
  198.2 78.0 %copy-start.1 = (bf16[8,4096]{1,0:T(8,128)(2,1)S(1)}, bf16[8,4096]{1,0:T(8,128)(2,1)}, u32[]{:S(2)}) copy-start(bf16[8,4096]{1,0:T(8,128)(2,1)} %param.6) | copy-start | bytes 196612
  244.3 30.3 %all-to-all-start.1 = ((bf16[1,4,16,2,4096]{4,3,0,2,1:T(2,128)(2,1)}), bf16[1,4,16,2,4096]{4,3,0,2,1:T(2,128)(2,1)S(1)}, u32[]{:S(2)}, u32[]{:S(2)}) async-start(bf16[1,4,16,2,4096]{4,3,0,2,1:T(2,128)(2,1)} %copy.28), calls=%async_computation.2 | async-start | bytes 2097152 | tf_op jit(solution)/shard_map/all_to_all | solution.py:45
Sparse Core Ops, SparseCore 0:
  10.7 37.1 all-gather.1
  198.3 42.6 reduce-scatter.1
where the time goes:
time: 283 us
  waiting for transfers between devices  106 us (37%)
  blocking collectives  99.5 us (35%)
  matrix products  45.2 us (16%)
  between operations  13.5 us (5%)
  local copies, waits for them, and re-layouts  12.6 us (4%)
  starting transfers between devices  4.65 us (2%)
    all_to_all x1, blocking collectives, local(): lax.all_to_all(grouped, 'ep', split_axis=1, concat_axis=1, tiled=True)  99.5 us
    reduce_scatter x1, waiting for transfers between devices, local(): lax.psum_scatter(partial_rounded, 'dp', scatter_dimension=0, tiled=True)  42.8 us
    all_gather x1, waiting for transfers between devices, local(): grouped = lax.all_gather(outgoing[None], 'dp', axis=0, tiled=True)  37.3 us
    all_to_all x1, waiting for transfers between devices, local(): lax.all_to_all(summed.astype(jnp.bfloat16), 'ep', split_axis=1, concat_ax...  25.5 us
    dot_general x1, matrix products, local(): jnp.einsum('gsecf,efd->gsecd', hidden, down_weight, preferred_element_typ...  14.9 us
    dot_general x1, matrix products, local(): jnp.einsum('gsecd,edf->gsecf', arrived, gate_weight, preferred_element_ty...  14.5 us
    dot_general x1, matrix products, local(): jnp.einsum('gsecd,edf->gsecf', arrived, up_weight, preferred_element_type...  14.3 us
    convert_element_type x1, local copies, waits for them, and re-layouts, local(): partial_rounded = partial_value.astype(jnp.bfloat16)  6.42 us
  transfers between devices with their start and end apart: 3, of which 3 were waited for; matrix products, arithmetic and copies ran while one was open for 0% of the time, Pallas kernels for 0%

commit v1 on v0

v1 whole, which is shorter than its diff:
```python
import functools

import jax
import jax.numpy as jnp
from jax import lax
from jax.experimental import pallas as pl
from jax.experimental.pallas import tpu as pltpu
from jax.sharding import PartitionSpec as P

BF16 = jnp.bfloat16
F32 = jnp.float32
NT = (((1,), (1,)), ((), ()))


def add_up(*parts):
    total = parts[0].astype(F32)
    for part in parts[1:]:
        total = total + part.astype(F32)
    return total.astype(BF16)


def hop(x, ep_count, dp_count, ep_mask, dp_mask):
    pairs = [
        (i, ((i // dp_count) ^ ep_mask) * dp_count + ((i % dp_count) ^ dp_mask))
        for i in range(ep_count * dp_count)
    ]
    return lax.ppermute(x, ("ep", "dp"), pairs)


def ep_order(ep_count):
    return sorted(range(1, ep_count), key=lambda m: (-m.bit_length(), m))


def gather_rows(x, ep_count, dp_count):
    send = functools.partial(hop, ep_count=ep_count, dp_count=dp_count)
    blocks = {(0, 0): x}
    for m in ep_order(ep_count):
        blocks[m, 0] = send(x, ep_mask=m, dp_mask=0)
    for d in range(2, dp_count, 2):
        for m in [0] + ep_order(ep_count):
            blocks[m, d] = send(blocks[m, 0], ep_mask=0, dp_mask=d)
    near = jnp.concatenate(
        [blocks[m, d] for d in range(0, dp_count, 2) for m in range(ep_count)], axis=0
    )
    return jnp.concatenate([near, send(near, ep_mask=0, dp_mask=1)], axis=0)


def scatter_rows(y, ep_count, dp_count):
    send = functools.partial(hop, ep_count=ep_count, dp_count=dp_count)
    rows = y.shape[0]
    y = y.reshape(2, dp_count // 2, ep_count, rows // (ep_count * dp_count), y.shape[1])
    y = add_up(y[0], send(y[1], ep_mask=0, dp_mask=1))
    y = add_up(y[0], *[send(y[d // 2], ep_mask=0, dp_mask=d) for d in range(2, dp_count, 2)])
    return add_up(y[0], *[send(y[m], ep_mask=m, dp_mask=0) for m in ep_order(ep_count)])


def hidden_kernel(width, expert_total, first_ref, x_ref, gate_ref, up_ref, h_ref):
    model_width = gate_ref.shape[1]
    step = gate_ref.shape[0]
    x = x_ref[:, :model_width]
    gate_acts = lax.dot_general(x, gate_ref[...], NT, preferred_element_type=F32)
    up_acts = lax.dot_general(x, up_ref[...], NT, preferred_element_type=F32)
    shape = (x_ref.shape[1] - model_width, step)
    row = lax.broadcasted_iota(jnp.int32, shape, 0)
    column = lax.broadcasted_iota(jnp.int32, shape, 1)
    expert = first_ref[0] + pl.program_id(0) * (step // width) + column // width
    spread = (lax.rem(row, expert_total) == expert).astype(F32).astype(BF16)
    weight = jnp.dot(x_ref[:, model_width:], spread, preferred_element_type=F32)
    h_ref[...] = (jax.nn.silu(gate_acts) * up_acts * weight).astype(BF16)


def down_kernel(h_ref, down_ref, y_ref):
    y_ref[...] = jnp.dot(h_ref[...], down_ref[...], preferred_element_type=F32).astype(BF16)


def experts(rows, gate, up, down, first, width, expert_total):
    token_count = rows.shape[0]
    units, model_width = gate.shape
    step = 2 * width if units % (2 * width) == 0 else width
    hidden = pl.pallas_call(
        functools.partial(hidden_kernel, width, expert_total),
        grid=(units // step,),
        in_specs=[
            pl.BlockSpec(memory_space=pltpu.SMEM),
            pl.BlockSpec(rows.shape, lambda i: (0, 0)),
            pl.BlockSpec((step, model_width), lambda i: (i, 0)),
            pl.BlockSpec((step, model_width), lambda i: (i, 0)),
        ],
        out_specs=pl.BlockSpec((token_count, step), lambda i: (0, i)),
        out_shape=jax.ShapeDtypeStruct((token_count, units), BF16),
        compiler_params=pltpu.CompilerParams(vmem_limit_bytes=32 << 20),
        name="hidden",
    )(first, rows, gate, up)
    piece = 512
    return pl.pallas_call(
        down_kernel,
        grid=(model_width // piece,),
        in_specs=[
            pl.BlockSpec((token_count, units), lambda i: (0, 0)),
            pl.BlockSpec((units, piece), lambda i: (0, i)),
        ],
        out_specs=pl.BlockSpec((token_count, piece), lambda i: (0, i)),
        out_shape=jax.ShapeDtypeStruct((token_count, model_width), BF16),
        compiler_params=pltpu.CompilerParams(vmem_limit_bytes=32 << 20),
        name="down",
    )(hidden, down)


def experts_plain(rows, gate, up, down, first, width, expert_total):
    units, model_width = gate.shape
    x = rows[:, :model_width]
    gate_acts = lax.dot_general(x, gate, NT, preferred_element_type=F32)
    up_acts = lax.dot_general(x, up, NT, preferred_element_type=F32)
    row = jnp.arange(rows.shape[1] - model_width, dtype=jnp.int32)[:, None]
    expert = first[0] + jnp.arange(units, dtype=jnp.int32)[None, :] // width
    spread = (row % expert_total == expert).astype(BF16)
    weight = jnp.dot(rows[:, model_width:], spread, preferred_element_type=F32)
    hidden = (jax.nn.silu(gate_acts) * up_acts * weight).astype(BF16)
    return jnp.dot(hidden, down, preferred_element_type=F32).astype(BF16)


def local(tokens, expert_ids, gate_scores, gate_weight, up_weight, down_weight):
    model_width = tokens.shape[1]
    ep_count = lax.axis_size("ep")
    dp_count = lax.axis_size("dp")
    local_experts, _, width = gate_weight.shape
    expert_total = local_experts * ep_count
    gate = jnp.swapaxes(gate_weight, 1, 2).reshape(local_experts * width, model_width)
    up = jnp.swapaxes(up_weight, 1, 2).reshape(local_experts * width, model_width)
    down = down_weight.reshape(local_experts * width, model_width)
    first = (lax.axis_index("ep") * local_experts).astype(jnp.int32).reshape(1)

    weights = gate_scores / jnp.sum(gate_scores, axis=1, keepdims=True)
    named = expert_ids[:, :, None] == jnp.arange(expert_total, dtype=jnp.int32)[None, None, :]
    dense = jnp.sum(jnp.where(named, weights[:, :, None], 0.0), axis=1)
    high = lax.reduce_precision(dense, 8, 7)
    message = jnp.concatenate([tokens, high.astype(BF16), (dense - high).astype(BF16)], axis=1)

    powers = all(n & (n - 1) == 0 for n in (ep_count, dp_count))
    if powers and ep_count <= 8 and 2 <= dp_count <= 8:
        rows = gather_rows(message, ep_count, dp_count)
        partial = experts(rows, gate, up, down, first, width, expert_total)
        return scatter_rows(partial, ep_count, dp_count)
    rows = lax.all_gather(message, ("ep", "dp"), axis=0, tiled=True)
    partial = experts_plain(rows, gate, up, down, first, width, expert_total)
    return lax.psum_scatter(partial, ("ep", "dp"), scatter_dimension=0, tiled=True)


def solution(mesh):
    in_specs = (
        P(("rep", "ep", "dp"), None),
        P(("rep", "ep", "dp"), None),
        P(("rep", "ep", "dp"), None),
        P("ep", None, "dp"),
        P("ep", None, "dp"),
        P("ep", "dp", None),
    )
    out_specs = P(("rep", "ep", "dp"), None)
    return jax.shard_map(local, mesh=mesh, in_specs=in_specs, out_specs=out_specs, check_vma=False)
```

time: 283 us -> 75.1 us (0.27)
  blocking collectives: 99.5 us -> 0 us
  waiting for transfers between devices: 106 us -> 20.7 us
  matrix products: 45.2 us -> 0 us
  Pallas kernels: 0 us -> 33.4 us
  between operations: 13.5 us -> 0.13 us
  starting transfers between devices: 4.65 us -> 16.1 us
  local copies, waits for them, and re-layouts: 12.6 us -> 1.21 us
    all_to_all x1 -> x0, blocking collectives: 99.5 us -> none  [local(): lax.all_to_all(grouped, 'ep', split_axis=1, concat_axis=1, tiled=True)]
    dot_general x5 -> x0, matrix products: 45.2 us -> none  [the longest x1 14.9 us: local(): jnp.einsum('gsecf,efd->gsecd', hidden, down_weight, preferred_element_typ...]
    reduce_scatter x1 -> x0, waiting for transfers between devices: 42.8 us -> none  [local(): lax.psum_scatter(partial_rounded, 'dp', scatter_dimension=0, tiled=True)]
    all_gather x1 -> x0, waiting for transfers between devices: 37.3 us -> none  [local(): grouped = lax.all_gather(outgoing[None], 'dp', axis=0, tiled=True)]
    pallas_call x0 -> x2, Pallas kernels: none -> 33.4 us  [the longest x1 21.8 us: experts(): pl.pallas_call(functools.partial(hidden_kernel, width, expert_total), gri...]
    all_to_all x1 -> x0, waiting for transfers between devices: 25.5 us -> none  [local(): lax.all_to_all(summed.astype(jnp.bfloat16), 'ep', split_axis=1, concat_ax...]
    ppermute x0 -> x13, waiting for transfers between devices: none -> 20.7 us  [hop(): return lax.ppermute(x, ('ep', 'dp'), pairs)]
    ppermute x0 -> x13, starting transfers between devices: none -> 16.1 us  [hop(): return lax.ppermute(x, ('ep', 'dp'), pairs)]
  transfers between devices with their start and end apart: 3 -> 13, of which waited for: 3 -> 9; matrix products, arithmetic and copies ran while one was open for 0% -> 0% of each run, Pallas kernels for 0% -> 0%
where the time goes in v1:
time: 75.1 us; the launch traced here: 74.8 us
  Pallas kernels  33.4 us (44%)
  waiting for transfers between devices  20.7 us (28%)
  starting transfers between devices  16.1 us (21%)
  other arithmetic  3.2 us (4%)
  local copies, waits for them, and re-layouts  1.21 us (2%)
    pallas_call x1, Pallas kernels, experts(): pl.pallas_call(functools.partial(hidden_kernel, width, expert_total), gri...  21.8 us
    ppermute x13, waiting for transfers between devices, hop(): return lax.ppermute(x, ('ep', 'dp'), pairs)  20.7 us
    ppermute x13, starting transfers between devices, hop(): return lax.ppermute(x, ('ep', 'dp'), pairs)  16.1 us
    pallas_call x1, Pallas kernels, experts(): pl.pallas_call(down_kernel, grid=(model_width // piece,), in_specs=[pl.Bl...  11.6 us
  transfers between devices with their start and end apart: 13, of which 9 were waited for; matrix products, arithmetic and copies ran while one was open for 0% of the time, Pallas kernels for 0%

profile of v1, /device:TPU:0, one launch (start us, length us, event | category | flops | bytes accessed | tf_op | source)
XLA Modules:
  0.0 74.8 jit_solution(3083871338694727208)
XLA Ops:
  0.0 0.8 %reduce_sum.18 = f32[8]{0:T(128)S(1)} reduce(f32[8,8]{1,0:T(8,128)} %param.8, f32[]{:T(128)} %constant.8.clone.1), dimensions={1}, to_apply=%region_0.0 | reduce | flops 56 | bytes 292 | tf_op jit(solution)/shard_map/reduce_sum | solution.py:133
  0.8 0.8 %broadcast_divide_fusion = f32[8,8]{1,0:T(8,128)S(1)} fusion(f32[8,8]{1,0:T(8,128)} %param.8, f32[8]{0:T(128)S(1)} %reduce_sum.18), kind=kLoop, calls=%fused_computation.36 | loop fusion | flops 64 | bytes 544 | tf_op jit(solution)/shard_map/div | solution.py:133
  1.6 0.8 %select_reduce_fusion = f32[8,64]{1,0:T(8,128)S(1)} fusion(f32[8,8]{1,0:T(8,128)S(1)} %broadcast_divide_fusion, s32[8,8]{1,0:T(8,128)} %param.7), kind=kLoop, calls=%fused_computation.31 | loop fusion | flops 11776 | bytes 2560 | tf_op jit(solution)/shard_map/reduce_sum | solution.py:135
  2.4 0.9 %concatenate.10 = bf16[8,4224]{1,0:T(8,128)(2,1)S(1)} concatenate(bf16[8,4096]{1,0:T(8,128)(2,1)} %param.6, bf16[8,64]{1,0:T(8,128)(2,1)S(1)} %get-tuple-element.27, bf16[8,64]{1,0:T(8,128)(2,1)S(1)} %get-tuple-element.26), dimensions={1} | concatenate | bytes 135168 | tf_op jit(solution)/shard_map/concatenate | solution.py:137
  3.3 3.0 %collective-permute-start = (bf16[8,4224]{1,0:T(8,128)(2,1)S(1)}, bf16[8,4224]{1,0:T(8,128)(2,1)S(1)}, u32[]{:S(2)}, u32[]{:S(2)}) collective-permute-start(bf16[8,4224]{1,0:T(8,128)(2,1)S(1)} %concatenate.10), channel_id=1, source_target_pairs={{0,4},{1,5},{2,6},{3,7},{4,0},{5,1},{6,2},{7,3},{8,12},{9,13},{10,... | collective-permute-start | bytes 202760 | tf_op jit(solution)/shard_map/ppermute | solution.py:27
  6.3 2.6 %collective-permute-start.1 = (bf16[8,4224]{1,0:T(8,128)(2,1)S(1)}, bf16[8,4224]{1,0:T(8,128)(2,1)S(1)}, u32[]{:S(2)}, u32[]{:S(2)}) collective-permute-start(bf16[8,4224]{1,0:T(8,128)(2,1)S(1)} %concatenate.10), channel_id=1, source_target_pairs={{0,8},{1,9},{2,10},{3,11},{4,12},{5,13},{6,14},{7,15},{8,0},{9,1},... | collective-permute-start | bytes 202760 | tf_op jit(solution)/shard_map/ppermute | solution.py:27
  8.9 0.0 collective-permute-start.2
  8.9 1.7 %collective-permute-start.3 = (bf16[8,4224]{1,0:T(8,128)(2,1)S(1)}, bf16[8,4224]{1,0:T(8,128)(2,1)S(1)}, u32[]{:S(2)}, u32[]{:S(2)}) collective-permute-start(bf16[8,4224]{1,0:T(8,128)(2,1)S(1)} %concatenate.10), channel_id=1, source_target_pairs={{0,2},{1,3},{2,0},{3,1},{4,6},{5,7},{6,4},{7,5},{8,10},{9,11},{10,... | collective-permute-start | bytes 202760 | tf_op jit(solution)/shard_map/ppermute | solution.py:27
  10.6 0.0 collective-permute-done
  10.6 0.4 collective-permute-start.4
  11.0 2.7 %collective-permute-done.1 = bf16[8,4224]{1,0:T(8,128)(2,1)S(1)} collective-permute-done((bf16[8,4224]{1,0:T(8,128)(2,1)S(1)}, bf16[8,4224]{1,0:T(8,128)(2,1)S(1)}, u32[]{:S(2)}, u32[]{:S(2)}) %collective-permute-start.1) | collective-permute-done | bytes 67616 | tf_op jit(solution)/shard_map/ppermute | solution.py:27
  13.7 1.5 %collective-permute-start.5 = (bf16[8,4224]{1,0:T(8,128)(2,1)S(1)}, bf16[8,4224]{1,0:T(8,128)(2,1)S(1)}, u32[]{:S(2)}, u32[]{:S(2)}) collective-permute-start(bf16[8,4224]{1,0:T(8,128)(2,1)S(1)} %collective-permute-done.1), channel_id=1, source_target_pairs={{0,2},{1,3},{2,0},{3,1},{4,6},{5,7},{6,4},{7,5},{8,10},{9,11},{10,... | collective-permute-start | bytes 202760 | tf_op jit(solution)/shard_map/ppermute | solution.py:27
  15.2 0.0 collective-permute-done.2
  15.2 1.4 %collective-permute-start.6 = (bf16[8,4224]{1,0:T(8,128)(2,1)S(1)}, bf16[8,4224]{1,0:T(8,128)(2,1)S(1)}, u32[]{:S(2)}, u32[]{:S(2)}) collective-permute-start(bf16[8,4224]{1,0:T(8,128)(2,1)S(1)} %collective-permute-done.2), channel_id=1, source_target_pairs={{0,2},{1,3},{2,0},{3,1},{4,6},{5,7},{6,4},{7,5},{8,10},{9,11},{10,... | collective-permute-start | bytes 202760 | tf_op jit(solution)/shard_map/ppermute | solution.py:27
  16.6 0.0 collective-permute-done.3
  16.7 0.0 collective-permute-done.4
  16.7 1.3 %collective-permute-done.5 = bf16[8,4224]{1,0:T(8,128)(2,1)S(1)} collective-permute-done((bf16[8,4224]{1,0:T(8,128)(2,1)S(1)}, bf16[8,4224]{1,0:T(8,128)(2,1)S(1)}, u32[]{:S(2)}, u32[]{:S(2)}) %collective-permute-start.5) | collective-permute-done | bytes 67616 | tf_op jit(solution)/shard_map/ppermute | solution.py:27
  18.0 1.5 %collective-permute-done.6 = bf16[8,4224]{1,0:T(8,128)(2,1)S(1)} collective-permute-done((bf16[8,4224]{1,0:T(8,128)(2,1)S(1)}, bf16[8,4224]{1,0:T(8,128)(2,1)S(1)}, u32[]{:S(2)}, u32[]{:S(2)}) %collective-permute-start.6) | collective-permute-done | bytes 67616 | tf_op jit(solution)/shard_map/ppermute | solution.py:27
  19.5 0.1 collective-permute-start.7
  19.6 1.9 %collective-permute-done.7 = bf16[64,4224]{1,0:T(8,128)(2,1)S(1)} collective-permute-done((bf16[64,4224]{1,0:T(8,128)(2,1)S(1)}, bf16[64,4224]{1,0:T(8,128)(2,1)S(1)}, u32[]{:S(2)}, u32[]{:S(2)}) %collective-permute-start.7) | collective-permute-done | bytes 540704 | tf_op jit(solution)/shard_map/ppermute | solution.py:27
  21.6 21.8 %hidden.1.h_ref = bf16[128,3072]{1,0:T(8,128)(2,1)S(1)} custom-call(s32[1]{0:T(128)} %bitcast.first_ref, bf16[128,4224]{1,0:T(8,128)(2,1)S(1)} %constant_dynamic-update-slice_fusion.8.x_ref, bf16[3072,4096]{1,0:T(8,128)(2,1)} %bitcast.29, bf16[3072,4096]{1,0:T(8,128)(2,1)} %bitcast.30), custom_call_target="tpu_custom_call" | custom-call | tf_op jit(solution)/shard_map/hidden/pallas_call | solution.py:80
  43.4 11.6 %down.1 = bf16[128,4096]{1,0:T(8,128)(2,1)S(1)} custom-call(bf16[128,3072]{1,0:T(8,128)(2,1)S(1)} %hidden.1.h_ref, bf16[3072,4096]{1,0:T(8,128)(2,1)} %bitcast.31), custom_call_target="tpu_custom_call" | custom-call | tf_op jit(solution)/shard_map/down/pallas_call | solution.py:95
  55.0 0.1 fusion.6
  55.1 0.2 collective-permute-start.8
  55.3 1.8 %collective-permute-done.8 = bf16[2,4,8,4096]{3,2,1,0:T(8,128)(2,1)S(1)} collective-permute-done((bf16[2,4,8,4096]{3,2,1,0:T(8,128)(2,1)S(1)}, bf16[2,4,8,4096]{3,2,1,0:T(8,128)(2,1)S(1)}, u32[]{:S(2)}, u32[]{:S(2)}) %collective-permute-start.8) | collective-permute-done | bytes 524320 | tf_op jit(solution)/shard_map/ppermute | solution.py:27
  57.1 0.1 fusion
  57.2 1.5 %collective-permute-start.9 = (bf16[4,8,4096]{2,1,0:T(8,128)(2,1)S(1)}, bf16[4,8,4096]{2,1,0:T(8,128)(2,1)S(1)}, u32[]{:S(2)}, u32[]{:S(2)}) collective-permute-start(bf16[4,8,4096]{2,1,0:T(8,128)(2,1)S(1)} %slice_bitcast_fusion), channel_id=1, source_target_pairs={{0,2},{1,3},{2,0},{3,1},{4,6},{5,7},{6,4},{7,5},{8,10},{9,11},{10,... | collective-permute-start | bytes 786440 | tf_op jit(solution)/shard_map/ppermute | solution.py:27
  58.7 7.0 %collective-permute-done.9 = bf16[4,8,4096]{2,1,0:T(8,128)(2,1)S(1)} collective-permute-done((bf16[4,8,4096]{2,1,0:T(8,128)(2,1)S(1)}, bf16[4,8,4096]{2,1,0:T(8,128)(2,1)S(1)}, u32[]{:S(2)}, u32[]{:S(2)}) %collective-permute-start.9) | collective-permute-done | bytes 262176 | tf_op jit(solution)/shard_map/ppermute | solution.py:27
  65.6 0.1 fusion.1
  65.7 1.6 %collective-permute-start.10 = (bf16[8,4096]{1,0:T(8,128)(2,1)S(1)}, bf16[8,4096]{1,0:T(8,128)(2,1)S(1)}, u32[]{:S(2)}, u32[]{:S(2)}) collective-permute-start(bf16[8,4096]{1,0:T(8,128)(2,1)S(1)} %get-tuple-element.7), channel_id=1, source_target_pairs={{0,8},{1,9},{2,10},{3,11},{4,12},{5,13},{6,14},{7,15},{8,0},{9,1},... | collective-permute-start | bytes 196616 | tf_op jit(solution)/shard_map/ppermute | solution.py:27
  67.3 1.7 %collective-permute-start.11 = (bf16[8,4096]{1,0:T(8,128)(2,1)S(1)}, bf16[8,4096]{1,0:T(8,128)(2,1)S(1)}, u32[]{:S(2)}, u32[]{:S(2)}) collective-permute-start(bf16[8,4096]{1,0:T(8,128)(2,1)S(1)} %get-tuple-element.9), channel_id=1, source_target_pairs={{0,12},{1,13},{2,14},{3,15},{4,8},{5,9},{6,10},{7,11},{8,4},{9,5},... | collective-permute-start | bytes 196616 | tf_op jit(solution)/shard_map/ppermute | solution.py:27
  69.1 0.5 collective-permute-start.12
  69.6 3.2 %collective-permute-done.10 = bf16[8,4096]{1,0:T(8,128)(2,1)S(1)} collective-permute-done((bf16[8,4096]{1,0:T(8,128)(2,1)S(1)}, bf16[8,4096]{1,0:T(8,128)(2,1)S(1)}, u32[]{:S(2)}, u32[]{:S(2)}) %collective-permute-start.10) | collective-permute-done | bytes 65568 | tf_op jit(solution)/shard_map/ppermute | solution.py:27
  72.8 0.7 collective-permute-done.11
  73.6 0.6 collective-permute-done.12
  74.1 0.7 fusion.4
  (12 shorter events, 0.2 us)
Async XLA Ops:
  3.3 7.3 %collective-permute-start = (bf16[8,4224]{1,0:T(8,128)(2,1)S(1)}, bf16[8,4224]{1,0:T(8,128)(2,1)S(1)}, u32[]{:S(2)}, u32[]{:S(2)}) collective-permute-start(bf16[8,4224]{1,0:T(8,128)(2,1)S(1)} %concatenate.10), channel_id=1, source_target_pairs={{0,4},{1,5},{2,6},{3,7},{4,0},{5,1},{6,2},{7,3},{8,12},{9,13},{10,... | collective-permute-start | bytes 202760 | tf_op jit(solution)/shard_map/ppermute | solution.py:27
  6.3 7.4 %collective-permute-start.1 = (bf16[8,4224]{1,0:T(8,128)(2,1)S(1)}, bf16[8,4224]{1,0:T(8,128)(2,1)S(1)}, u32[]{:S(2)}, u32[]{:S(2)}) collective-permute-start(bf16[8,4224]{1,0:T(8,128)(2,1)S(1)} %concatenate.10), channel_id=1, source_target_pairs={{0,8},{1,9},{2,10},{3,11},{4,12},{5,13},{6,14},{7,15},{8,0},{9,1},... | collective-permute-start | bytes 202760 | tf_op jit(solution)/shard_map/ppermute | solution.py:27
  8.9 6.3 %collective-permute-start.2 = (bf16[8,4224]{1,0:T(8,128)(2,1)S(1)}, bf16[8,4224]{1,0:T(8,128)(2,1)S(1)}, u32[]{:S(2)}, u32[]{:S(2)}) collective-permute-start(bf16[8,4224]{1,0:T(8,128)(2,1)S(1)} %concatenate.10), channel_id=1, source_target_pairs={{0,12},{1,13},{2,14},{3,15},{4,8},{5,9},{6,10},{7,11},{8,4},{9,5},... | collective-permute-start | bytes 202760 | tf_op jit(solution)/shard_map/ppermute | solution.py:27
  8.9 7.7 %collective-permute-start.3 = (bf16[8,4224]{1,0:T(8,128)(2,1)S(1)}, bf16[8,4224]{1,0:T(8,128)(2,1)S(1)}, u32[]{:S(2)}, u32[]{:S(2)}) collective-permute-start(bf16[8,4224]{1,0:T(8,128)(2,1)S(1)} %concatenate.10), channel_id=1, source_target_pairs={{0,2},{1,3},{2,0},{3,1},{4,6},{5,7},{6,4},{7,5},{8,10},{9,11},{10,... | collective-permute-start | bytes 202760 | tf_op jit(solution)/shard_map/ppermute | solution.py:27
  10.6 6.0 %collective-permute-start.4 = (bf16[8,4224]{1,0:T(8,128)(2,1)S(1)}, bf16[8,4224]{1,0:T(8,128)(2,1)S(1)}, u32[]{:S(2)}, u32[]{:S(2)}) collective-permute-start(bf16[8,4224]{1,0:T(8,128)(2,1)S(1)} %collective-permute-done), channel_id=1, source_target_pairs={{0,2},{1,3},{2,0},{3,1},{4,6},{5,7},{6,4},{7,5},{8,10},{9,11},{10,... | collective-permute-start | bytes 202760 | tf_op jit(solution)/shard_map/ppermute | solution.py:27
  13.7 4.3 %collective-permute-start.5 = (bf16[8,4224]{1,0:T(8,128)(2,1)S(1)}, bf16[8,4224]{1,0:T(8,128)(2,1)S(1)}, u32[]{:S(2)}, u32[]{:S(2)}) collective-permute-start(bf16[8,4224]{1,0:T(8,128)(2,1)S(1)} %collective-permute-done.1), channel_id=1, source_target_pairs={{0,2},{1,3},{2,0},{3,1},{4,6},{5,7},{6,4},{7,5},{8,10},{9,11},{10,... | collective-permute-start | bytes 202760 | tf_op jit(solution)/shard_map/ppermute | solution.py:27
  15.2 4.3 %collective-permute-start.6 = (bf16[8,4224]{1,0:T(8,128)(2,1)S(1)}, bf16[8,4224]{1,0:T(8,128)(2,1)S(1)}, u32[]{:S(2)}, u32[]{:S(2)}) collective-permute-start(bf16[8,4224]{1,0:T(8,128)(2,1)S(1)} %collective-permute-done.2), channel_id=1, source_target_pairs={{0,2},{1,3},{2,0},{3,1},{4,6},{5,7},{6,4},{7,5},{8,10},{9,11},{10,... | collective-permute-start | bytes 202760 | tf_op jit(solution)/shard_map/ppermute | solution.py:27
  19.5 2.0 %collective-permute-start.7 = (bf16[64,4224]{1,0:T(8,128)(2,1)S(1)}, bf16[64,4224]{1,0:T(8,128)(2,1)S(1)}, u32[]{:S(2)}, u32[]{:S(2)}) collective-permute-start(bf16[64,4224]{1,0:T(8,128)(2,1)S(1)} %get-tuple-element.10), channel_id=1, source_target_pairs={{0,1},{1,0},{2,3},{3,2},{4,5},{5,4},{6,7},{7,6},{8,9},{9,8},{10,11... | collective-permute-start | bytes 1622024 | tf_op jit(solution)/shard_map/ppermute | solution.py:27
  55.1 2.0 %collective-permute-start.8 = (bf16[2,4,8,4096]{3,2,1,0:T(8,128)(2,1)S(1)}, bf16[2,4,8,4096]{3,2,1,0:T(8,128)(2,1)S(1)}, u32[]{:S(2)}, u32[]{:S(2)}) collective-permute-start(bf16[2,4,8,4096]{3,2,1,0:T(8,128)(2,1)S(1)} %bitcast.33), channel_id=1, source_target_pairs={{0,1},{1,0},{2,3},{3,2},{4,5},{5,4},{6,7},{7,6},{8,9},{9,8},{10,11... | collective-permute-start | bytes 1572872 | tf_op jit(solution)/shard_map/ppermute | solution.py:27
  57.2 8.4 %collective-permute-start.9 = (bf16[4,8,4096]{2,1,0:T(8,128)(2,1)S(1)}, bf16[4,8,4096]{2,1,0:T(8,128)(2,1)S(1)}, u32[]{:S(2)}, u32[]{:S(2)}) collective-permute-start(bf16[4,8,4096]{2,1,0:T(8,128)(2,1)S(1)} %slice_bitcast_fusion), channel_id=1, source_target_pairs={{0,2},{1,3},{2,0},{3,1},{4,6},{5,7},{6,4},{7,5},{8,10},{9,11},{10,... | collective-permute-start | bytes 786440 | tf_op jit(solution)/shard_map/ppermute | solution.py:27
  65.7 7.1 %collective-permute-start.10 = (bf16[8,4096]{1,0:T(8,128)(2,1)S(1)}, bf16[8,4096]{1,0:T(8,128)(2,1)S(1)}, u32[]{:S(2)}, u32[]{:S(2)}) collective-permute-start(bf16[8,4096]{1,0:T(8,128)(2,1)S(1)} %get-tuple-element.7), channel_id=1, source_target_pairs={{0,8},{1,9},{2,10},{3,11},{4,12},{5,13},{6,14},{7,15},{8,0},{9,1},... | collective-permute-start | bytes 196616 | tf_op jit(solution)/shard_map/ppermute | solution.py:27
  67.3 6.2 %collective-permute-start.11 = (bf16[8,4096]{1,0:T(8,128)(2,1)S(1)}, bf16[8,4096]{1,0:T(8,128)(2,1)S(1)}, u32[]{:S(2)}, u32[]{:S(2)}) collective-permute-start(bf16[8,4096]{1,0:T(8,128)(2,1)S(1)} %get-tuple-element.9), channel_id=1, source_target_pairs={{0,12},{1,13},{2,14},{3,15},{4,8},{5,9},{6,10},{7,11},{8,4},{9,5},... | collective-permute-start | bytes 196616 | tf_op jit(solution)/shard_map/ppermute | solution.py:27
  69.1 5.0 %collective-permute-start.12 = (bf16[8,4096]{1,0:T(8,128)(2,1)S(1)}, bf16[8,4096]{1,0:T(8,128)(2,1)S(1)}, u32[]{:S(2)}, u32[]{:S(2)}) collective-permute-start(bf16[8,4096]{1,0:T(8,128)(2,1)S(1)} %get-tuple-element.8), channel_id=1, source_target_pairs={{0,4},{1,5},{2,6},{3,7},{4,0},{5,1},{6,2},{7,3},{8,12},{9,13},{10,... | collective-permute-start | bytes 196616 | tf_op jit(solution)/shard_map/ppermute | solution.py:27

commit v2 on v1

--- a/solution.py
+++ b/solution.py
@@ -54,56 +54,88 @@
     return add_up(y[0], *[send(y[m], ep_mask=m, dp_mask=0) for m in ep_order(ep_count)])
 
 
-def hidden_kernel(width, expert_total, first_ref, x_ref, gate_ref, up_ref, h_ref):
-    model_width = gate_ref.shape[1]
-    step = gate_ref.shape[0]
-    x = x_ref[:, :model_width]
-    gate_acts = lax.dot_general(x, gate_ref[...], NT, preferred_element_type=F32)
-    up_acts = lax.dot_general(x, up_ref[...], NT, preferred_element_type=F32)
-    shape = (x_ref.shape[1] - model_width, step)
-    row = lax.broadcasted_iota(jnp.int32, shape, 0)
-    column = lax.broadcasted_iota(jnp.int32, shape, 1)
-    expert = first_ref[0] + pl.program_id(0) * (step // width) + column // width
-    spread = (lax.rem(row, expert_total) == expert).astype(F32).astype(BF16)
-    weight = jnp.dot(x_ref[:, model_width:], spread, preferred_element_type=F32)
-    h_ref[...] = (jax.nn.silu(gate_acts) * up_acts * weight).astype(BF16)
+def experts_kernel(width, expert_total, step, piece, slots, down_slots,
+                   first_ref, x_ref, gate_ref, up_ref, down_ref, y_ref,
+                   h_ref, gate_buf, up_buf, down_buf, gate_sem, up_sem, down_sem):
+    units, model_width = gate_ref.shape
+    steps, pieces = units // step, model_width // piece
 
+    def rows_copy(ref, buf, sem, i):
+        return pltpu.make_async_copy(
+            ref.at[pl.ds(i * step, step), :], buf.at[i % slots], sem.at[i % slots]
+        )
 
-def down_kernel(h_ref, down_ref, y_ref):
-    y_ref[...] = jnp.dot(h_ref[...], down_ref[...], preferred_element_type=F32).astype(BF16)
+    def gate_copy(i):
+        return rows_copy(gate_ref, gate_buf, gate_sem, i)
+
+    def up_copy(i):
+        return rows_copy(up_ref, up_buf, up_sem, i)
+
+    def down_copy(j):
+        slot = j % down_slots
+        return pltpu.make_async_copy(
+            down_ref.at[:, pl.ds(j * piece, piece)], down_buf.at[slot], down_sem.at[slot]
+        )
+
+    for i in range(min(slots, steps)):
+        gate_copy(i).start()
+        up_copy(i).start()
+    begun = 0
+    for i in range(steps):
+        x = x_ref[:, :model_width]
+        rows = slice(i * step, (i + 1) * step)
+        shape = (step, x_ref.shape[1] - model_width)
+        expert = first_ref[0] + (lax.broadcasted_iota(jnp.int32, shape, 0) + i * step) // width
+        column = lax.rem(lax.broadcasted_iota(jnp.int32, shape, 1), expert_total)
+        spread = (column == expert).astype(F32).astype(BF16)
+        weight = lax.dot_general(spread, x_ref[:, model_width:], NT, preferred_element_type=F32)
+        gate_copy(i).wait()
+        gate_acts = lax.dot_general(gate_buf[i % slots], x, NT, preferred_element_type=F32)
+        gate_acts = jax.nn.silu(gate_acts) * weight
+        up_copy(i).wait()
+        up_acts = lax.dot_general(up_buf[i % slots], x, NT, preferred_element_type=F32)
+        h_ref[:, rows] = (gate_acts * up_acts).T.astype(BF16)
+        if i + slots < steps:
+            gate_copy(i + slots).start()
+            up_copy(i + slots).start()
+        else:
+            goal = min(pieces, down_slots) * (i + slots - steps + 1) // slots
+            for j in range(begun, goal):
+                down_copy(j).start()
+            begun = max(begun, goal)
+    for j in range(pieces):
+        down_copy(j).wait()
+        y_ref[:, j * piece : (j + 1) * piece] = jnp.dot(
+            h_ref[...], down_buf[j % down_slots], preferred_element_type=F32
+        ).astype(BF16)
+        if j + down_slots < pieces:
+            down_copy(j + down_slots).start()
 
 
 def experts(rows, gate, up, down, first, width, expert_total):
     token_count = rows.shape[0]
     units, model_width = gate.shape
     step = 2 * width if units % (2 * width) == 0 else width
-    hidden = pl.pallas_call(
-        functools.partial(hidden_kernel, width, expert_total),
-        grid=(units // step,),
-        in_specs=[
-            pl.BlockSpec(memory_space=pltpu.SMEM),
-            pl.BlockSpec(rows.shape, lambda i: (0, 0)),
-            pl.BlockSpec((step, model_width), lambda i: (i, 0)),
-            pl.BlockSpec((step, model_width), lambda i: (i, 0)),
+    piece, slots, down_slots = 512, 3, 6
+    whole = pl.BlockSpec(memory_space=pltpu.VMEM)
+    away = pl.BlockSpec(memory_space=pl.ANY)
+    return pl.pallas_call(
+        functools.partial(experts_kernel, width, expert_total, step, piece, slots, down_slots),
+        in_specs=[pl.BlockSpec(memory_space=pltpu.SMEM), whole, away, away, away],
+        out_specs=whole,
+        out_shape=jax.ShapeDtypeStruct((token_count, model_width), BF16),
+        scratch_shapes=[
+            pltpu.VMEM((token_count, units), BF16),
+            pltpu.VMEM((slots, step, model_width), BF16),
+            pltpu.VMEM((slots, step, model_width), BF16),
+            pltpu.VMEM((down_slots, units, piece), BF16),
+            pltpu.SemaphoreType.DMA((slots,)),
+            pltpu.SemaphoreType.DMA((slots,)),
+            pltpu.SemaphoreType.DMA((down_slots,)),
         ],
-        out_specs=pl.BlockSpec((token_count, step), lambda i: (0, i)),
-        out_shape=jax.ShapeDtypeStruct((token_count, units), BF16),
-        compiler_params=pltpu.CompilerParams(vmem_limit_bytes=32 << 20),
-        name="hidden",
-    )(first, rows, gate, up)
-    piece = 512
-    return pl.pallas_call(
-        down_kernel,
-        grid=(model_width // piece,),
-        in_specs=[
-            pl.BlockSpec((token_count, units), lambda i: (0, 0)),
-            pl.BlockSpec((units, piece), lambda i: (0, i)),
-        ],
-        out_specs=pl.BlockSpec((token_count, piece), lambda i: (0, i)),
-        out_shape=jax.ShapeDtypeStruct((token_count, model_width), BF16),
-        compiler_params=pltpu.CompilerParams(vmem_limit_bytes=32 << 20),
-        name="down",
-    )(hidden, down)
+        compiler_params=pltpu.CompilerParams(vmem_limit_bytes=44 << 20),
+        name="experts",
+    )(first, rows, gate, up, down)
 
 
 def experts_plain(rows, gate, up, down, first, width, expert_total):

time: 75.1 us -> 77.6 us (1.033)
  Pallas kernels: 33.4 us -> 36 us
    pallas_call x2 -> x1, Pallas kernels: 33.4 us -> 36 us  [experts(): pl.pallas_call(functools.partial(experts_kernel, width, expert_total, ste...]
  transfers between devices with their start and end apart: 13 -> 13, of which waited for: 9 -> 8; matrix products, arithmetic and copies ran while one was open for 0% -> 0% of each run, Pallas kernels for 0% -> 0%
where the time goes in v2:
time: 77.6 us; the launch traced here: 77.4 us
  Pallas kernels  36 us (46%)
  waiting for transfers between devices  20.7 us (27%)
  starting transfers between devices  16.1 us (21%)
  other arithmetic  3.2 us (4%)
  local copies, waits for them, and re-layouts  1.21 us (2%)
    pallas_call x1, Pallas kernels, experts(): pl.pallas_call(functools.partial(experts_kernel, width, expert_total, ste...  36 us
    ppermute x13, waiting for transfers between devices, hop(): return lax.ppermute(x, ('ep', 'dp'), pairs)  20.7 us
    ppermute x13, starting transfers between devices, hop(): return lax.ppermute(x, ('ep', 'dp'), pairs)  16.1 us
  transfers between devices with their start and end apart: 13, of which 8 were waited for; matrix products, arithmetic and copies ran while one was open for 0% of the time, Pallas kernels for 0%

profile of v2, /device:TPU:0, one launch (start us, length us, event | category | flops | bytes accessed | tf_op | source)
XLA Modules:
  0.0 77.4 jit_solution(3146967681640888703)
XLA Ops:
  0.0 0.8 %reduce_sum.18 = f32[8]{0:T(128)S(1)} reduce(f32[8,8]{1,0:T(8,128)} %param.8, f32[]{:T(128)} %constant.8.clone.1), dimensions={1}, to_apply=%region_0.0 | reduce | flops 56 | bytes 292 | tf_op jit(solution)/shard_map/reduce_sum | solution.py:165
  0.8 0.8 broadcast_divide_fusion
  1.6 0.8 %select_reduce_fusion = f32[8,64]{1,0:T(8,128)S(1)} fusion(f32[8,8]{1,0:T(8,128)S(1)} %broadcast_divide_fusion, s32[8,8]{1,0:T(8,128)} %param.7), kind=kLoop, calls=%fused_computation.31 | loop fusion | flops 11776 | bytes 2560 | tf_op jit(solution)/shard_map/reduce_sum | solution.py:167
  2.4 0.9 %concatenate.10 = bf16[8,4224]{1,0:T(8,128)(2,1)S(1)} concatenate(bf16[8,4096]{1,0:T(8,128)(2,1)} %param.6, bf16[8,64]{1,0:T(8,128)(2,1)S(1)} %get-tuple-element.27, bf16[8,64]{1,0:T(8,128)(2,1)S(1)} %get-tuple-element.26), dimensions={1} | concatenate | bytes 135168 | tf_op jit(solution)/shard_map/concatenate | solution.py:169
  3.3 3.0 %collective-permute-start = (bf16[8,4224]{1,0:T(8,128)(2,1)S(1)}, bf16[8,4224]{1,0:T(8,128)(2,1)S(1)}, u32[]{:S(2)}, u32[]{:S(2)}) collective-permute-start(bf16[8,4224]{1,0:T(8,128)(2,1)S(1)} %concatenate.10), channel_id=1, source_target_pairs={{0,4},{1,5},{2,6},{3,7},{4,0},{5,1},{6,2},{7,3},{8,12},{9,13},{10,... | collective-permute-start | bytes 202760 | tf_op jit(solution)/shard_map/ppermute | solution.py:27
  6.3 2.6 %collective-permute-start.1 = (bf16[8,4224]{1,0:T(8,128)(2,1)S(1)}, bf16[8,4224]{1,0:T(8,128)(2,1)S(1)}, u32[]{:S(2)}, u32[]{:S(2)}) collective-permute-start(bf16[8,4224]{1,0:T(8,128)(2,1)S(1)} %concatenate.10), channel_id=1, source_target_pairs={{0,8},{1,9},{2,10},{3,11},{4,12},{5,13},{6,14},{7,15},{8,0},{9,1},... | collective-permute-start | bytes 202760 | tf_op jit(solution)/shard_map/ppermute | solution.py:27
  8.9 0.0 collective-permute-start.2
  8.9 1.7 %collective-permute-start.3 = (bf16[8,4224]{1,0:T(8,128)(2,1)S(1)}, bf16[8,4224]{1,0:T(8,128)(2,1)S(1)}, u32[]{:S(2)}, u32[]{:S(2)}) collective-permute-start(bf16[8,4224]{1,0:T(8,128)(2,1)S(1)} %concatenate.10), channel_id=1, source_target_pairs={{0,2},{1,3},{2,0},{3,1},{4,6},{5,7},{6,4},{7,5},{8,10},{9,11},{10,... | collective-permute-start | bytes 202760 | tf_op jit(solution)/shard_map/ppermute | solution.py:27
  10.6 0.0 collective-permute-done
  10.6 0.4 collective-permute-start.4
  11.0 2.7 %collective-permute-done.1 = bf16[8,4224]{1,0:T(8,128)(2,1)S(1)} collective-permute-done((bf16[8,4224]{1,0:T(8,128)(2,1)S(1)}, bf16[8,4224]{1,0:T(8,128)(2,1)S(1)}, u32[]{:S(2)}, u32[]{:S(2)}) %collective-permute-start.1) | collective-permute-done | bytes 67616 | tf_op jit(solution)/shard_map/ppermute | solution.py:27
  13.7 1.5 %collective-permute-start.5 = (bf16[8,4224]{1,0:T(8,128)(2,1)S(1)}, bf16[8,4224]{1,0:T(8,128)(2,1)S(1)}, u32[]{:S(2)}, u32[]{:S(2)}) collective-permute-start(bf16[8,4224]{1,0:T(8,128)(2,1)S(1)} %collective-permute-done.1), channel_id=1, source_target_pairs={{0,2},{1,3},{2,0},{3,1},{4,6},{5,7},{6,4},{7,5},{8,10},{9,11},{10,... | collective-permute-start | bytes 202760 | tf_op jit(solution)/shard_map/ppermute | solution.py:27
  15.2 0.0 collective-permute-done.2
  15.2 1.4 %collective-permute-start.6 = (bf16[8,4224]{1,0:T(8,128)(2,1)S(1)}, bf16[8,4224]{1,0:T(8,128)(2,1)S(1)}, u32[]{:S(2)}, u32[]{:S(2)}) collective-permute-start(bf16[8,4224]{1,0:T(8,128)(2,1)S(1)} %collective-permute-done.2), channel_id=1, source_target_pairs={{0,2},{1,3},{2,0},{3,1},{4,6},{5,7},{6,4},{7,5},{8,10},{9,11},{10,... | collective-permute-start | bytes 202760 | tf_op jit(solution)/shard_map/ppermute | solution.py:27
  16.6 0.0 collective-permute-done.3
  16.7 0.0 collective-permute-done.4
  16.7 1.3 %collective-permute-done.5 = bf16[8,4224]{1,0:T(8,128)(2,1)S(1)} collective-permute-done((bf16[8,4224]{1,0:T(8,128)(2,1)S(1)}, bf16[8,4224]{1,0:T(8,128)(2,1)S(1)}, u32[]{:S(2)}, u32[]{:S(2)}) %collective-permute-start.5) | collective-permute-done | bytes 67616 | tf_op jit(solution)/shard_map/ppermute | solution.py:27
  18.0 1.5 %collective-permute-done.6 = bf16[8,4224]{1,0:T(8,128)(2,1)S(1)} collective-permute-done((bf16[8,4224]{1,0:T(8,128)(2,1)S(1)}, bf16[8,4224]{1,0:T(8,128)(2,1)S(1)}, u32[]{:S(2)}, u32[]{:S(2)}) %collective-permute-start.6) | collective-permute-done | bytes 67616 | tf_op jit(solution)/shard_map/ppermute | solution.py:27
  19.5 0.1 collective-permute-start.7
  19.6 1.9 %collective-permute-done.7 = bf16[64,4224]{1,0:T(8,128)(2,1)S(1)} collective-permute-done((bf16[64,4224]{1,0:T(8,128)(2,1)S(1)}, bf16[64,4224]{1,0:T(8,128)(2,1)S(1)}, u32[]{:S(2)}, u32[]{:S(2)}) %collective-permute-start.7) | collective-permute-done | bytes 540704 | tf_op jit(solution)/shard_map/ppermute | solution.py:27
  21.6 36.0 %experts.1 = bf16[128,4096]{1,0:T(8,128)(2,1)S(1)} custom-call(s32[1]{0:T(128)} %bitcast.first_ref, bf16[128,4224]{1,0:T(8,128)(2,1)S(1)} %constant_dynamic-update-slice_fusion.8.x_ref, bf16[3072,4096]{1,0:T(8,128)(2,1)} %bitcast.29, bf16[3072,4096]{1,0:T(8,128)(2,1)} %bitcast.30, bf16[3072,4096]{1,0:T(8,128)(2,1)} %bitcast.31), custom_call_target="tpu_custom_call" | custom-call | tf_op jit(solution)/shard_map/experts/pallas_call | solution.py:122
  57.6 0.1 fusion.6
  57.7 0.2 collective-permute-start.8
  57.9 1.8 %collective-permute-done.8 = bf16[2,4,8,4096]{3,2,1,0:T(8,128)(2,1)S(1)} collective-permute-done((bf16[2,4,8,4096]{3,2,1,0:T(8,128)(2,1)S(1)}, bf16[2,4,8,4096]{3,2,1,0:T(8,128)(2,1)S(1)}, u32[]{:S(2)}, u32[]{:S(2)}) %collective-permute-start.8) | collective-permute-done | bytes 524320 | tf_op jit(solution)/shard_map/ppermute | solution.py:27
  59.6 0.1 fusion
  59.8 1.5 %collective-permute-start.9 = (bf16[4,8,4096]{2,1,0:T(8,128)(2,1)S(1)}, bf16[4,8,4096]{2,1,0:T(8,128)(2,1)S(1)}, u32[]{:S(2)}, u32[]{:S(2)}) collective-permute-start(bf16[4,8,4096]{2,1,0:T(8,128)(2,1)S(1)} %slice_bitcast_fusion), channel_id=1, source_target_pairs={{0,2},{1,3},{2,0},{3,1},{4,6},{5,7},{6,4},{7,5},{8,10},{9,11},{10,... | collective-permute-start | bytes 786440 | tf_op jit(solution)/shard_map/ppermute | solution.py:27
  61.2 7.0 %collective-permute-done.9 = bf16[4,8,4096]{2,1,0:T(8,128)(2,1)S(1)} collective-permute-done((bf16[4,8,4096]{2,1,0:T(8,128)(2,1)S(1)}, bf16[4,8,4096]{2,1,0:T(8,128)(2,1)S(1)}, u32[]{:S(2)}, u32[]{:S(2)}) %collective-permute-start.9) | collective-permute-done | bytes 262176 | tf_op jit(solution)/shard_map/ppermute | solution.py:27
  68.2 0.1 fusion.1
  68.3 1.6 %collective-permute-start.10 = (bf16[8,4096]{1,0:T(8,128)(2,1)S(1)}, bf16[8,4096]{1,0:T(8,128)(2,1)S(1)}, u32[]{:S(2)}, u32[]{:S(2)}) collective-permute-start(bf16[8,4096]{1,0:T(8,128)(2,1)S(1)} %get-tuple-element.7), channel_id=1, source_target_pairs={{0,8},{1,9},{2,10},{3,11},{4,12},{5,13},{6,14},{7,15},{8,0},{9,1},... | collective-permute-start | bytes 196616 | tf_op jit(solution)/shard_map/ppermute | solution.py:27
  69.9 1.7 %collective-permute-start.11 = (bf16[8,4096]{1,0:T(8,128)(2,1)S(1)}, bf16[8,4096]{1,0:T(8,128)(2,1)S(1)}, u32[]{:S(2)}, u32[]{:S(2)}) collective-permute-start(bf16[8,4096]{1,0:T(8,128)(2,1)S(1)} %get-tuple-element.9), channel_id=1, source_target_pairs={{0,12},{1,13},{2,14},{3,15},{4,8},{5,9},{6,10},{7,11},{8,4},{9,5},... | collective-permute-start | bytes 196616 | tf_op jit(solution)/shard_map/ppermute | solution.py:27
  71.6 0.5 collective-permute-start.12
  72.1 4.0 %collective-permute-done.10 = bf16[8,4096]{1,0:T(8,128)(2,1)S(1)} collective-permute-done((bf16[8,4096]{1,0:T(8,128)(2,1)S(1)}, bf16[8,4096]{1,0:T(8,128)(2,1)S(1)}, u32[]{:S(2)}, u32[]{:S(2)}) %collective-permute-start.10) | collective-permute-done | bytes 65568 | tf_op jit(solution)/shard_map/ppermute | solution.py:27
  76.1 0.0 collective-permute-done.11
  76.1 0.6 collective-permute-done.12
  76.7 0.7 fusion.4
  (12 shorter events, 0.2 us)
Async XLA Ops:
  3.3 7.3 %collective-permute-start = (bf16[8,4224]{1,0:T(8,128)(2,1)S(1)}, bf16[8,4224]{1,0:T(8,128)(2,1)S(1)}, u32[]{:S(2)}, u32[]{:S(2)}) collective-permute-start(bf16[8,4224]{1,0:T(8,128)(2,1)S(1)} %concatenate.10), channel_id=1, source_target_pairs={{0,4},{1,5},{2,6},{3,7},{4,0},{5,1},{6,2},{7,3},{8,12},{9,13},{10,... | collective-permute-start | bytes 202760 | tf_op jit(solution)/shard_map/ppermute | solution.py:27
  6.3 7.4 %collective-permute-start.1 = (bf16[8,4224]{1,0:T(8,128)(2,1)S(1)}, bf16[8,4224]{1,0:T(8,128)(2,1)S(1)}, u32[]{:S(2)}, u32[]{:S(2)}) collective-permute-start(bf16[8,4224]{1,0:T(8,128)(2,1)S(1)} %concatenate.10), channel_id=1, source_target_pairs={{0,8},{1,9},{2,10},{3,11},{4,12},{5,13},{6,14},{7,15},{8,0},{9,1},... | collective-permute-start | bytes 202760 | tf_op jit(solution)/shard_map/ppermute | solution.py:27
  8.9 6.3 %collective-permute-start.2 = (bf16[8,4224]{1,0:T(8,128)(2,1)S(1)}, bf16[8,4224]{1,0:T(8,128)(2,1)S(1)}, u32[]{:S(2)}, u32[]{:S(2)}) collective-permute-start(bf16[8,4224]{1,0:T(8,128)(2,1)S(1)} %concatenate.10), channel_id=1, source_target_pairs={{0,12},{1,13},{2,14},{3,15},{4,8},{5,9},{6,10},{7,11},{8,4},{9,5},... | collective-permute-start | bytes 202760 | tf_op jit(solution)/shard_map/ppermute | solution.py:27
  8.9 7.7 %collective-permute-start.3 = (bf16[8,4224]{1,0:T(8,128)(2,1)S(1)}, bf16[8,4224]{1,0:T(8,128)(2,1)S(1)}, u32[]{:S(2)}, u32[]{:S(2)}) collective-permute-start(bf16[8,4224]{1,0:T(8,128)(2,1)S(1)} %concatenate.10), channel_id=1, source_target_pairs={{0,2},{1,3},{2,0},{3,1},{4,6},{5,7},{6,4},{7,5},{8,10},{9,11},{10,... | collective-permute-start | bytes 202760 | tf_op jit(solution)/shard_map/ppermute | solution.py:27
  10.6 6.0 %collective-permute-start.4 = (bf16[8,4224]{1,0:T(8,128)(2,1)S(1)}, bf16[8,4224]{1,0:T(8,128)(2,1)S(1)}, u32[]{:S(2)}, u32[]{:S(2)}) collective-permute-start(bf16[8,4224]{1,0:T(8,128)(2,1)S(1)} %collective-permute-done), channel_id=1, source_target_pairs={{0,2},{1,3},{2,0},{3,1},{4,6},{5,7},{6,4},{7,5},{8,10},{9,11},{10,... | collective-permute-start | bytes 202760 | tf_op jit(solution)/shard_map/ppermute | solution.py:27
  13.7 4.3 %collective-permute-start.5 = (bf16[8,4224]{1,0:T(8,128)(2,1)S(1)}, bf16[8,4224]{1,0:T(8,128)(2,1)S(1)}, u32[]{:S(2)}, u32[]{:S(2)}) collective-permute-start(bf16[8,4224]{1,0:T(8,128)(2,1)S(1)} %collective-permute-done.1), channel_id=1, source_target_pairs={{0,2},{1,3},{2,0},{3,1},{4,6},{5,7},{6,4},{7,5},{8,10},{9,11},{10,... | collective-permute-start | bytes 202760 | tf_op jit(solution)/shard_map/ppermute | solution.py:27
  15.2 4.3 %collective-permute-start.6 = (bf16[8,4224]{1,0:T(8,128)(2,1)S(1)}, bf16[8,4224]{1,0:T(8,128)(2,1)S(1)}, u32[]{:S(2)}, u32[]{:S(2)}) collective-permute-start(bf16[8,4224]{1,0:T(8,128)(2,1)S(1)} %collective-permute-done.2), channel_id=1, source_target_pairs={{0,2},{1,3},{2,0},{3,1},{4,6},{5,7},{6,4},{7,5},{8,10},{9,11},{10,... | collective-permute-start | bytes 202760 | tf_op jit(solution)/shard_map/ppermute | solution.py:27
  19.5 2.0 %collective-permute-start.7 = (bf16[64,4224]{1,0:T(8,128)(2,1)S(1)}, bf16[64,4224]{1,0:T(8,128)(2,1)S(1)}, u32[]{:S(2)}, u32[]{:S(2)}) collective-permute-start(bf16[64,4224]{1,0:T(8,128)(2,1)S(1)} %get-tuple-element.10), channel_id=1, source_target_pairs={{0,1},{1,0},{2,3},{3,2},{4,5},{5,4},{6,7},{7,6},{8,9},{9,8},{10,11... | collective-permute-start | bytes 1622024 | tf_op jit(solution)/shard_map/ppermute | solution.py:27
  57.7 2.0 %collective-permute-start.8 = (bf16[2,4,8,4096]{3,2,1,0:T(8,128)(2,1)S(1)}, bf16[2,4,8,4096]{3,2,1,0:T(8,128)(2,1)S(1)}, u32[]{:S(2)}, u32[]{:S(2)}) collective-permute-start(bf16[2,4,8,4096]{3,2,1,0:T(8,128)(2,1)S(1)} %bitcast.33), channel_id=1, source_target_pairs={{0,1},{1,0},{2,3},{3,2},{4,5},{5,4},{6,7},{7,6},{8,9},{9,8},{10,11... | collective-permute-start | bytes 1572872 | tf_op jit(solution)/shard_map/ppermute | solution.py:27
  59.8 8.4 %collective-permute-start.9 = (bf16[4,8,4096]{2,1,0:T(8,128)(2,1)S(1)}, bf16[4,8,4096]{2,1,0:T(8,128)(2,1)S(1)}, u32[]{:S(2)}, u32[]{:S(2)}) collective-permute-start(bf16[4,8,4096]{2,1,0:T(8,128)(2,1)S(1)} %slice_bitcast_fusion), channel_id=1, source_target_pairs={{0,2},{1,3},{2,0},{3,1},{4,6},{5,7},{6,4},{7,5},{8,10},{9,11},{10,... | collective-permute-start | bytes 786440 | tf_op jit(solution)/shard_map/ppermute | solution.py:27
  68.3 7.8 %collective-permute-start.10 = (bf16[8,4096]{1,0:T(8,128)(2,1)S(1)}, bf16[8,4096]{1,0:T(8,128)(2,1)S(1)}, u32[]{:S(2)}, u32[]{:S(2)}) collective-permute-start(bf16[8,4096]{1,0:T(8,128)(2,1)S(1)} %get-tuple-element.7), channel_id=1, source_target_pairs={{0,8},{1,9},{2,10},{3,11},{4,12},{5,13},{6,14},{7,15},{8,0},{9,1},... | collective-permute-start | bytes 196616 | tf_op jit(solution)/shard_map/ppermute | solution.py:27
  69.9 6.2 %collective-permute-start.11 = (bf16[8,4096]{1,0:T(8,128)(2,1)S(1)}, bf16[8,4096]{1,0:T(8,128)(2,1)S(1)}, u32[]{:S(2)}, u32[]{:S(2)}) collective-permute-start(bf16[8,4096]{1,0:T(8,128)(2,1)S(1)} %get-tuple-element.9), channel_id=1, source_target_pairs={{0,12},{1,13},{2,14},{3,15},{4,8},{5,9},{6,10},{7,11},{8,4},{9,5},... | collective-permute-start | bytes 196616 | tf_op jit(solution)/shard_map/ppermute | solution.py:27
  71.6 5.1 %collective-permute-start.12 = (bf16[8,4096]{1,0:T(8,128)(2,1)S(1)}, bf16[8,4096]{1,0:T(8,128)(2,1)S(1)}, u32[]{:S(2)}, u32[]{:S(2)}) collective-permute-start(bf16[8,4096]{1,0:T(8,128)(2,1)S(1)} %get-tuple-element.8), channel_id=1, source_target_pairs={{0,4},{1,5},{2,6},{3,7},{4,0},{5,1},{6,2},{7,3},{8,12},{9,13},{10,... | collective-permute-start | bytes 196616 | tf_op jit(solution)/shard_map/ppermute | solution.py:27

commit v3 on v2

--- a/solution.py
+++ b/solution.py
@@ -54,69 +54,112 @@
     return add_up(y[0], *[send(y[m], ep_mask=m, dp_mask=0) for m in ep_order(ep_count)])
 
 
+def message_kernel(expert_total, tokens_ref, ids_ref, scores_ref, out_ref):
+    model_width = tokens_ref.shape[1]
+    out_ref[:, :model_width] = tokens_ref[...]
+    weights = scores_ref[...] / jnp.sum(scores_ref[...], axis=1, keepdims=True)
+    shape = (tokens_ref.shape[0], 2 * expert_total)
+    column = lax.broadcasted_iota(jnp.int32, shape, 1)
+    dense = jnp.zeros(shape, F32)
+    for k in range(ids_ref.shape[1]):
+        named = ids_ref[:, k : k + 1] == lax.rem(column, expert_total)
+        dense = dense + jnp.where(named, weights[:, k : k + 1], 0.0)
+    high = dense.astype(BF16).astype(F32)
+    out_ref[:, model_width:] = jnp.where(column < expert_total, high, dense - high).astype(BF16)
+
+
+def message(tokens, expert_ids, gate_scores, expert_total):
+    whole = pl.BlockSpec(memory_space=pltpu.VMEM)
+    shape = (tokens.shape[0], tokens.shape[1] + 2 * expert_total)
+    return pl.pallas_call(
+        functools.partial(message_kernel, expert_total),
+        in_specs=[whole] * 3,
+        out_specs=whole,
+        out_shape=jax.ShapeDtypeStruct(shape, BF16),
+        compiler_params=pltpu.CompilerParams(vmem_limit_bytes=4 << 20),
+        name="message",
+    )(tokens, expert_ids, gate_scores)
+
+
 def experts_kernel(width, expert_total, step, piece, slots, down_slots,
                    first_ref, x_ref, gate_ref, up_ref, down_ref, y_ref,
-                   h_ref, gate_buf, up_buf, down_buf, gate_sem, up_sem, down_sem):
+                   h_ref, buf, down_buf, sem, down_sem):
     units, model_width = gate_ref.shape
     steps, pieces = units // step, model_width // piece
-
-    def rows_copy(ref, buf, sem, i):
+    per_step = -(-down_slots // slots)
+
+    def tile_copy(which, i):
+        slot = lax.rem(i, slots)
         return pltpu.make_async_copy(
-            ref.at[pl.ds(i * step, step), :], buf.at[i % slots], sem.at[i % slots]
+            (gate_ref, up_ref)[which].at[pl.ds(pl.multiple_of(i * step, step), step), :],
+            buf.at[slot, pl.ds(which * step, step), :],
+            sem.at[which, slot],
         )
 
-    def gate_copy(i):
-        return rows_copy(gate_ref, gate_buf, gate_sem, i)
-
-    def up_copy(i):
-        return rows_copy(up_ref, up_buf, up_sem, i)
-
     def down_copy(j):
-        slot = j % down_slots
+        slot = lax.rem(j, down_slots)
         return pltpu.make_async_copy(
-            down_ref.at[:, pl.ds(j * piece, piece)], down_buf.at[slot], down_sem.at[slot]
+            down_ref.at[:, pl.ds(pl.multiple_of(j * piece, piece), piece)],
+            down_buf.at[slot],
+            down_sem.at[slot],
         )
 
-    for i in range(min(slots, steps)):
-        gate_copy(i).start()
-        up_copy(i).start()
-    begun = 0
-    for i in range(steps):
-        x = x_ref[:, :model_width]
-        rows = slice(i * step, (i + 1) * step)
+    for i in range(slots):
+        tile_copy(0, i).start()
+        tile_copy(1, i).start()
+
+    def hidden_step(i, carry):
         shape = (step, x_ref.shape[1] - model_width)
         expert = first_ref[0] + (lax.broadcasted_iota(jnp.int32, shape, 0) + i * step) // width
         column = lax.rem(lax.broadcasted_iota(jnp.int32, shape, 1), expert_total)
         spread = (column == expert).astype(F32).astype(BF16)
         weight = lax.dot_general(spread, x_ref[:, model_width:], NT, preferred_element_type=F32)
-        gate_copy(i).wait()
-        gate_acts = lax.dot_general(gate_buf[i % slots], x, NT, preferred_element_type=F32)
-        gate_acts = jax.nn.silu(gate_acts) * weight
-        up_copy(i).wait()
-        up_acts = lax.dot_general(up_buf[i % slots], x, NT, preferred_element_type=F32)
-        h_ref[:, rows] = (gate_acts * up_acts).T.astype(BF16)
-        if i + slots < steps:
-            gate_copy(i + slots).start()
-            up_copy(i + slots).start()
-        else:
-            goal = min(pieces, down_slots) * (i + slots - steps + 1) // slots
-            for j in range(begun, goal):
-                down_copy(j).start()
-            begun = max(begun, goal)
-    for j in range(pieces):
+        tile_copy(0, i).wait()
+        tile_copy(1, i).wait()
+        acts = lax.dot_general(
+            buf[lax.rem(i, slots)], x_ref[:, :model_width], NT, preferred_element_type=F32
+        )
+        hidden = jax.nn.silu(acts[:step]) * acts[step:] * weight
+        h_ref[:, pl.ds(pl.multiple_of(i * step, step), step)] = hidden.T.astype(BF16)
+
+        @pl.when(i + slots < steps)
+        def _():
+            tile_copy(0, i + slots).start()
+            tile_copy(1, i + slots).start()
+
+        @pl.when(i + slots >= steps)
+        def _():
+            for k in range(per_step):
+                j = (i + slots - steps) * per_step + k
+
+                @pl.when(j < down_slots)
+                def _():
+                    down_copy(j).start()
+
+        return carry
+
+    lax.fori_loop(0, steps, hidden_step, 0)
+
+    def down_step(j, carry):
         down_copy(j).wait()
-        y_ref[:, j * piece : (j + 1) * piece] = jnp.dot(
-            h_ref[...], down_buf[j % down_slots], preferred_element_type=F32
+        y_ref[:, pl.ds(pl.multiple_of(j * piece, piece), piece)] = jnp.dot(
+            h_ref[...], down_buf[lax.rem(j, down_slots)], preferred_element_type=F32
         ).astype(BF16)
-        if j + down_slots < pieces:
+
+        @pl.when(j + down_slots < pieces)
+        def _():
             down_copy(j + down_slots).start()
+
+        return carry
+
+    lax.fori_loop(0, pieces, down_step, 0)
 
 
 def experts(rows, gate, up, down, first, width, expert_total):
     token_count = rows.shape[0]
     units, model_width = gate.shape
-    step = 2 * width if units % (2 * width) == 0 else width
-    piece, slots, down_slots = 512, 3, 6
+    step, piece = 2 * width, 512
+    slots, down_slots = min(3, units // step), min(6, model_width // piece)
     whole = pl.BlockSpec(memory_space=pltpu.VMEM)
     away = pl.BlockSpec(memory_space=pl.ANY)
     return pl.pallas_call(
@@ -126,11 +169,9 @@
         out_shape=jax.ShapeDtypeStruct((token_count, model_width), BF16),
         scratch_shapes=[
             pltpu.VMEM((token_count, units), BF16),
-            pltpu.VMEM((slots, step, model_width), BF16),
-            pltpu.VMEM((slots, step, model_width), BF16),
+            pltpu.VMEM((slots, 2 * step, model_width), BF16),
             pltpu.VMEM((down_slots, units, piece), BF16),
-            pltpu.SemaphoreType.DMA((slots,)),
-            pltpu.SemaphoreType.DMA((slots,)),
+            pltpu.SemaphoreType.DMA((2, slots)),
             pltpu.SemaphoreType.DMA((down_slots,)),
         ],
         compiler_params=pltpu.CompilerParams(vmem_limit_bytes=44 << 20),
@@ -162,18 +203,14 @@
     down = down_weight.reshape(local_experts * width, model_width)
     first = (lax.axis_index("ep") * local_experts).astype(jnp.int32).reshape(1)
 
-    weights = gate_scores / jnp.sum(gate_scores, axis=1, keepdims=True)
-    named = expert_ids[:, :, None] == jnp.arange(expert_total, dtype=jnp.int32)[None, None, :]
-    dense = jnp.sum(jnp.where(named, weights[:, :, None], 0.0), axis=1)
-    high = lax.reduce_precision(dense, 8, 7)
-    message = jnp.concatenate([tokens, high.astype(BF16), (dense - high).astype(BF16)], axis=1)
+    sent = message(tokens, expert_ids, gate_scores, expert_total)
 
     powers = all(n & (n - 1) == 0 for n in (ep_count, dp_count))
-    if powers and ep_count <= 8 and 2 <= dp_count <= 8:
-        rows = gather_rows(message, ep_count, dp_count)
+    if powers and ep_count <= 8 and 2 <= dp_count <= 8 and local_experts % 2 == 0:
+        rows = gather_rows(sent, ep_count, dp_count)
         partial = experts(rows, gate, up, down, first, width, expert_total)
         return scatter_rows(partial, ep_count, dp_count)
-    rows = lax.all_gather(message, ("ep", "dp"), axis=0, tiled=True)
+    rows = lax.all_gather(sent, ("ep", "dp"), axis=0, tiled=True)
     partial = experts_plain(rows, gate, up, down, first, width, expert_total)
     return lax.psum_scatter(partial, ("ep", "dp"), scatter_dimension=0, tiled=True)
 

time: 77.6 us -> 66 us (0.85)
  Pallas kernels: 36 us -> 25.4 us
  other arithmetic: 3.2 us -> 0.85 us
  local copies, waits for them, and re-layouts: 1.21 us -> 2.49 us
    pallas_call x1, Pallas kernels: 36 us -> 25.2 us  [experts(): pl.pallas_call(functools.partial(experts_kernel, width, expert_total, ste...]
    unnamed x7 -> x13, local copies, waits for them, and re-layouts: 0.11 us -> 2.32 us
    reduce_sum x2 -> x0, other arithmetic: 1.58 us -> none  [the longest x1 0.8 us: local(): weights = gate_scores / jnp.sum(gate_scores, axis=1, keepdims=True)]
    concatenate x1 -> x0, local copies, waits for them, and re-layouts: 0.93 us -> none  [local(): jnp.concatenate([tokens, high.astype(BF16), (dense - high).astype(BF16)],...]
where the time goes in v3:
time: 66 us; the launch traced here: 65.8 us
  Pallas kernels  25.4 us (38%)
  waiting for transfers between devices  20.7 us (31%)
  starting transfers between devices  16.2 us (25%)
  local copies, waits for them, and re-layouts  2.49 us (4%)
  other arithmetic  0.85 us (1%)
    pallas_call x1, Pallas kernels, experts(): pl.pallas_call(functools.partial(experts_kernel, width, expert_total, ste...  25.2 us
    ppermute x13, waiting for transfers between devices, hop(): return lax.ppermute(x, ('ep', 'dp'), pairs)  20.7 us
    ppermute x13, starting transfers between devices, hop(): return lax.ppermute(x, ('ep', 'dp'), pairs)  16.2 us
    unnamed x13, local copies, waits for them, and re-layouts  2.32 us
  transfers between devices with their start and end apart: 13, of which 8 were waited for; matrix products, arithmetic and copies ran while one was open for 0% of the time, Pallas kernels for 0%

profile of v3, /device:TPU:0, one launch (start us, length us, event | category | flops | bytes accessed | tf_op | source)
XLA Modules:
  0.0 65.8 jit_solution(6097450997357711209)
XLA Ops:
  0.0 0.0 copy-start
  0.0 0.8 %copy-done = bf16[8,4096]{1,0:T(8,128)(2,1)S(1)} copy-done((bf16[8,4096]{1,0:T(8,128)(2,1)S(1)}, bf16[8,4096]{1,0:T(8,128)(2,1)}, u32[]{:S(2)}) %copy-start) | copy-done | bytes 65560
  0.8 0.0 copy-start.1
  0.8 0.7 %copy-done.1 = s32[8,8]{1,0:T(8,128)S(1)} copy-done((s32[8,8]{1,0:T(8,128)S(1)}, s32[8,8]{1,0:T(8,128)}, u32[]{:S(2)}) %copy-start.1) | copy-done | bytes 280
  1.5 0.0 copy-start.2
  1.5 0.7 %copy-done.2 = f32[8,8]{1,0:T(8,128)S(1)} copy-done((f32[8,8]{1,0:T(8,128)S(1)}, f32[8,8]{1,0:T(8,128)}, u32[]{:S(2)}) %copy-start.2) | copy-done | bytes 280
  2.2 0.2 message.1
  2.4 3.1 %collective-permute-start = (bf16[8,4224]{1,0:T(8,128)(2,1)S(1)}, bf16[8,4224]{1,0:T(8,128)(2,1)S(1)}, u32[]{:S(2)}, u32[]{:S(2)}) collective-permute-start(bf16[8,4224]{1,0:T(8,128)(2,1)S(1)} %message.1), channel_id=1, source_target_pairs={{0,4},{1,5},{2,6},{3,7},{4,0},{5,1},{6,2},{7,3},{8,12},{9,13},{10,... | collective-permute-start | bytes 202760 | tf_op jit(solution)/shard_map/ppermute | solution.py:27
  5.5 2.6 %collective-permute-start.1 = (bf16[8,4224]{1,0:T(8,128)(2,1)S(1)}, bf16[8,4224]{1,0:T(8,128)(2,1)S(1)}, u32[]{:S(2)}, u32[]{:S(2)}) collective-permute-start(bf16[8,4224]{1,0:T(8,128)(2,1)S(1)} %message.1), channel_id=1, source_target_pairs={{0,8},{1,9},{2,10},{3,11},{4,12},{5,13},{6,14},{7,15},{8,0},{9,1},... | collective-permute-start | bytes 202760 | tf_op jit(solution)/shard_map/ppermute | solution.py:27
  8.1 0.0 collective-permute-start.2
  8.1 1.7 %collective-permute-start.3 = (bf16[8,4224]{1,0:T(8,128)(2,1)S(1)}, bf16[8,4224]{1,0:T(8,128)(2,1)S(1)}, u32[]{:S(2)}, u32[]{:S(2)}) collective-permute-start(bf16[8,4224]{1,0:T(8,128)(2,1)S(1)} %message.1), channel_id=1, source_target_pairs={{0,2},{1,3},{2,0},{3,1},{4,6},{5,7},{6,4},{7,5},{8,10},{9,11},{10,... | collective-permute-start | bytes 202760 | tf_op jit(solution)/shard_map/ppermute | solution.py:27
  9.8 0.0 collective-permute-done
  9.8 0.4 collective-permute-start.4
  10.2 2.7 %collective-permute-done.1 = bf16[8,4224]{1,0:T(8,128)(2,1)S(1)} collective-permute-done((bf16[8,4224]{1,0:T(8,128)(2,1)S(1)}, bf16[8,4224]{1,0:T(8,128)(2,1)S(1)}, u32[]{:S(2)}, u32[]{:S(2)}) %collective-permute-start.1) | collective-permute-done | bytes 67616 | tf_op jit(solution)/shard_map/ppermute | solution.py:27
  12.9 1.5 %collective-permute-start.5 = (bf16[8,4224]{1,0:T(8,128)(2,1)S(1)}, bf16[8,4224]{1,0:T(8,128)(2,1)S(1)}, u32[]{:S(2)}, u32[]{:S(2)}) collective-permute-start(bf16[8,4224]{1,0:T(8,128)(2,1)S(1)} %collective-permute-done.1), channel_id=1, source_target_pairs={{0,2},{1,3},{2,0},{3,1},{4,6},{5,7},{6,4},{7,5},{8,10},{9,11},{10,... | collective-permute-start | bytes 202760 | tf_op jit(solution)/shard_map/ppermute | solution.py:27
  14.4 0.0 collective-permute-done.2
  14.4 1.4 %collective-permute-start.6 = (bf16[8,4224]{1,0:T(8,128)(2,1)S(1)}, bf16[8,4224]{1,0:T(8,128)(2,1)S(1)}, u32[]{:S(2)}, u32[]{:S(2)}) collective-permute-start(bf16[8,4224]{1,0:T(8,128)(2,1)S(1)} %collective-permute-done.2), channel_id=1, source_target_pairs={{0,2},{1,3},{2,0},{3,1},{4,6},{5,7},{6,4},{7,5},{8,10},{9,11},{10,... | collective-permute-start | bytes 202760 | tf_op jit(solution)/shard_map/ppermute | solution.py:27
  15.8 0.0 collective-permute-done.3
  15.9 0.0 collective-permute-done.4
  15.9 1.3 %collective-permute-done.5 = bf16[8,4224]{1,0:T(8,128)(2,1)S(1)} collective-permute-done((bf16[8,4224]{1,0:T(8,128)(2,1)S(1)}, bf16[8,4224]{1,0:T(8,128)(2,1)S(1)}, u32[]{:S(2)}, u32[]{:S(2)}) %collective-permute-start.5) | collective-permute-done | bytes 67616 | tf_op jit(solution)/shard_map/ppermute | solution.py:27
  17.2 1.5 %collective-permute-done.6 = bf16[8,4224]{1,0:T(8,128)(2,1)S(1)} collective-permute-done((bf16[8,4224]{1,0:T(8,128)(2,1)S(1)}, bf16[8,4224]{1,0:T(8,128)(2,1)S(1)}, u32[]{:S(2)}, u32[]{:S(2)}) %collective-permute-start.6) | collective-permute-done | bytes 67616 | tf_op jit(solution)/shard_map/ppermute | solution.py:27
  18.7 0.1 collective-permute-start.7
  18.8 1.9 %collective-permute-done.7 = bf16[64,4224]{1,0:T(8,128)(2,1)S(1)} collective-permute-done((bf16[64,4224]{1,0:T(8,128)(2,1)S(1)}, bf16[64,4224]{1,0:T(8,128)(2,1)S(1)}, u32[]{:S(2)}, u32[]{:S(2)}) %collective-permute-start.7) | collective-permute-done | bytes 540704 | tf_op jit(solution)/shard_map/ppermute | solution.py:27
  20.7 25.2 %experts.1 = bf16[128,4096]{1,0:T(8,128)(2,1)S(1)} custom-call(s32[1]{0:T(128)} %bitcast.first_ref, bf16[128,4224]{1,0:T(8,128)(2,1)S(1)} %constant_dynamic-update-slice_fusion.8.x_ref, bf16[3072,4096]{1,0:T(8,128)(2,1)} %bitcast.29, bf16[3072,4096]{1,0:T(8,128)(2,1)} %bitcast.30, bf16[3072,4096]{1,0:T(8,128)(2,1)} %bitcast.31), custom_call_target="tpu_custom_call" | custom-call | tf_op jit(solution)/shard_map/experts/pallas_call | solution.py:165
  46.0 0.1 fusion.5
  46.1 0.2 collective-permute-start.8
  46.3 1.8 %collective-permute-done.8 = bf16[2,4,8,4096]{3,2,1,0:T(8,128)(2,1)S(1)} collective-permute-done((bf16[2,4,8,4096]{3,2,1,0:T(8,128)(2,1)S(1)}, bf16[2,4,8,4096]{3,2,1,0:T(8,128)(2,1)S(1)}, u32[]{:S(2)}, u32[]{:S(2)}) %collective-permute-start.8) | collective-permute-done | bytes 524320 | tf_op jit(solution)/shard_map/ppermute | solution.py:27
  48.0 0.1 fusion
  48.2 1.5 %collective-permute-start.9 = (bf16[4,8,4096]{2,1,0:T(8,128)(2,1)S(1)}, bf16[4,8,4096]{2,1,0:T(8,128)(2,1)S(1)}, u32[]{:S(2)}, u32[]{:S(2)}) collective-permute-start(bf16[4,8,4096]{2,1,0:T(8,128)(2,1)S(1)} %slice_bitcast_fusion), channel_id=1, source_target_pairs={{0,2},{1,3},{2,0},{3,1},{4,6},{5,7},{6,4},{7,5},{8,10},{9,11},{10,... | collective-permute-start | bytes 786440 | tf_op jit(solution)/shard_map/ppermute | solution.py:27
  49.6 7.0 %collective-permute-done.9 = bf16[4,8,4096]{2,1,0:T(8,128)(2,1)S(1)} collective-permute-done((bf16[4,8,4096]{2,1,0:T(8,128)(2,1)S(1)}, bf16[4,8,4096]{2,1,0:T(8,128)(2,1)S(1)}, u32[]{:S(2)}, u32[]{:S(2)}) %collective-permute-start.9) | collective-permute-done | bytes 262176 | tf_op jit(solution)/shard_map/ppermute | solution.py:27
  56.6 0.1 fusion.1
  56.7 1.6 %collective-permute-start.10 = (bf16[8,4096]{1,0:T(8,128)(2,1)S(1)}, bf16[8,4096]{1,0:T(8,128)(2,1)S(1)}, u32[]{:S(2)}, u32[]{:S(2)}) collective-permute-start(bf16[8,4096]{1,0:T(8,128)(2,1)S(1)} %get-tuple-element.7), channel_id=1, source_target_pairs={{0,8},{1,9},{2,10},{3,11},{4,12},{5,13},{6,14},{7,15},{8,0},{9,1},... | collective-permute-start | bytes 196616 | tf_op jit(solution)/shard_map/ppermute | solution.py:27
  58.3 1.7 %collective-permute-start.11 = (bf16[8,4096]{1,0:T(8,128)(2,1)S(1)}, bf16[8,4096]{1,0:T(8,128)(2,1)S(1)}, u32[]{:S(2)}, u32[]{:S(2)}) collective-permute-start(bf16[8,4096]{1,0:T(8,128)(2,1)S(1)} %get-tuple-element.9), channel_id=1, source_target_pairs={{0,12},{1,13},{2,14},{3,15},{4,8},{5,9},{6,10},{7,11},{8,4},{9,5},... | collective-permute-start | bytes 196616 | tf_op jit(solution)/shard_map/ppermute | solution.py:27
  60.0 0.5 collective-permute-start.12
  60.5 4.0 %collective-permute-done.10 = bf16[8,4096]{1,0:T(8,128)(2,1)S(1)} collective-permute-done((bf16[8,4096]{1,0:T(8,128)(2,1)S(1)}, bf16[8,4096]{1,0:T(8,128)(2,1)S(1)}, u32[]{:S(2)}, u32[]{:S(2)}) %collective-permute-start.10) | collective-permute-done | bytes 65568 | tf_op jit(solution)/shard_map/ppermute | solution.py:27
  64.5 0.0 collective-permute-done.11
  64.5 0.6 collective-permute-done.12
  65.1 0.7 %fusion.4 = bf16[8,4096]{1,0:T(8,128)(2,1)} fusion(bf16[8,4096]{1,0:T(8,128)(2,1)S(1)} %collective-permute-done.12, bf16[8,4096]{1,0:T(8,128)(2,1)S(1)} %collective-permute-done.11, bf16[8,4096]{1,0:T(8,128)(2,1)S(1)} %collective-permute-done.10, bf16[4,8,4096]{2,1,0:T(8,128)(2,1)S(1)} %fusion.1), kind=kLoop, calls=%fused_computation.9 | loop fusion | flops 262144 | bytes 327680 | tf_op jit(solution)/shard_map/convert_element_type | solution.py:19
  (11 shorter events, 0.2 us)
Async XLA Ops:
  0.0 0.8 %copy-start = (bf16[8,4096]{1,0:T(8,128)(2,1)S(1)}, bf16[8,4096]{1,0:T(8,128)(2,1)}, u32[]{:S(2)}) copy-start(bf16[8,4096]{1,0:T(8,128)(2,1)} %tokens_ref.1) | copy-start | bytes 196612
  0.8 0.7 %copy-start.1 = (s32[8,8]{1,0:T(8,128)S(1)}, s32[8,8]{1,0:T(8,128)}, u32[]{:S(2)}) copy-start(s32[8,8]{1,0:T(8,128)} %ids_ref.1) | copy-start | bytes 772
  1.5 0.7 %copy-start.2 = (f32[8,8]{1,0:T(8,128)S(1)}, f32[8,8]{1,0:T(8,128)}, u32[]{:S(2)}) copy-start(f32[8,8]{1,0:T(8,128)} %scores_ref.1) | copy-start | bytes 772
  2.4 7.4 %collective-permute-start = (bf16[8,4224]{1,0:T(8,128)(2,1)S(1)}, bf16[8,4224]{1,0:T(8,128)(2,1)S(1)}, u32[]{:S(2)}, u32[]{:S(2)}) collective-permute-start(bf16[8,4224]{1,0:T(8,128)(2,1)S(1)} %message.1), channel_id=1, source_target_pairs={{0,4},{1,5},{2,6},{3,7},{4,0},{5,1},{6,2},{7,3},{8,12},{9,13},{10,... | collective-permute-start | bytes 202760 | tf_op jit(solution)/shard_map/ppermute | solution.py:27
  5.5 7.4 %collective-permute-start.1 = (bf16[8,4224]{1,0:T(8,128)(2,1)S(1)}, bf16[8,4224]{1,0:T(8,128)(2,1)S(1)}, u32[]{:S(2)}, u32[]{:S(2)}) collective-permute-start(bf16[8,4224]{1,0:T(8,128)(2,1)S(1)} %message.1), channel_id=1, source_target_pairs={{0,8},{1,9},{2,10},{3,11},{4,12},{5,13},{6,14},{7,15},{8,0},{9,1},... | collective-permute-start | bytes 202760 | tf_op jit(solution)/shard_map/ppermute | solution.py:27
  8.1 6.3 %collective-permute-start.2 = (bf16[8,4224]{1,0:T(8,128)(2,1)S(1)}, bf16[8,4224]{1,0:T(8,128)(2,1)S(1)}, u32[]{:S(2)}, u32[]{:S(2)}) collective-permute-start(bf16[8,4224]{1,0:T(8,128)(2,1)S(1)} %message.1), channel_id=1, source_target_pairs={{0,12},{1,13},{2,14},{3,15},{4,8},{5,9},{6,10},{7,11},{8,4},{9,5},... | collective-permute-start | bytes 202760 | tf_op jit(solution)/shard_map/ppermute | solution.py:27
  8.1 7.7 %collective-permute-start.3 = (bf16[8,4224]{1,0:T(8,128)(2,1)S(1)}, bf16[8,4224]{1,0:T(8,128)(2,1)S(1)}, u32[]{:S(2)}, u32[]{:S(2)}) collective-permute-start(bf16[8,4224]{1,0:T(8,128)(2,1)S(1)} %message.1), channel_id=1, source_target_pairs={{0,2},{1,3},{2,0},{3,1},{4,6},{5,7},{6,4},{7,5},{8,10},{9,11},{10,... | collective-permute-start | bytes 202760 | tf_op jit(solution)/shard_map/ppermute | solution.py:27
  9.8 6.0 %collective-permute-start.4 = (bf16[8,4224]{1,0:T(8,128)(2,1)S(1)}, bf16[8,4224]{1,0:T(8,128)(2,1)S(1)}, u32[]{:S(2)}, u32[]{:S(2)}) collective-permute-start(bf16[8,4224]{1,0:T(8,128)(2,1)S(1)} %collective-permute-done), channel_id=1, source_target_pairs={{0,2},{1,3},{2,0},{3,1},{4,6},{5,7},{6,4},{7,5},{8,10},{9,11},{10,... | collective-permute-start | bytes 202760 | tf_op jit(solution)/shard_map/ppermute | solution.py:27
  12.9 4.3 %collective-permute-start.5 = (bf16[8,4224]{1,0:T(8,128)(2,1)S(1)}, bf16[8,4224]{1,0:T(8,128)(2,1)S(1)}, u32[]{:S(2)}, u32[]{:S(2)}) collective-permute-start(bf16[8,4224]{1,0:T(8,128)(2,1)S(1)} %collective-permute-done.1), channel_id=1, source_target_pairs={{0,2},{1,3},{2,0},{3,1},{4,6},{5,7},{6,4},{7,5},{8,10},{9,11},{10,... | collective-permute-start | bytes 202760 | tf_op jit(solution)/shard_map/ppermute | solution.py:27
  14.4 4.3 %collective-permute-start.6 = (bf16[8,4224]{1,0:T(8,128)(2,1)S(1)}, bf16[8,4224]{1,0:T(8,128)(2,1)S(1)}, u32[]{:S(2)}, u32[]{:S(2)}) collective-permute-start(bf16[8,4224]{1,0:T(8,128)(2,1)S(1)} %collective-permute-done.2), channel_id=1, source_target_pairs={{0,2},{1,3},{2,0},{3,1},{4,6},{5,7},{6,4},{7,5},{8,10},{9,11},{10,... | collective-permute-start | bytes 202760 | tf_op jit(solution)/shard_map/ppermute | solution.py:27
  18.7 2.0 %collective-permute-start.7 = (bf16[64,4224]{1,0:T(8,128)(2,1)S(1)}, bf16[64,4224]{1,0:T(8,128)(2,1)S(1)}, u32[]{:S(2)}, u32[]{:S(2)}) collective-permute-start(bf16[64,4224]{1,0:T(8,128)(2,1)S(1)} %get-tuple-element.10), channel_id=1, source_target_pairs={{0,1},{1,0},{2,3},{3,2},{4,5},{5,4},{6,7},{7,6},{8,9},{9,8},{10,11... | collective-permute-start | bytes 1622024 | tf_op jit(solution)/shard_map/ppermute | solution.py:27
  46.1 2.0 %collective-permute-start.8 = (bf16[2,4,8,4096]{3,2,1,0:T(8,128)(2,1)S(1)}, bf16[2,4,8,4096]{3,2,1,0:T(8,128)(2,1)S(1)}, u32[]{:S(2)}, u32[]{:S(2)}) collective-permute-start(bf16[2,4,8,4096]{3,2,1,0:T(8,128)(2,1)S(1)} %bitcast.33), channel_id=1, source_target_pairs={{0,1},{1,0},{2,3},{3,2},{4,5},{5,4},{6,7},{7,6},{8,9},{9,8},{10,11... | collective-permute-start | bytes 1572872 | tf_op jit(solution)/shard_map/ppermute | solution.py:27
  48.2 8.4 %collective-permute-start.9 = (bf16[4,8,4096]{2,1,0:T(8,128)(2,1)S(1)}, bf16[4,8,4096]{2,1,0:T(8,128)(2,1)S(1)}, u32[]{:S(2)}, u32[]{:S(2)}) collective-permute-start(bf16[4,8,4096]{2,1,0:T(8,128)(2,1)S(1)} %slice_bitcast_fusion), channel_id=1, source_target_pairs={{0,2},{1,3},{2,0},{3,1},{4,6},{5,7},{6,4},{7,5},{8,10},{9,11},{10,... | collective-permute-start | bytes 786440 | tf_op jit(solution)/shard_map/ppermute | solution.py:27
  56.7 7.8 %collective-permute-start.10 = (bf16[8,4096]{1,0:T(8,128)(2,1)S(1)}, bf16[8,4096]{1,0:T(8,128)(2,1)S(1)}, u32[]{:S(2)}, u32[]{:S(2)}) collective-permute-start(bf16[8,4096]{1,0:T(8,128)(2,1)S(1)} %get-tuple-element.7), channel_id=1, source_target_pairs={{0,8},{1,9},{2,10},{3,11},{4,12},{5,13},{6,14},{7,15},{8,0},{9,1},... | collective-permute-start | bytes 196616 | tf_op jit(solution)/shard_map/ppermute | solution.py:27
  58.3 6.2 %collective-permute-start.11 = (bf16[8,4096]{1,0:T(8,128)(2,1)S(1)}, bf16[8,4096]{1,0:T(8,128)(2,1)S(1)}, u32[]{:S(2)}, u32[]{:S(2)}) collective-permute-start(bf16[8,4096]{1,0:T(8,128)(2,1)S(1)} %get-tuple-element.9), channel_id=1, source_target_pairs={{0,12},{1,13},{2,14},{3,15},{4,8},{5,9},{6,10},{7,11},{8,4},{9,5},... | collective-permute-start | bytes 196616 | tf_op jit(solution)/shard_map/ppermute | solution.py:27
  60.0 5.1 %collective-permute-start.12 = (bf16[8,4096]{1,0:T(8,128)(2,1)S(1)}, bf16[8,4096]{1,0:T(8,128)(2,1)S(1)}, u32[]{:S(2)}, u32[]{:S(2)}) collective-permute-start(bf16[8,4096]{1,0:T(8,128)(2,1)S(1)} %get-tuple-element.8), channel_id=1, source_target_pairs={{0,4},{1,5},{2,6},{3,7},{4,0},{5,1},{6,2},{7,3},{8,12},{9,13},{10,... | collective-permute-start | bytes 196616 | tf_op jit(solution)/shard_map/ppermute | solution.py:27

commit v4 on v3

--- a/solution.py
+++ b/solution.py
@@ -47,38 +47,59 @@
 
 def scatter_rows(y, ep_count, dp_count):
     send = functools.partial(hop, ep_count=ep_count, dp_count=dp_count)
-    rows = y.shape[0]
+    rows, half = y.shape[0], ep_count // 2
     y = y.reshape(2, dp_count // 2, ep_count, rows // (ep_count * dp_count), y.shape[1])
     y = add_up(y[0], send(y[1], ep_mask=0, dp_mask=1))
-    y = add_up(y[0], *[send(y[d // 2], ep_mask=0, dp_mask=d) for d in range(2, dp_count, 2)])
-    return add_up(y[0], *[send(y[m], ep_mask=m, dp_mask=0) for m in ep_order(ep_count)])
-
-
-def message_kernel(expert_total, tokens_ref, ids_ref, scores_ref, out_ref):
+    others = range(2, dp_count, 2)
+    far = [send(y[d // 2, half:], ep_mask=0, dp_mask=d) for d in others]
+    near = [send(y[d // 2, :half], ep_mask=0, dp_mask=d) for d in others]
+    far_sum = add_up(y[0, half:], *far)
+    far_sent = [send(far_sum[m - half], ep_mask=m, dp_mask=0) for m in range(half, ep_count)]
+    near, far_sent[0] = lax.optimization_barrier((near, far_sent[0]))
+    near_sum = add_up(y[0, :half], *near)
+    near_sent = [send(near_sum[m], ep_mask=m, dp_mask=0) for m in range(1, half)]
+    return add_up(near_sum[0], *near_sent, *far_sent)
+
+
+def message_kernel(expert_total, tokens_ref, ids_ref, scores_ref, out_ref, ids_buf, scores_buf, sem):
     model_width = tokens_ref.shape[1]
-    out_ref[:, :model_width] = tokens_ref[...]
-    weights = scores_ref[...] / jnp.sum(scores_ref[...], axis=1, keepdims=True)
+    copies = [
+        pltpu.make_async_copy(ids_ref, ids_buf, sem.at[0]),
+        pltpu.make_async_copy(scores_ref, scores_buf, sem.at[1]),
+        pltpu.make_async_copy(tokens_ref, out_ref.at[:, pl.ds(0, model_width)], sem.at[2]),
+    ]
+    for copy in copies:
+        copy.start()
+    copies[0].wait()
+    copies[1].wait()
+    weights = scores_buf[...] / jnp.sum(scores_buf[...], axis=1, keepdims=True)
     shape = (tokens_ref.shape[0], 2 * expert_total)
     column = lax.broadcasted_iota(jnp.int32, shape, 1)
     dense = jnp.zeros(shape, F32)
     for k in range(ids_ref.shape[1]):
-        named = ids_ref[:, k : k + 1] == lax.rem(column, expert_total)
+        named = ids_buf[:, k : k + 1] == lax.rem(column, expert_total)
         dense = dense + jnp.where(named, weights[:, k : k + 1], 0.0)
     high = dense.astype(BF16).astype(F32)
     out_ref[:, model_width:] = jnp.where(column < expert_total, high, dense - high).astype(BF16)
+    copies[2].wait()
 
 
 def message(tokens, expert_ids, gate_scores, expert_total):
-    whole = pl.BlockSpec(memory_space=pltpu.VMEM)
     shape = (tokens.shape[0], tokens.shape[1] + 2 * expert_total)
+    operands = (tokens, expert_ids, gate_scores)
     return pl.pallas_call(
         functools.partial(message_kernel, expert_total),
-        in_specs=[whole] * 3,
-        out_specs=whole,
+        in_specs=[pl.BlockSpec(memory_space=pltpu.HBM)] * 3,
+        out_specs=pl.BlockSpec(memory_space=pltpu.VMEM),
         out_shape=jax.ShapeDtypeStruct(shape, BF16),
+        scratch_shapes=[
+            pltpu.VMEM(expert_ids.shape, jnp.int32),
+            pltpu.VMEM(gate_scores.shape, F32),
+            pltpu.SemaphoreType.DMA((3,)),
+        ],
         compiler_params=pltpu.CompilerParams(vmem_limit_bytes=4 << 20),
         name="message",
-    )(tokens, expert_ids, gate_scores)
+    )(*[pltpu.with_memory_space_constraint(a, pltpu.HBM) for a in operands])
 
 
 def experts_kernel(width, expert_total, step, piece, slots, down_slots,
@@ -206,7 +227,7 @@
     sent = message(tokens, expert_ids, gate_scores, expert_total)
 
     powers = all(n & (n - 1) == 0 for n in (ep_count, dp_count))
-    if powers and ep_count <= 8 and 2 <= dp_count <= 8 and local_experts % 2 == 0:
+    if powers and 2 <= ep_count <= 8 and 2 <= dp_count <= 8 and local_experts % 2 == 0:
         rows = gather_rows(sent, ep_count, dp_count)
         partial = experts(rows, gate, up, down, first, width, expert_total)
         return scatter_rows(partial, ep_count, dp_count)

time: 66 us -> 65.4 us (level)
  local copies, waits for them, and re-layouts: 2.49 us -> 0.28 us
  Pallas kernels: 25.4 us -> 26.2 us
  waiting for transfers between devices: 20.7 us -> 21.4 us
    unnamed x13 -> x7, local copies, waits for them, and re-layouts: 2.32 us -> 0.11 us
    pallas_call x1, Pallas kernels: 0.18 us -> 0.91 us  [message(): pl.pallas_call(functools.partial(message_kernel, expert_total), in_specs=...]
    ppermute x13 -> x14, waiting for transfers between devices: 20.7 us -> 21.4 us  [hop(): return lax.ppermute(x, ('ep', 'dp'), pairs)]
    ppermute x13 -> x14, starting transfers between devices: 16.2 us -> 16.4 us  [hop(): return lax.ppermute(x, ('ep', 'dp'), pairs)]
  transfers between devices with their start and end apart: 13 -> 14, of which waited for: 8 -> 9; matrix products, arithmetic and copies ran while one was open for 0% -> 0% of each run, Pallas kernels for 0% -> 0%
where the time goes in v4:
time: 65.4 us; the launch traced here: 65.2 us
  Pallas kernels  26.2 us (40%)
  waiting for transfers between devices  21.4 us (33%)
  starting transfers between devices  16.4 us (25%)
  other arithmetic  0.86 us (1%)
    pallas_call x1, Pallas kernels, experts(): pl.pallas_call(functools.partial(experts_kernel, width, expert_total, ste...  25.2 us
    ppermute x14, waiting for transfers between devices, hop(): return lax.ppermute(x, ('ep', 'dp'), pairs)  21.4 us
    ppermute x14, starting transfers between devices, hop(): return lax.ppermute(x, ('ep', 'dp'), pairs)  16.4 us
  transfers between devices with their start and end apart: 14, of which 9 were waited for; matrix products, arithmetic and copies ran while one was open for 0% of the time, Pallas kernels for 0%

profile of v4, /device:TPU:0, one launch (start us, length us, event | category | flops | bytes accessed | tf_op | source)
XLA Modules:
  0.0 65.2 jit_solution(12054284430732950404)
XLA Ops:
  0.0 0.9 %message.1 = bf16[8,4224]{1,0:T(8,128)(2,1)S(1)} custom-call(bf16[8,4096]{1,0:T(8,128)(2,1)} %tokens_ref.1, s32[8,8]{1,0:T(8,128)} %ids_ref.1, f32[8,8]{1,0:T(8,128)} %scores_ref.1), custom_call_target="tpu_custom_call" | custom-call | tf_op jit(solution)/shard_map/message/pallas_call | solution.py:90
  0.9 3.1 %collective-permute-start = (bf16[8,4224]{1,0:T(8,128)(2,1)S(1)}, bf16[8,4224]{1,0:T(8,128)(2,1)S(1)}, u32[]{:S(2)}, u32[]{:S(2)}) collective-permute-start(bf16[8,4224]{1,0:T(8,128)(2,1)S(1)} %message.1), channel_id=1, source_target_pairs={{0,4},{1,5},{2,6},{3,7},{4,0},{5,1},{6,2},{7,3},{8,12},{9,13},{10,... | collective-permute-start | bytes 202760 | tf_op jit(solution)/shard_map/ppermute | solution.py:27
  4.0 2.6 %collective-permute-start.1 = (bf16[8,4224]{1,0:T(8,128)(2,1)S(1)}, bf16[8,4224]{1,0:T(8,128)(2,1)S(1)}, u32[]{:S(2)}, u32[]{:S(2)}) collective-permute-start(bf16[8,4224]{1,0:T(8,128)(2,1)S(1)} %message.1), channel_id=1, source_target_pairs={{0,8},{1,9},{2,10},{3,11},{4,12},{5,13},{6,14},{7,15},{8,0},{9,1},... | collective-permute-start | bytes 202760 | tf_op jit(solution)/shard_map/ppermute | solution.py:27
  6.6 0.0 collective-permute-start.2
  6.6 1.7 %collective-permute-start.3 = (bf16[8,4224]{1,0:T(8,128)(2,1)S(1)}, bf16[8,4224]{1,0:T(8,128)(2,1)S(1)}, u32[]{:S(2)}, u32[]{:S(2)}) collective-permute-start(bf16[8,4224]{1,0:T(8,128)(2,1)S(1)} %message.1), channel_id=1, source_target_pairs={{0,2},{1,3},{2,0},{3,1},{4,6},{5,7},{6,4},{7,5},{8,10},{9,11},{10,... | collective-permute-start | bytes 202760 | tf_op jit(solution)/shard_map/ppermute | solution.py:27
  8.3 0.0 collective-permute-done
  8.3 0.4 collective-permute-start.4
  8.7 2.7 %collective-permute-done.1 = bf16[8,4224]{1,0:T(8,128)(2,1)S(1)} collective-permute-done((bf16[8,4224]{1,0:T(8,128)(2,1)S(1)}, bf16[8,4224]{1,0:T(8,128)(2,1)S(1)}, u32[]{:S(2)}, u32[]{:S(2)}) %collective-permute-start.1) | collective-permute-done | bytes 67616 | tf_op jit(solution)/shard_map/ppermute | solution.py:27
  11.4 1.5 %collective-permute-start.5 = (bf16[8,4224]{1,0:T(8,128)(2,1)S(1)}, bf16[8,4224]{1,0:T(8,128)(2,1)S(1)}, u32[]{:S(2)}, u32[]{:S(2)}) collective-permute-start(bf16[8,4224]{1,0:T(8,128)(2,1)S(1)} %collective-permute-done.1), channel_id=1, source_target_pairs={{0,2},{1,3},{2,0},{3,1},{4,6},{5,7},{6,4},{7,5},{8,10},{9,11},{10,... | collective-permute-start | bytes 202760 | tf_op jit(solution)/shard_map/ppermute | solution.py:27
  12.9 0.0 collective-permute-done.2
  12.9 1.4 %collective-permute-start.6 = (bf16[8,4224]{1,0:T(8,128)(2,1)S(1)}, bf16[8,4224]{1,0:T(8,128)(2,1)S(1)}, u32[]{:S(2)}, u32[]{:S(2)}) collective-permute-start(bf16[8,4224]{1,0:T(8,128)(2,1)S(1)} %collective-permute-done.2), channel_id=1, source_target_pairs={{0,2},{1,3},{2,0},{3,1},{4,6},{5,7},{6,4},{7,5},{8,10},{9,11},{10,... | collective-permute-start | bytes 202760 | tf_op jit(solution)/shard_map/ppermute | solution.py:27
  14.3 0.0 collective-permute-done.3
  14.4 0.0 collective-permute-done.4
  14.4 1.3 %collective-permute-done.5 = bf16[8,4224]{1,0:T(8,128)(2,1)S(1)} collective-permute-done((bf16[8,4224]{1,0:T(8,128)(2,1)S(1)}, bf16[8,4224]{1,0:T(8,128)(2,1)S(1)}, u32[]{:S(2)}, u32[]{:S(2)}) %collective-permute-start.5) | collective-permute-done | bytes 67616 | tf_op jit(solution)/shard_map/ppermute | solution.py:27
  15.7 1.5 %collective-permute-done.6 = bf16[8,4224]{1,0:T(8,128)(2,1)S(1)} collective-permute-done((bf16[8,4224]{1,0:T(8,128)(2,1)S(1)}, bf16[8,4224]{1,0:T(8,128)(2,1)S(1)}, u32[]{:S(2)}, u32[]{:S(2)}) %collective-permute-start.6) | collective-permute-done | bytes 67616 | tf_op jit(solution)/shard_map/ppermute | solution.py:27
  17.2 0.1 collective-permute-start.7
  17.3 1.9 %collective-permute-done.7 = bf16[64,4224]{1,0:T(8,128)(2,1)S(1)} collective-permute-done((bf16[64,4224]{1,0:T(8,128)(2,1)S(1)}, bf16[64,4224]{1,0:T(8,128)(2,1)S(1)}, u32[]{:S(2)}, u32[]{:S(2)}) %collective-permute-start.7) | collective-permute-done | bytes 540704 | tf_op jit(solution)/shard_map/ppermute | solution.py:27
  19.3 25.2 %experts.1 = bf16[128,4096]{1,0:T(8,128)(2,1)S(1)} custom-call(s32[1]{0:T(128)} %bitcast.first_ref, bf16[128,4224]{1,0:T(8,128)(2,1)S(1)} %constant_dynamic-update-slice_fusion.8.x_ref, bf16[3072,4096]{1,0:T(8,128)(2,1)} %bitcast.36, bf16[3072,4096]{1,0:T(8,128)(2,1)} %bitcast.37, bf16[3072,4096]{1,0:T(8,128)(2,1)} %bitcast.38), custom_call_target="tpu_custom_call" | custom-call | tf_op jit(solution)/shard_map/experts/pallas_call | solution.py:186
  44.5 0.1 fusion.6
  44.6 0.2 collective-permute-start.8
  44.8 1.8 %collective-permute-done.8 = bf16[2,4,8,4096]{3,2,1,0:T(8,128)(2,1)S(1)} collective-permute-done((bf16[2,4,8,4096]{3,2,1,0:T(8,128)(2,1)S(1)}, bf16[2,4,8,4096]{3,2,1,0:T(8,128)(2,1)S(1)}, u32[]{:S(2)}, u32[]{:S(2)}) %collective-permute-start.8) | collective-permute-done | bytes 524320 | tf_op jit(solution)/shard_map/ppermute | solution.py:27
  46.6 0.1 fusion
  46.7 1.5 %collective-permute-start.10 = (bf16[2,8,4096]{2,1,0:T(8,128)(2,1)S(1)}, bf16[2,8,4096]{2,1,0:T(8,128)(2,1)S(1)}, u32[]{:S(2)}, u32[]{:S(2)}) collective-permute-start(bf16[2,8,4096]{2,1,0:T(8,128)(2,1)S(1)} %get-tuple-element.12), channel_id=1, source_target_pairs={{0,2},{1,3},{2,0},{3,1},{4,6},{5,7},{6,4},{7,5},{8,10},{9,11},{10,... | collective-permute-start | bytes 393224 | tf_op jit(solution)/shard_map/ppermute | solution.py:27
  48.2 0.6 collective-permute-start.9
  48.8 4.3 %collective-permute-done.10 = bf16[2,8,4096]{2,1,0:T(8,128)(2,1)S(1)} collective-permute-done((bf16[2,8,4096]{2,1,0:T(8,128)(2,1)S(1)}, bf16[2,8,4096]{2,1,0:T(8,128)(2,1)S(1)}, u32[]{:S(2)}, u32[]{:S(2)}) %collective-permute-start.10) | collective-permute-done | bytes 131104 | tf_op jit(solution)/shard_map/ppermute | solution.py:27
  53.2 1.6 %collective-permute-start.11 = (bf16[8,4096]{1,0:T(8,128)(2,1)S(1)}, bf16[8,4096]{1,0:T(8,128)(2,1)S(1)}, u32[]{:S(2)}, u32[]{:S(2)}) collective-permute-start(bf16[8,4096]{1,0:T(8,128)(2,1)S(1)} %get-tuple-element.13), channel_id=1, source_target_pairs={{0,8},{1,9},{2,10},{3,11},{4,12},{5,13},{6,14},{7,15},{8,0},{9,1},... | collective-permute-start | bytes 196616 | tf_op jit(solution)/shard_map/ppermute | solution.py:27
  54.8 1.7 %collective-permute-start.13 = (bf16[8,4096]{1,0:T(8,128)(2,1)S(1)}, bf16[8,4096]{1,0:T(8,128)(2,1)S(1)}, u32[]{:S(2)}, u32[]{:S(2)}) collective-permute-start(bf16[8,4096]{1,0:T(8,128)(2,1)S(1)} %get-tuple-element.14), channel_id=1, source_target_pairs={{0,12},{1,13},{2,14},{3,15},{4,8},{5,9},{6,10},{7,11},{8,4},{9,5},... | collective-permute-start | bytes 196616 | tf_op jit(solution)/shard_map/ppermute | solution.py:27
  56.5 0.0 collective-permute-done.9
  56.5 3.7 %collective-permute-done.11 = bf16[8,4096]{1,0:T(8,128)(2,1)S(1)} collective-permute-done((bf16[8,4096]{1,0:T(8,128)(2,1)S(1)}, bf16[8,4096]{1,0:T(8,128)(2,1)S(1)}, u32[]{:S(2)}, u32[]{:S(2)}) %collective-permute-start.11) | collective-permute-done | bytes 65568 | tf_op jit(solution)/shard_map/ppermute | solution.py:27
  60.2 0.1 collective-permute-start.12
  60.3 1.1 %collective-permute-done.13 = bf16[8,4096]{1,0:T(8,128)(2,1)S(1)} collective-permute-done((bf16[8,4096]{1,0:T(8,128)(2,1)S(1)}, bf16[8,4096]{1,0:T(8,128)(2,1)S(1)}, u32[]{:S(2)}, u32[]{:S(2)}) %collective-permute-start.13) | collective-permute-done | bytes 65568 | tf_op jit(solution)/shard_map/ppermute | solution.py:27
  61.5 3.1 %collective-permute-done.12 = bf16[8,4096]{1,0:T(8,128)(2,1)S(1)} collective-permute-done((bf16[8,4096]{1,0:T(8,128)(2,1)S(1)}, bf16[8,4096]{1,0:T(8,128)(2,1)S(1)}, u32[]{:S(2)}, u32[]{:S(2)}) %collective-permute-start.12) | collective-permute-done | bytes 65568 | tf_op jit(solution)/shard_map/ppermute | solution.py:27
  64.6 0.7 %fusion.5 = bf16[8,4096]{1,0:T(8,128)(2,1)} fusion(bf16[8,4096]{1,0:T(8,128)(2,1)S(1)} %collective-permute-done.13, bf16[8,4096]{1,0:T(8,128)(2,1)S(1)} %collective-permute-done.11, bf16[8,4096]{1,0:T(8,128)(2,1)S(1)} %collective-permute-done.12, bf16[2,8,4096]{2,1,0:T(8,128)(2,1)S(1)} %fusion.2), kind=kLoop, calls=%fused_computation.13 | loop fusion | flops 262144 | bytes 327680 | tf_op jit(solution)/shard_map/convert_element_type | solution.py:19
  (14 shorter events, 0.3 us)
Async XLA Ops:
  0.9 7.4 %collective-permute-start = (bf16[8,4224]{1,0:T(8,128)(2,1)S(1)}, bf16[8,4224]{1,0:T(8,128)(2,1)S(1)}, u32[]{:S(2)}, u32[]{:S(2)}) collective-permute-start(bf16[8,4224]{1,0:T(8,128)(2,1)S(1)} %message.1), channel_id=1, source_target_pairs={{0,4},{1,5},{2,6},{3,7},{4,0},{5,1},{6,2},{7,3},{8,12},{9,13},{10,... | collective-permute-start | bytes 202760 | tf_op jit(solution)/shard_map/ppermute | solution.py:27
  4.0 7.4 %collective-permute-start.1 = (bf16[8,4224]{1,0:T(8,128)(2,1)S(1)}, bf16[8,4224]{1,0:T(8,128)(2,1)S(1)}, u32[]{:S(2)}, u32[]{:S(2)}) collective-permute-start(bf16[8,4224]{1,0:T(8,128)(2,1)S(1)} %message.1), channel_id=1, source_target_pairs={{0,8},{1,9},{2,10},{3,11},{4,12},{5,13},{6,14},{7,15},{8,0},{9,1},... | collective-permute-start | bytes 202760 | tf_op jit(solution)/shard_map/ppermute | solution.py:27
  6.6 6.3 %collective-permute-start.2 = (bf16[8,4224]{1,0:T(8,128)(2,1)S(1)}, bf16[8,4224]{1,0:T(8,128)(2,1)S(1)}, u32[]{:S(2)}, u32[]{:S(2)}) collective-permute-start(bf16[8,4224]{1,0:T(8,128)(2,1)S(1)} %message.1), channel_id=1, source_target_pairs={{0,12},{1,13},{2,14},{3,15},{4,8},{5,9},{6,10},{7,11},{8,4},{9,5},... | collective-permute-start | bytes 202760 | tf_op jit(solution)/shard_map/ppermute | solution.py:27
  6.6 7.7 %collective-permute-start.3 = (bf16[8,4224]{1,0:T(8,128)(2,1)S(1)}, bf16[8,4224]{1,0:T(8,128)(2,1)S(1)}, u32[]{:S(2)}, u32[]{:S(2)}) collective-permute-start(bf16[8,4224]{1,0:T(8,128)(2,1)S(1)} %message.1), channel_id=1, source_target_pairs={{0,2},{1,3},{2,0},{3,1},{4,6},{5,7},{6,4},{7,5},{8,10},{9,11},{10,... | collective-permute-start | bytes 202760 | tf_op jit(solution)/shard_map/ppermute | solution.py:27
  8.3 6.0 %collective-permute-start.4 = (bf16[8,4224]{1,0:T(8,128)(2,1)S(1)}, bf16[8,4224]{1,0:T(8,128)(2,1)S(1)}, u32[]{:S(2)}, u32[]{:S(2)}) collective-permute-start(bf16[8,4224]{1,0:T(8,128)(2,1)S(1)} %collective-permute-done), channel_id=1, source_target_pairs={{0,2},{1,3},{2,0},{3,1},{4,6},{5,7},{6,4},{7,5},{8,10},{9,11},{10,... | collective-permute-start | bytes 202760 | tf_op jit(solution)/shard_map/ppermute | solution.py:27
  11.4 4.3 %collective-permute-start.5 = (bf16[8,4224]{1,0:T(8,128)(2,1)S(1)}, bf16[8,4224]{1,0:T(8,128)(2,1)S(1)}, u32[]{:S(2)}, u32[]{:S(2)}) collective-permute-start(bf16[8,4224]{1,0:T(8,128)(2,1)S(1)} %collective-permute-done.1), channel_id=1, source_target_pairs={{0,2},{1,3},{2,0},{3,1},{4,6},{5,7},{6,4},{7,5},{8,10},{9,11},{10,... | collective-permute-start | bytes 202760 | tf_op jit(solution)/shard_map/ppermute | solution.py:27
  12.9 4.3 %collective-permute-start.6 = (bf16[8,4224]{1,0:T(8,128)(2,1)S(1)}, bf16[8,4224]{1,0:T(8,128)(2,1)S(1)}, u32[]{:S(2)}, u32[]{:S(2)}) collective-permute-start(bf16[8,4224]{1,0:T(8,128)(2,1)S(1)} %collective-permute-done.2), channel_id=1, source_target_pairs={{0,2},{1,3},{2,0},{3,1},{4,6},{5,7},{6,4},{7,5},{8,10},{9,11},{10,... | collective-permute-start | bytes 202760 | tf_op jit(solution)/shard_map/ppermute | solution.py:27
  17.2 2.0 %collective-permute-start.7 = (bf16[64,4224]{1,0:T(8,128)(2,1)S(1)}, bf16[64,4224]{1,0:T(8,128)(2,1)S(1)}, u32[]{:S(2)}, u32[]{:S(2)}) collective-permute-start(bf16[64,4224]{1,0:T(8,128)(2,1)S(1)} %get-tuple-element.15), channel_id=1, source_target_pairs={{0,1},{1,0},{2,3},{3,2},{4,5},{5,4},{6,7},{7,6},{8,9},{9,8},{10,11... | collective-permute-start | bytes 1622024 | tf_op jit(solution)/shard_map/ppermute | solution.py:27
  44.6 2.0 %collective-permute-start.8 = (bf16[2,4,8,4096]{3,2,1,0:T(8,128)(2,1)S(1)}, bf16[2,4,8,4096]{3,2,1,0:T(8,128)(2,1)S(1)}, u32[]{:S(2)}, u32[]{:S(2)}) collective-permute-start(bf16[2,4,8,4096]{3,2,1,0:T(8,128)(2,1)S(1)} %bitcast.40), channel_id=1, source_target_pairs={{0,1},{1,0},{2,3},{3,2},{4,5},{5,4},{6,7},{7,6},{8,9},{9,8},{10,11... | collective-permute-start | bytes 1572872 | tf_op jit(solution)/shard_map/ppermute | solution.py:27
  46.7 6.4 %collective-permute-start.10 = (bf16[2,8,4096]{2,1,0:T(8,128)(2,1)S(1)}, bf16[2,8,4096]{2,1,0:T(8,128)(2,1)S(1)}, u32[]{:S(2)}, u32[]{:S(2)}) collective-permute-start(bf16[2,8,4096]{2,1,0:T(8,128)(2,1)S(1)} %get-tuple-element.12), channel_id=1, source_target_pairs={{0,2},{1,3},{2,0},{3,1},{4,6},{5,7},{6,4},{7,5},{8,10},{9,11},{10,... | collective-permute-start | bytes 393224 | tf_op jit(solution)/shard_map/ppermute | solution.py:27
  48.2 8.4 %collective-permute-start.9 = (bf16[2,8,4096]{2,1,0:T(8,128)(2,1)S(1)}, bf16[2,8,4096]{2,1,0:T(8,128)(2,1)S(1)}, u32[]{:S(2)}, u32[]{:S(2)}) collective-permute-start(bf16[2,8,4096]{2,1,0:T(8,128)(2,1)S(1)} %get-tuple-element.11), channel_id=1, source_target_pairs={{0,2},{1,3},{2,0},{3,1},{4,6},{5,7},{6,4},{7,5},{8,10},{9,11},{10,... | collective-permute-start | bytes 393224 | tf_op jit(solution)/shard_map/ppermute | solution.py:27
  53.2 7.0 %collective-permute-start.11 = (bf16[8,4096]{1,0:T(8,128)(2,1)S(1)}, bf16[8,4096]{1,0:T(8,128)(2,1)S(1)}, u32[]{:S(2)}, u32[]{:S(2)}) collective-permute-start(bf16[8,4096]{1,0:T(8,128)(2,1)S(1)} %get-tuple-element.13), channel_id=1, source_target_pairs={{0,8},{1,9},{2,10},{3,11},{4,12},{5,13},{6,14},{7,15},{8,0},{9,1},... | collective-permute-start | bytes 196616 | tf_op jit(solution)/shard_map/ppermute | solution.py:27
  54.8 6.7 %collective-permute-start.13 = (bf16[8,4096]{1,0:T(8,128)(2,1)S(1)}, bf16[8,4096]{1,0:T(8,128)(2,1)S(1)}, u32[]{:S(2)}, u32[]{:S(2)}) collective-permute-start(bf16[8,4096]{1,0:T(8,128)(2,1)S(1)} %get-tuple-element.14), channel_id=1, source_target_pairs={{0,12},{1,13},{2,14},{3,15},{4,8},{5,9},{6,10},{7,11},{8,4},{9,5},... | collective-permute-start | bytes 196616 | tf_op jit(solution)/shard_map/ppermute | solution.py:27
  60.2 4.3 %collective-permute-start.12 = (bf16[8,4096]{1,0:T(8,128)(2,1)S(1)}, bf16[8,4096]{1,0:T(8,128)(2,1)S(1)}, u32[]{:S(2)}, u32[]{:S(2)}) collective-permute-start(bf16[8,4096]{1,0:T(8,128)(2,1)S(1)} %slice_bitcast_fusion.5), channel_id=1, source_target_pairs={{0,4},{1,5},{2,6},{3,7},{4,0},{5,1},{6,2},{7,3},{8,12},{9,13},{10,... | collective-permute-start | bytes 196616 | tf_op jit(solution)/shard_map/ppermute | solution.py:27

commit v5 on v4

--- a/solution.py
+++ b/solution.py
@@ -31,34 +31,56 @@
     return sorted(range(1, ep_count), key=lambda m: (-m.bit_length(), m))
 
 
-def gather_rows(x, ep_count, dp_count):
+def pack_kernel(*refs):
+    out_ref = refs[-1]
+    rows = refs[0].shape[0]
+    for i, ref in enumerate(refs[:-1]):
+        out_ref[i * rows : (i + 1) * rows, :] = ref[...]
+
+
+def pack(blocks):
+    whole = pl.BlockSpec(memory_space=pltpu.VMEM)
+    shape = (len(blocks) * blocks[0].shape[0], blocks[0].shape[1])
+    return pl.pallas_call(
+        pack_kernel,
+        in_specs=[whole] * len(blocks),
+        out_specs=whole,
+        out_shape=jax.ShapeDtypeStruct(shape, BF16),
+        compiler_params=pltpu.CompilerParams(vmem_limit_bytes=3 << 20),
+        name="pack",
+    )(*blocks)
+
+
+def gather_rows(x, ep_count, dp_count, fetches):
     send = functools.partial(hop, ep_count=ep_count, dp_count=dp_count)
+    order = ep_order(ep_count)
     blocks = {(0, 0): x}
-    for m in ep_order(ep_count):
+    for m in order:
         blocks[m, 0] = send(x, ep_mask=m, dp_mask=0)
+    tiles = []
+    if len(order) > 1:
+        tile = fetches[0]([blocks[order[0], 0]])
+        blocks[order[1], 0], tile = lax.optimization_barrier((blocks[order[1], 0], tile))
+        tiles.append(tile)
     for d in range(2, dp_count, 2):
-        for m in [0] + ep_order(ep_count):
+        for m in [0] + order:
             blocks[m, d] = send(blocks[m, 0], ep_mask=0, dp_mask=d)
-    near = jnp.concatenate(
-        [blocks[m, d] for d in range(0, dp_count, 2) for m in range(ep_count)], axis=0
-    )
-    return jnp.concatenate([near, send(near, ep_mask=0, dp_mask=1)], axis=0)
+    if dp_count > 2:
+        last = order[-1]
+        tile = fetches[len(tiles)]([blocks[last, 0]])
+        blocks[last, 2], tile = lax.optimization_barrier((blocks[last, 2], tile))
+        tiles.append(tile)
+    near = pack([blocks[m, d] for d in range(0, dp_count, 2) for m in range(ep_count)])
+    return near, send(near, ep_mask=0, dp_mask=1), tiles
 
 
 def scatter_rows(y, ep_count, dp_count):
     send = functools.partial(hop, ep_count=ep_count, dp_count=dp_count)
-    rows, half = y.shape[0], ep_count // 2
+    rows = y.shape[0]
     y = y.reshape(2, dp_count // 2, ep_count, rows // (ep_count * dp_count), y.shape[1])
     y = add_up(y[0], send(y[1], ep_mask=0, dp_mask=1))
-    others = range(2, dp_count, 2)
-    far = [send(y[d // 2, half:], ep_mask=0, dp_mask=d) for d in others]
-    near = [send(y[d // 2, :half], ep_mask=0, dp_mask=d) for d in others]
-    far_sum = add_up(y[0, half:], *far)
-    far_sent = [send(far_sum[m - half], ep_mask=m, dp_mask=0) for m in range(half, ep_count)]
-    near, far_sent[0] = lax.optimization_barrier((near, far_sent[0]))
-    near_sum = add_up(y[0, :half], *near)
-    near_sent = [send(near_sum[m], ep_mask=m, dp_mask=0) for m in range(1, half)]
-    return add_up(near_sum[0], *near_sent, *far_sent)
+    y = add_up(y[0], *[send(y[d // 2], ep_mask=0, dp_mask=d) for d in range(2, dp_count, 2)])
+    return add_up(y[0], *[send(y[m], ep_mask=m, dp_mask=0) for m in ep_order(ep_count)])
 
 
 def message_kernel(expert_total, tokens_ref, ids_ref, scores_ref, out_ref, ids_buf, scores_buf, sem):
@@ -102,9 +124,42 @@
     )(*[pltpu.with_memory_space_constraint(a, pltpu.HBM) for a in operands])
 
 
-def experts_kernel(width, expert_total, step, piece, slots, down_slots,
-                   first_ref, x_ref, gate_ref, up_ref, down_ref, y_ref,
-                   h_ref, buf, down_buf, sem, down_sem):
+def fetch_kernel(first_row, gate_ref, up_ref, *refs):
+    out_ref, sem = refs[-2:]
+    step = out_ref.shape[0] // 2
+    copies = [
+        pltpu.make_async_copy(
+            ref.at[pl.ds(first_row, step), :], out_ref.at[pl.ds(k * step, step), :], sem.at[k]
+        )
+        for k, ref in enumerate((gate_ref, up_ref))
+    ]
+    for copy in copies:
+        copy.start()
+    for copy in copies:
+        copy.wait()
+
+
+def fetch(gate, up, tile, step, after):
+    model_width = gate.shape[1]
+    away = pl.BlockSpec(memory_space=pl.ANY)
+    return pl.pallas_call(
+        functools.partial(fetch_kernel, tile * step),
+        in_specs=[away] * (2 + len(after)),
+        out_specs=pl.BlockSpec(memory_space=pltpu.VMEM),
+        out_shape=pltpu.VMEM((2 * step, model_width), BF16),
+        scratch_shapes=[pltpu.SemaphoreType.DMA((2,))],
+        compiler_params=pltpu.CompilerParams(vmem_limit_bytes=1 << 20),
+        cost_estimate=pl.CostEstimate(
+            flops=0, bytes_accessed=4 * step * model_width, transcendentals=0
+        ),
+        name="fetch",
+    )(*[pltpu.with_memory_space_constraint(a, pltpu.HBM) for a in (gate, up)], *after)
+
+
+def experts_kernel(width, expert_total, step, piece, slots, down_slots, held,
+                   near_ref, far_ref, gate_ref, up_ref, down_ref, *refs):
+    held_refs = refs[:held]
+    y_ref, x_ref, h_ref, buf, down_buf, sem, down_sem = refs[held:]
     units, model_width = gate_ref.shape
     steps, pieces = units // step, model_width // piece
     per_step = -(-down_slots // slots)
@@ -125,23 +180,29 @@
             down_sem.at[slot],
         )
 
-    for i in range(slots):
+    for i in range(held, held + slots):
         tile_copy(0, i).start()
         tile_copy(1, i).start()
 
-    def hidden_step(i, carry):
+    first = lax.axis_index("ep") * (units // width)
+    near_count = near_ref.shape[0]
+    x_ref[:near_count, :] = near_ref[...]
+    x_ref[near_count:, :] = far_ref[...]
+
+    def hidden_tile(i, tile):
         shape = (step, x_ref.shape[1] - model_width)
-        expert = first_ref[0] + (lax.broadcasted_iota(jnp.int32, shape, 0) + i * step) // width
+        expert = first + (lax.broadcasted_iota(jnp.int32, shape, 0) + i * step) // width
         column = lax.rem(lax.broadcasted_iota(jnp.int32, shape, 1), expert_total)
         spread = (column == expert).astype(F32).astype(BF16)
         weight = lax.dot_general(spread, x_ref[:, model_width:], NT, preferred_element_type=F32)
+        acts = lax.dot_general(tile[...], x_ref[:, :model_width], NT, preferred_element_type=F32)
+        hidden = jax.nn.silu(acts[:step]) * acts[step:] * weight
+        h_ref[:, pl.ds(pl.multiple_of(i * step, step), step)] = hidden.T.astype(BF16)
+
+    def hidden_step(i, carry):
         tile_copy(0, i).wait()
         tile_copy(1, i).wait()
-        acts = lax.dot_general(
-            buf[lax.rem(i, slots)], x_ref[:, :model_width], NT, preferred_element_type=F32
-        )
-        hidden = jax.nn.silu(acts[:step]) * acts[step:] * weight
-        h_ref[:, pl.ds(pl.multiple_of(i * step, step), step)] = hidden.T.astype(BF16)
+        hidden_tile(i, buf.at[lax.rem(i, slots)])
 
         @pl.when(i + slots < steps)
         def _():
@@ -159,7 +220,9 @@
 
         return carry
 
-    lax.fori_loop(0, steps, hidden_step, 0)
+    for i in range(held):
+        hidden_tile(i, held_refs[i])
+    lax.fori_loop(held, steps, hidden_step, 0)
 
     def down_step(j, carry):
         down_copy(j).wait()
@@ -176,28 +239,37 @@
     lax.fori_loop(0, pieces, down_step, 0)
 
 
-def experts(rows, gate, up, down, first, width, expert_total):
-    token_count = rows.shape[0]
+def experts(near, far, gate, up, down, width, expert_total, tiles):
+    token_count = near.shape[0] + far.shape[0]
     units, model_width = gate.shape
     step, piece = 2 * width, 512
-    slots, down_slots = min(3, units // step), min(6, model_width // piece)
+    slots, down_slots = min(2, units // step - len(tiles)), min(5, model_width // piece)
     whole = pl.BlockSpec(memory_space=pltpu.VMEM)
     away = pl.BlockSpec(memory_space=pl.ANY)
     return pl.pallas_call(
-        functools.partial(experts_kernel, width, expert_total, step, piece, slots, down_slots),
-        in_specs=[pl.BlockSpec(memory_space=pltpu.SMEM), whole, away, away, away],
+        functools.partial(
+            experts_kernel, width, expert_total, step, piece, slots, down_slots, len(tiles)
+        ),
+        in_specs=[whole, whole, away, away, away]
+        + [whole] * len(tiles),
         out_specs=whole,
         out_shape=jax.ShapeDtypeStruct((token_count, model_width), BF16),
         scratch_shapes=[
+            pltpu.VMEM((token_count, near.shape[1]), BF16),
             pltpu.VMEM((token_count, units), BF16),
             pltpu.VMEM((slots, 2 * step, model_width), BF16),
             pltpu.VMEM((down_slots, units, piece), BF16),
             pltpu.SemaphoreType.DMA((2, slots)),
             pltpu.SemaphoreType.DMA((down_slots,)),
         ],
-        compiler_params=pltpu.CompilerParams(vmem_limit_bytes=44 << 20),
+        compiler_params=pltpu.CompilerParams(vmem_limit_bytes=34 << 20),
         name="experts",
-    )(first, rows, gate, up, down)
+    )(
+        near,
+        far,
+        *[pltpu.with_memory_space_constraint(a, pltpu.HBM) for a in (gate, up, down)],
+        *[pltpu.with_memory_space_constraint(t, pltpu.VMEM) for t in tiles],
+    )
 
 
 def experts_plain(rows, gate, up, down, first, width, expert_total):
@@ -227,9 +299,10 @@
     sent = message(tokens, expert_ids, gate_scores, expert_total)
 
     powers = all(n & (n - 1) == 0 for n in (ep_count, dp_count))
-    if powers and 2 <= ep_count <= 8 and 2 <= dp_count <= 8 and local_experts % 2 == 0:
-        rows = gather_rows(sent, ep_count, dp_count)
-        partial = experts(rows, gate, up, down, first, width, expert_total)
+    if powers and 2 <= ep_count <= 8 and 2 <= dp_count <= 8 and local_experts % 2 == 0 and local_experts >= 8:
+        fetches = [functools.partial(fetch, gate, up, tile, 2 * width) for tile in range(2)]
+        near, far, tiles = gather_rows(sent, ep_count, dp_count, fetches)
+        partial = experts(near, far, gate, up, down, width, expert_total, tiles)
         return scatter_rows(partial, ep_count, dp_count)
     rows = lax.all_gather(sent, ("ep", "dp"), axis=0, tiled=True)
     partial = experts_plain(rows, gate, up, down, first, width, expert_total)

time: 65.4 us -> 70 us (1.070)
  Pallas kernels: 26.2 us -> 33.1 us
  starting transfers between devices: 16.4 us -> 15.3 us
  waiting for transfers between devices: 21.4 us -> 20.4 us
    pallas_call x0 -> x3, Pallas kernels: none -> 5.76 us  [the longest x2 5.72 us: fetch(): pl.pallas_call(functools.partial(fetch_kernel, tile * step), in_specs=[aw...]
    pallas_call x1, Pallas kernels: 25.2 us -> 26.4 us  [experts(): pl.pallas_call(functools.partial(experts_kernel, width, expert_total, ste...]
    ppermute x14 -> x13, starting transfers between devices: 16.4 us -> 15.3 us  [hop(): return lax.ppermute(x, ('ep', 'dp'), pairs)]
    ppermute x14 -> x13, waiting for transfers between devices: 21.4 us -> 20.4 us  [hop(): return lax.ppermute(x, ('ep', 'dp'), pairs)]
  transfers between devices with their start and end apart: 14 -> 13, of which waited for: 9 -> 7; matrix products, arithmetic and copies ran while one was open for 0% -> 0% of each run, Pallas kernels for 0% -> 8%
where the time goes in v5:
time: 70 us; the launch traced here: 69.8 us
  Pallas kernels  33.1 us (47%)
  waiting for transfers between devices  20.4 us (29%)
  starting transfers between devices  15.3 us (22%)
  other arithmetic  0.85 us (1%)
    pallas_call x1, Pallas kernels, experts(): pl.pallas_call(functools.partial(experts_kernel, width, expert_total, ste...  26.4 us
    ppermute x13, waiting for transfers between devices, hop(): return lax.ppermute(x, ('ep', 'dp'), pairs)  20.4 us
    ppermute x13, starting transfers between devices, hop(): return lax.ppermute(x, ('ep', 'dp'), pairs)  15.3 us
    pallas_call x2, Pallas kernels, fetch(): pl.pallas_call(functools.partial(fetch_kernel, tile * step), in_specs=[aw...  5.72 us
  transfers between devices with their start and end apart: 13, of which 7 were waited for; matrix products, arithmetic and copies ran while one was open for 0% of the time, Pallas kernels for 8%

profile of v5, /device:TPU:0, one launch (start us, length us, event | category | flops | bytes accessed | tf_op | source)
XLA Modules:
  0.0 69.8 jit_solution(1209790937484831406)
XLA Ops:
  0.0 0.9 %message.1.refs_0_ = bf16[8,4224]{1,0:T(8,128)(2,1)S(1)} custom-call(bf16[8,4096]{1,0:T(8,128)(2,1)} %tokens_ref.1, s32[8,8]{1,0:T(8,128)} %ids_ref.1, f32[8,8]{1,0:T(8,128)} %scores_ref.1), custom_call_target="tpu_custom_call" | custom-call | tf_op jit(solution)/shard_map/message/pallas_call | solution.py:112
  0.9 3.1 %collective-permute-start = (bf16[8,4224]{1,0:T(8,128)(2,1)S(1)}, bf16[8,4224]{1,0:T(8,128)(2,1)S(1)}, u32[]{:S(2)}, u32[]{:S(2)}) collective-permute-start(bf16[8,4224]{1,0:T(8,128)(2,1)S(1)} %message.1.refs_0_), channel_id=1, source_target_pairs={{0,4},{1,5},{2,6},{3,7},{4,0},{5,1},{6,2},{7,3},{8,12},{9,13},{10,... | collective-permute-start | bytes 202760 | tf_op jit(solution)/shard_map/ppermute | solution.py:27
  4.0 2.6 %collective-permute-start.1 = (bf16[8,4224]{1,0:T(8,128)(2,1)S(1)}, bf16[8,4224]{1,0:T(8,128)(2,1)S(1)}, u32[]{:S(2)}, u32[]{:S(2)}) collective-permute-start(bf16[8,4224]{1,0:T(8,128)(2,1)S(1)} %message.1.refs_0_), channel_id=1, source_target_pairs={{0,8},{1,9},{2,10},{3,11},{4,12},{5,13},{6,14},{7,15},{8,0},{9,1},... | collective-permute-start | bytes 202760 | tf_op jit(solution)/shard_map/ppermute | solution.py:27
  6.6 0.0 collective-permute-start.2
  6.6 1.7 %collective-permute-start.3 = (bf16[8,4224]{1,0:T(8,128)(2,1)S(1)}, bf16[8,4224]{1,0:T(8,128)(2,1)S(1)}, u32[]{:S(2)}, u32[]{:S(2)}) collective-permute-start(bf16[8,4224]{1,0:T(8,128)(2,1)S(1)} %message.1.refs_0_), channel_id=1, source_target_pairs={{0,2},{1,3},{2,0},{3,1},{4,6},{5,7},{6,4},{7,5},{8,10},{9,11},{10,... | collective-permute-start | bytes 202760 | tf_op jit(solution)/shard_map/ppermute | solution.py:27
  8.3 0.0 collective-permute-done.refs_0_.refs_1_
  8.3 0.3 collective-permute-start.4
  8.6 2.8 %collective-permute-done.1.refs_0_.refs_2_ = bf16[8,4224]{1,0:T(8,128)(2,1)S(1)} collective-permute-done((bf16[8,4224]{1,0:T(8,128)(2,1)S(1)}, bf16[8,4224]{1,0:T(8,128)(2,1)S(1)}, u32[]{:S(2)}, u32[]{:S(2)}) %collective-permute-start.1) | collective-permute-done | bytes 67616 | tf_op jit(solution)/shard_map/ppermute | solution.py:27
  11.4 2.9 %fetch.2.refs_0_ = bf16[768,4096]{1,0:T(8,128)(2,1)S(1)} custom-call(bf16[3072,4096]{1,0:T(8,128)(2,1)} %bitcast.28, bf16[3072,4096]{1,0:T(8,128)(2,1)} %bitcast.31, bf16[8,4224]{1,0:T(8,128)(2,1)S(1)} %collective-permute-done.1.refs_0_.refs_2_), custom_call_target="tpu_custom_call" | custom-call | bytes 6291456 | tf_op jit(solution)/shard_map/fetch/pallas_call | solution.py:145
  14.3 0.0 collective-permute-done.2.refs_3_
  14.3 1.6 %collective-permute-start.5 = (bf16[8,4224]{1,0:T(8,128)(2,1)S(1)}, bf16[8,4224]{1,0:T(8,128)(2,1)S(1)}, u32[]{:S(2)}, u32[]{:S(2)}) collective-permute-start(bf16[8,4224]{1,0:T(8,128)(2,1)S(1)} %collective-permute-done.1.refs_0_.refs_2_), channel_id=1, source_target_pairs={{0,2},{1,3},{2,0},{3,1},{4,6},{5,7},{6,4},{7,5},{8,10},{9,11},{10,... | collective-permute-start | bytes 202760 | tf_op jit(solution)/shard_map/ppermute | solution.py:27
  15.8 0.5 collective-permute-start.6
  16.4 2.9 %fetch.3.refs_1_ = bf16[768,4096]{1,0:T(8,128)(2,1)S(1)} custom-call(bf16[3072,4096]{1,0:T(8,128)(2,1)} %bitcast.29, bf16[3072,4096]{1,0:T(8,128)(2,1)} %bitcast.32, bf16[8,4224]{1,0:T(8,128)(2,1)S(1)} %collective-permute-done.refs_0_.refs_1_), custom_call_target="tpu_custom_call" | custom-call | bytes 6291456 | tf_op jit(solution)/shard_map/fetch/pallas_call | solution.py:145
  19.2 0.0 collective-permute-done.4.refs_5_
  19.3 0.0 collective-permute-done.3.refs_4_
  19.3 0.0 collective-permute-done.5.refs_6_
  19.3 0.9 %collective-permute-done.6.refs_7_ = bf16[8,4224]{1,0:T(8,128)(2,1)S(1)} collective-permute-done((bf16[8,4224]{1,0:T(8,128)(2,1)S(1)}, bf16[8,4224]{1,0:T(8,128)(2,1)S(1)}, u32[]{:S(2)}, u32[]{:S(2)}) %collective-permute-start.6) | collective-permute-done | bytes 67616 | tf_op jit(solution)/shard_map/ppermute | solution.py:27
  20.2 0.1 collective-permute-start.7
  20.2 1.9 %collective-permute-done.7.far_ref = bf16[64,4224]{1,0:T(8,128)(2,1)S(1)} collective-permute-done((bf16[64,4224]{1,0:T(8,128)(2,1)S(1)}, bf16[64,4224]{1,0:T(8,128)(2,1)S(1)}, u32[]{:S(2)}, u32[]{:S(2)}) %collective-permute-start.7) | collective-permute-done | bytes 540704 | tf_op jit(solution)/shard_map/ppermute | solution.py:27
  22.2 26.4 %experts.1 = bf16[128,4096]{1,0:T(8,128)(2,1)S(1)} custom-call(bf16[64,4224]{1,0:T(8,128)(2,1)S(1)} %pack.1.near_ref, bf16[64,4224]{1,0:T(8,128)(2,1)S(1)} %collective-permute-done.7.far_ref, bf16[3072,4096]{1,0:T(8,128)(2,1)} %bitcast.30, bf16[3072,4096]{1,0:T(8,128)(2,1)} %bitcast.33, bf16[3072,4096]{1,0:T(8,128)(2,1)} %bitcast.34, ...), custom_call_target="tpu_custom_call" | custom-call | tf_op jit(solution)/shard_map/experts/pallas_call | solution.py:249
  48.6 0.1 fusion.5
  48.6 0.2 collective-permute-start.8
  48.8 1.8 %collective-permute-done.8 = bf16[2,4,8,4096]{3,2,1,0:T(8,128)(2,1)S(1)} collective-permute-done((bf16[2,4,8,4096]{3,2,1,0:T(8,128)(2,1)S(1)}, bf16[2,4,8,4096]{3,2,1,0:T(8,128)(2,1)S(1)}, u32[]{:S(2)}, u32[]{:S(2)}) %collective-permute-start.8) | collective-permute-done | bytes 524320 | tf_op jit(solution)/shard_map/ppermute | solution.py:27
  50.6 0.1 fusion
  50.8 0.8 %collective-permute-start.9 = (bf16[4,8,4096]{2,1,0:T(8,128)(2,1)S(1)}, bf16[4,8,4096]{2,1,0:T(8,128)(2,1)S(1)}, u32[]{:S(2)}, u32[]{:S(2)}) collective-permute-start(bf16[4,8,4096]{2,1,0:T(8,128)(2,1)S(1)} %slice_bitcast_fusion), channel_id=1, source_target_pairs={{0,2},{1,3},{2,0},{3,1},{4,6},{5,7},{6,4},{7,5},{8,10},{9,11},{10,... | collective-permute-start | bytes 786440 | tf_op jit(solution)/shard_map/ppermute | solution.py:27
  51.6 7.6 %collective-permute-done.9 = bf16[4,8,4096]{2,1,0:T(8,128)(2,1)S(1)} collective-permute-done((bf16[4,8,4096]{2,1,0:T(8,128)(2,1)S(1)}, bf16[4,8,4096]{2,1,0:T(8,128)(2,1)S(1)}, u32[]{:S(2)}, u32[]{:S(2)}) %collective-permute-start.9) | collective-permute-done | bytes 262176 | tf_op jit(solution)/shard_map/ppermute | solution.py:27
  59.2 0.1 fusion.1
  59.3 0.6 collective-permute-start.10
  59.8 3.2 %collective-permute-start.12 = (bf16[8,4096]{1,0:T(8,128)(2,1)S(1)}, bf16[8,4096]{1,0:T(8,128)(2,1)S(1)}, u32[]{:S(2)}, u32[]{:S(2)}) collective-permute-start(bf16[8,4096]{1,0:T(8,128)(2,1)S(1)} %get-tuple-element.16), channel_id=1, source_target_pairs={{0,4},{1,5},{2,6},{3,7},{4,0},{5,1},{6,2},{7,3},{8,12},{9,13},{10,... | collective-permute-start | bytes 196616 | tf_op jit(solution)/shard_map/ppermute | solution.py:27
  63.1 0.6 collective-permute-start.11
  63.7 1.9 %collective-permute-done.10 = bf16[8,4096]{1,0:T(8,128)(2,1)S(1)} collective-permute-done((bf16[8,4096]{1,0:T(8,128)(2,1)S(1)}, bf16[8,4096]{1,0:T(8,128)(2,1)S(1)}, u32[]{:S(2)}, u32[]{:S(2)}) %collective-permute-start.10) | collective-permute-done | bytes 65568 | tf_op jit(solution)/shard_map/ppermute | solution.py:27
  65.6 0.0 collective-permute-done.12
  65.7 3.5 %collective-permute-done.11 = bf16[8,4096]{1,0:T(8,128)(2,1)S(1)} collective-permute-done((bf16[8,4096]{1,0:T(8,128)(2,1)S(1)}, bf16[8,4096]{1,0:T(8,128)(2,1)S(1)}, u32[]{:S(2)}, u32[]{:S(2)}) %collective-permute-start.11) | collective-permute-done | bytes 65568 | tf_op jit(solution)/shard_map/ppermute | solution.py:27
  69.2 0.7 fusion.4
  (3 shorter events, 0.1 us)
Async XLA Ops:
  0.9 7.4 %collective-permute-start = (bf16[8,4224]{1,0:T(8,128)(2,1)S(1)}, bf16[8,4224]{1,0:T(8,128)(2,1)S(1)}, u32[]{:S(2)}, u32[]{:S(2)}) collective-permute-start(bf16[8,4224]{1,0:T(8,128)(2,1)S(1)} %message.1.refs_0_), channel_id=1, source_target_pairs={{0,4},{1,5},{2,6},{3,7},{4,0},{5,1},{6,2},{7,3},{8,12},{9,13},{10,... | collective-permute-start | bytes 202760 | tf_op jit(solution)/shard_map/ppermute | solution.py:27
  4.0 7.4 %collective-permute-start.1 = (bf16[8,4224]{1,0:T(8,128)(2,1)S(1)}, bf16[8,4224]{1,0:T(8,128)(2,1)S(1)}, u32[]{:S(2)}, u32[]{:S(2)}) collective-permute-start(bf16[8,4224]{1,0:T(8,128)(2,1)S(1)} %message.1.refs_0_), channel_id=1, source_target_pairs={{0,8},{1,9},{2,10},{3,11},{4,12},{5,13},{6,14},{7,15},{8,0},{9,1},... | collective-permute-start | bytes 202760 | tf_op jit(solution)/shard_map/ppermute | solution.py:27
  6.6 7.7 %collective-permute-start.2 = (bf16[8,4224]{1,0:T(8,128)(2,1)S(1)}, bf16[8,4224]{1,0:T(8,128)(2,1)S(1)}, u32[]{:S(2)}, u32[]{:S(2)}) collective-permute-start(bf16[8,4224]{1,0:T(8,128)(2,1)S(1)} %message.1.refs_0_), channel_id=1, source_target_pairs={{0,12},{1,13},{2,14},{3,15},{4,8},{5,9},{6,10},{7,11},{8,4},{9,5},... | collective-permute-start | bytes 202760 | tf_op jit(solution)/shard_map/ppermute | solution.py:27
  6.6 12.7 %collective-permute-start.3 = (bf16[8,4224]{1,0:T(8,128)(2,1)S(1)}, bf16[8,4224]{1,0:T(8,128)(2,1)S(1)}, u32[]{:S(2)}, u32[]{:S(2)}) collective-permute-start(bf16[8,4224]{1,0:T(8,128)(2,1)S(1)} %message.1.refs_0_), channel_id=1, source_target_pairs={{0,2},{1,3},{2,0},{3,1},{4,6},{5,7},{6,4},{7,5},{8,10},{9,11},{10,... | collective-permute-start | bytes 202760 | tf_op jit(solution)/shard_map/ppermute | solution.py:27
  8.3 10.9 %collective-permute-start.4 = (bf16[8,4224]{1,0:T(8,128)(2,1)S(1)}, bf16[8,4224]{1,0:T(8,128)(2,1)S(1)}, u32[]{:S(2)}, u32[]{:S(2)}) collective-permute-start(bf16[8,4224]{1,0:T(8,128)(2,1)S(1)} %collective-permute-done.refs_0_.refs_1_), channel_id=1, source_target_pairs={{0,2},{1,3},{2,0},{3,1},{4,6},{5,7},{6,4},{7,5},{8,10},{9,11},{10,... | collective-permute-start | bytes 202760 | tf_op jit(solution)/shard_map/ppermute | solution.py:27
  14.3 5.0 %collective-permute-start.5 = (bf16[8,4224]{1,0:T(8,128)(2,1)S(1)}, bf16[8,4224]{1,0:T(8,128)(2,1)S(1)}, u32[]{:S(2)}, u32[]{:S(2)}) collective-permute-start(bf16[8,4224]{1,0:T(8,128)(2,1)S(1)} %collective-permute-done.1.refs_0_.refs_2_), channel_id=1, source_target_pairs={{0,2},{1,3},{2,0},{3,1},{4,6},{5,7},{6,4},{7,5},{8,10},{9,11},{10,... | collective-permute-start | bytes 202760 | tf_op jit(solution)/shard_map/ppermute | solution.py:27
  15.8 4.3 %collective-permute-start.6 = (bf16[8,4224]{1,0:T(8,128)(2,1)S(1)}, bf16[8,4224]{1,0:T(8,128)(2,1)S(1)}, u32[]{:S(2)}, u32[]{:S(2)}) collective-permute-start(bf16[8,4224]{1,0:T(8,128)(2,1)S(1)} %collective-permute-done.2.refs_3_), channel_id=1, source_target_pairs={{0,2},{1,3},{2,0},{3,1},{4,6},{5,7},{6,4},{7,5},{8,10},{9,11},{10,... | collective-permute-start | bytes 202760 | tf_op jit(solution)/shard_map/ppermute | solution.py:27
  20.2 2.0 %collective-permute-start.7 = (bf16[64,4224]{1,0:T(8,128)(2,1)S(1)}, bf16[64,4224]{1,0:T(8,128)(2,1)S(1)}, u32[]{:S(2)}, u32[]{:S(2)}) collective-permute-start(bf16[64,4224]{1,0:T(8,128)(2,1)S(1)} %pack.1.near_ref), channel_id=1, source_target_pairs={{0,1},{1,0},{2,3},{3,2},{4,5},{5,4},{6,7},{7,6},{8,9},{9,8},{10,11... | collective-permute-start | bytes 1622024 | tf_op jit(solution)/shard_map/ppermute | solution.py:27
  48.6 2.0 %collective-permute-start.8 = (bf16[2,4,8,4096]{3,2,1,0:T(8,128)(2,1)S(1)}, bf16[2,4,8,4096]{3,2,1,0:T(8,128)(2,1)S(1)}, u32[]{:S(2)}, u32[]{:S(2)}) collective-permute-start(bf16[2,4,8,4096]{3,2,1,0:T(8,128)(2,1)S(1)} %bitcast.36), channel_id=1, source_target_pairs={{0,1},{1,0},{2,3},{3,2},{4,5},{5,4},{6,7},{7,6},{8,9},{9,8},{10,11... | collective-permute-start | bytes 1572872 | tf_op jit(solution)/shard_map/ppermute | solution.py:27
  50.8 8.4 %collective-permute-start.9 = (bf16[4,8,4096]{2,1,0:T(8,128)(2,1)S(1)}, bf16[4,8,4096]{2,1,0:T(8,128)(2,1)S(1)}, u32[]{:S(2)}, u32[]{:S(2)}) collective-permute-start(bf16[4,8,4096]{2,1,0:T(8,128)(2,1)S(1)} %slice_bitcast_fusion), channel_id=1, source_target_pairs={{0,2},{1,3},{2,0},{3,1},{4,6},{5,7},{6,4},{7,5},{8,10},{9,11},{10,... | collective-permute-start | bytes 786440 | tf_op jit(solution)/shard_map/ppermute | solution.py:27
  59.3 6.4 %collective-permute-start.10 = (bf16[8,4096]{1,0:T(8,128)(2,1)S(1)}, bf16[8,4096]{1,0:T(8,128)(2,1)S(1)}, u32[]{:S(2)}, u32[]{:S(2)}) collective-permute-start(bf16[8,4096]{1,0:T(8,128)(2,1)S(1)} %get-tuple-element.15), channel_id=1, source_target_pairs={{0,8},{1,9},{2,10},{3,11},{4,12},{5,13},{6,14},{7,15},{8,0},{9,1},... | collective-permute-start | bytes 196616 | tf_op jit(solution)/shard_map/ppermute | solution.py:27
  59.8 5.8 %collective-permute-start.12 = (bf16[8,4096]{1,0:T(8,128)(2,1)S(1)}, bf16[8,4096]{1,0:T(8,128)(2,1)S(1)}, u32[]{:S(2)}, u32[]{:S(2)}) collective-permute-start(bf16[8,4096]{1,0:T(8,128)(2,1)S(1)} %get-tuple-element.16), channel_id=1, source_target_pairs={{0,4},{1,5},{2,6},{3,7},{4,0},{5,1},{6,2},{7,3},{8,12},{9,13},{10,... | collective-permute-start | bytes 196616 | tf_op jit(solution)/shard_map/ppermute | solution.py:27
  63.1 6.1 %collective-permute-start.11 = (bf16[8,4096]{1,0:T(8,128)(2,1)S(1)}, bf16[8,4096]{1,0:T(8,128)(2,1)S(1)}, u32[]{:S(2)}, u32[]{:S(2)}) collective-permute-start(bf16[8,4096]{1,0:T(8,128)(2,1)S(1)} %get-tuple-element.17), channel_id=1, source_target_pairs={{0,12},{1,13},{2,14},{3,15},{4,8},{5,9},{6,10},{7,11},{8,4},{9,5},... | collective-permute-start | bytes 196616 | tf_op jit(solution)/shard_map/ppermute | solution.py:27

commit v6 on v4

--- a/solution.py
+++ b/solution.py
@@ -47,18 +47,11 @@
 
 def scatter_rows(y, ep_count, dp_count):
     send = functools.partial(hop, ep_count=ep_count, dp_count=dp_count)
-    rows, half = y.shape[0], ep_count // 2
+    rows = y.shape[0]
     y = y.reshape(2, dp_count // 2, ep_count, rows // (ep_count * dp_count), y.shape[1])
     y = add_up(y[0], send(y[1], ep_mask=0, dp_mask=1))
-    others = range(2, dp_count, 2)
-    far = [send(y[d // 2, half:], ep_mask=0, dp_mask=d) for d in others]
-    near = [send(y[d // 2, :half], ep_mask=0, dp_mask=d) for d in others]
-    far_sum = add_up(y[0, half:], *far)
-    far_sent = [send(far_sum[m - half], ep_mask=m, dp_mask=0) for m in range(half, ep_count)]
-    near, far_sent[0] = lax.optimization_barrier((near, far_sent[0]))
-    near_sum = add_up(y[0, :half], *near)
-    near_sent = [send(near_sum[m], ep_mask=m, dp_mask=0) for m in range(1, half)]
-    return add_up(near_sum[0], *near_sent, *far_sent)
+    y = add_up(y[0], *[send(y[d // 2], ep_mask=0, dp_mask=d) for d in range(2, dp_count, 2)])
+    return add_up(y[0], *[send(y[m], ep_mask=m, dp_mask=0) for m in ep_order(ep_count)])
 
 
 def message_kernel(expert_total, tokens_ref, ids_ref, scores_ref, out_ref, ids_buf, scores_buf, sem):

time: 65.4 us -> 64.5 us (0.986)
  waiting for transfers between devices: 21.4 us -> 20.7 us
    ppermute x14 -> x13, waiting for transfers between devices: 21.4 us -> 20.7 us  [hop(): return lax.ppermute(x, ('ep', 'dp'), pairs)]
    ppermute x14 -> x13, starting transfers between devices: 16.4 us -> 16.2 us  [hop(): return lax.ppermute(x, ('ep', 'dp'), pairs)]
  transfers between devices with their start and end apart: 14 -> 13, of which waited for: 9 -> 8; matrix products, arithmetic and copies ran while one was open for 0% -> 0% of each run, Pallas kernels for 0% -> 0%
where the time goes in v6:
time: 64.5 us; the launch traced here: 64.3 us
  Pallas kernels  26.2 us (41%)
  waiting for transfers between devices  20.7 us (32%)
  starting transfers between devices  16.2 us (25%)
  other arithmetic  0.85 us (1%)
    pallas_call x1, Pallas kernels, experts(): pl.pallas_call(functools.partial(experts_kernel, width, expert_total, ste...  25.2 us
    ppermute x13, waiting for transfers between devices, hop(): return lax.ppermute(x, ('ep', 'dp'), pairs)  20.7 us
    ppermute x13, starting transfers between devices, hop(): return lax.ppermute(x, ('ep', 'dp'), pairs)  16.2 us
  transfers between devices with their start and end apart: 13, of which 8 were waited for; matrix products, arithmetic and copies ran while one was open for 0% of the time, Pallas kernels for 0%

profile of v6, /device:TPU:0, one launch (start us, length us, event | category | flops | bytes accessed | tf_op | source)
XLA Modules:
  0.0 64.3 jit_solution(11746205573808796538)
XLA Ops:
  0.0 0.9 %message.1 = bf16[8,4224]{1,0:T(8,128)(2,1)S(1)} custom-call(bf16[8,4096]{1,0:T(8,128)(2,1)} %tokens_ref.1, s32[8,8]{1,0:T(8,128)} %ids_ref.1, f32[8,8]{1,0:T(8,128)} %scores_ref.1), custom_call_target="tpu_custom_call" | custom-call | tf_op jit(solution)/shard_map/message/pallas_call | solution.py:83
  0.9 3.1 %collective-permute-start = (bf16[8,4224]{1,0:T(8,128)(2,1)S(1)}, bf16[8,4224]{1,0:T(8,128)(2,1)S(1)}, u32[]{:S(2)}, u32[]{:S(2)}) collective-permute-start(bf16[8,4224]{1,0:T(8,128)(2,1)S(1)} %message.1), channel_id=1, source_target_pairs={{0,4},{1,5},{2,6},{3,7},{4,0},{5,1},{6,2},{7,3},{8,12},{9,13},{10,... | collective-permute-start | bytes 202760 | tf_op jit(solution)/shard_map/ppermute | solution.py:27
  4.0 2.6 %collective-permute-start.1 = (bf16[8,4224]{1,0:T(8,128)(2,1)S(1)}, bf16[8,4224]{1,0:T(8,128)(2,1)S(1)}, u32[]{:S(2)}, u32[]{:S(2)}) collective-permute-start(bf16[8,4224]{1,0:T(8,128)(2,1)S(1)} %message.1), channel_id=1, source_target_pairs={{0,8},{1,9},{2,10},{3,11},{4,12},{5,13},{6,14},{7,15},{8,0},{9,1},... | collective-permute-start | bytes 202760 | tf_op jit(solution)/shard_map/ppermute | solution.py:27
  6.6 0.0 collective-permute-start.2
  6.6 1.7 %collective-permute-start.3 = (bf16[8,4224]{1,0:T(8,128)(2,1)S(1)}, bf16[8,4224]{1,0:T(8,128)(2,1)S(1)}, u32[]{:S(2)}, u32[]{:S(2)}) collective-permute-start(bf16[8,4224]{1,0:T(8,128)(2,1)S(1)} %message.1), channel_id=1, source_target_pairs={{0,2},{1,3},{2,0},{3,1},{4,6},{5,7},{6,4},{7,5},{8,10},{9,11},{10,... | collective-permute-start | bytes 202760 | tf_op jit(solution)/shard_map/ppermute | solution.py:27
  8.3 0.0 collective-permute-done
  8.3 0.4 collective-permute-start.4
  8.7 2.7 %collective-permute-done.1 = bf16[8,4224]{1,0:T(8,128)(2,1)S(1)} collective-permute-done((bf16[8,4224]{1,0:T(8,128)(2,1)S(1)}, bf16[8,4224]{1,0:T(8,128)(2,1)S(1)}, u32[]{:S(2)}, u32[]{:S(2)}) %collective-permute-start.1) | collective-permute-done | bytes 67616 | tf_op jit(solution)/shard_map/ppermute | solution.py:27
  11.4 1.5 %collective-permute-start.5 = (bf16[8,4224]{1,0:T(8,128)(2,1)S(1)}, bf16[8,4224]{1,0:T(8,128)(2,1)S(1)}, u32[]{:S(2)}, u32[]{:S(2)}) collective-permute-start(bf16[8,4224]{1,0:T(8,128)(2,1)S(1)} %collective-permute-done.1), channel_id=1, source_target_pairs={{0,2},{1,3},{2,0},{3,1},{4,6},{5,7},{6,4},{7,5},{8,10},{9,11},{10,... | collective-permute-start | bytes 202760 | tf_op jit(solution)/shard_map/ppermute | solution.py:27
  12.9 0.0 collective-permute-done.2
  12.9 1.4 %collective-permute-start.6 = (bf16[8,4224]{1,0:T(8,128)(2,1)S(1)}, bf16[8,4224]{1,0:T(8,128)(2,1)S(1)}, u32[]{:S(2)}, u32[]{:S(2)}) collective-permute-start(bf16[8,4224]{1,0:T(8,128)(2,1)S(1)} %collective-permute-done.2), channel_id=1, source_target_pairs={{0,2},{1,3},{2,0},{3,1},{4,6},{5,7},{6,4},{7,5},{8,10},{9,11},{10,... | collective-permute-start | bytes 202760 | tf_op jit(solution)/shard_map/ppermute | solution.py:27
  14.3 0.0 collective-permute-done.3
  14.4 0.0 collective-permute-done.4
  14.4 1.3 %collective-permute-done.5 = bf16[8,4224]{1,0:T(8,128)(2,1)S(1)} collective-permute-done((bf16[8,4224]{1,0:T(8,128)(2,1)S(1)}, bf16[8,4224]{1,0:T(8,128)(2,1)S(1)}, u32[]{:S(2)}, u32[]{:S(2)}) %collective-permute-start.5) | collective-permute-done | bytes 67616 | tf_op jit(solution)/shard_map/ppermute | solution.py:27
  15.7 1.5 %collective-permute-done.6 = bf16[8,4224]{1,0:T(8,128)(2,1)S(1)} collective-permute-done((bf16[8,4224]{1,0:T(8,128)(2,1)S(1)}, bf16[8,4224]{1,0:T(8,128)(2,1)S(1)}, u32[]{:S(2)}, u32[]{:S(2)}) %collective-permute-start.6) | collective-permute-done | bytes 67616 | tf_op jit(solution)/shard_map/ppermute | solution.py:27
  17.2 0.1 collective-permute-start.7
  17.3 1.9 %collective-permute-done.7 = bf16[64,4224]{1,0:T(8,128)(2,1)S(1)} collective-permute-done((bf16[64,4224]{1,0:T(8,128)(2,1)S(1)}, bf16[64,4224]{1,0:T(8,128)(2,1)S(1)}, u32[]{:S(2)}, u32[]{:S(2)}) %collective-permute-start.7) | collective-permute-done | bytes 540704 | tf_op jit(solution)/shard_map/ppermute | solution.py:27
  19.3 25.2 %experts.1 = bf16[128,4096]{1,0:T(8,128)(2,1)S(1)} custom-call(s32[1]{0:T(128)} %bitcast.first_ref, bf16[128,4224]{1,0:T(8,128)(2,1)S(1)} %constant_dynamic-update-slice_fusion.8.x_ref, bf16[3072,4096]{1,0:T(8,128)(2,1)} %bitcast.29, bf16[3072,4096]{1,0:T(8,128)(2,1)} %bitcast.30, bf16[3072,4096]{1,0:T(8,128)(2,1)} %bitcast.31), custom_call_target="tpu_custom_call" | custom-call | tf_op jit(solution)/shard_map/experts/pallas_call | solution.py:179
  44.5 0.1 fusion.5
  44.6 0.2 collective-permute-start.8
  44.8 1.8 %collective-permute-done.8 = bf16[2,4,8,4096]{3,2,1,0:T(8,128)(2,1)S(1)} collective-permute-done((bf16[2,4,8,4096]{3,2,1,0:T(8,128)(2,1)S(1)}, bf16[2,4,8,4096]{3,2,1,0:T(8,128)(2,1)S(1)}, u32[]{:S(2)}, u32[]{:S(2)}) %collective-permute-start.8) | collective-permute-done | bytes 524320 | tf_op jit(solution)/shard_map/ppermute | solution.py:27
  46.6 0.1 fusion
  46.7 1.5 %collective-permute-start.9 = (bf16[4,8,4096]{2,1,0:T(8,128)(2,1)S(1)}, bf16[4,8,4096]{2,1,0:T(8,128)(2,1)S(1)}, u32[]{:S(2)}, u32[]{:S(2)}) collective-permute-start(bf16[4,8,4096]{2,1,0:T(8,128)(2,1)S(1)} %slice_bitcast_fusion), channel_id=1, source_target_pairs={{0,2},{1,3},{2,0},{3,1},{4,6},{5,7},{6,4},{7,5},{8,10},{9,11},{10,... | collective-permute-start | bytes 786440 | tf_op jit(solution)/shard_map/ppermute | solution.py:27
  48.2 7.0 %collective-permute-done.9 = bf16[4,8,4096]{2,1,0:T(8,128)(2,1)S(1)} collective-permute-done((bf16[4,8,4096]{2,1,0:T(8,128)(2,1)S(1)}, bf16[4,8,4096]{2,1,0:T(8,128)(2,1)S(1)}, u32[]{:S(2)}, u32[]{:S(2)}) %collective-permute-start.9) | collective-permute-done | bytes 262176 | tf_op jit(solution)/shard_map/ppermute | solution.py:27
  55.1 0.1 fusion.1
  55.2 1.6 %collective-permute-start.10 = (bf16[8,4096]{1,0:T(8,128)(2,1)S(1)}, bf16[8,4096]{1,0:T(8,128)(2,1)S(1)}, u32[]{:S(2)}, u32[]{:S(2)}) collective-permute-start(bf16[8,4096]{1,0:T(8,128)(2,1)S(1)} %get-tuple-element.7), channel_id=1, source_target_pairs={{0,8},{1,9},{2,10},{3,11},{4,12},{5,13},{6,14},{7,15},{8,0},{9,1},... | collective-permute-start | bytes 196616 | tf_op jit(solution)/shard_map/ppermute | solution.py:27
  56.8 1.7 %collective-permute-start.11 = (bf16[8,4096]{1,0:T(8,128)(2,1)S(1)}, bf16[8,4096]{1,0:T(8,128)(2,1)S(1)}, u32[]{:S(2)}, u32[]{:S(2)}) collective-permute-start(bf16[8,4096]{1,0:T(8,128)(2,1)S(1)} %get-tuple-element.9), channel_id=1, source_target_pairs={{0,12},{1,13},{2,14},{3,15},{4,8},{5,9},{6,10},{7,11},{8,4},{9,5},... | collective-permute-start | bytes 196616 | tf_op jit(solution)/shard_map/ppermute | solution.py:27
  58.6 0.5 collective-permute-start.12
  59.1 4.0 %collective-permute-done.10 = bf16[8,4096]{1,0:T(8,128)(2,1)S(1)} collective-permute-done((bf16[8,4096]{1,0:T(8,128)(2,1)S(1)}, bf16[8,4096]{1,0:T(8,128)(2,1)S(1)}, u32[]{:S(2)}, u32[]{:S(2)}) %collective-permute-start.10) | collective-permute-done | bytes 65568 | tf_op jit(solution)/shard_map/ppermute | solution.py:27
  63.1 0.0 collective-permute-done.11
  63.1 0.6 collective-permute-done.12
  63.6 0.7 %fusion.4 = bf16[8,4096]{1,0:T(8,128)(2,1)} fusion(bf16[8,4096]{1,0:T(8,128)(2,1)S(1)} %collective-permute-done.12, bf16[8,4096]{1,0:T(8,128)(2,1)S(1)} %collective-permute-done.11, bf16[8,4096]{1,0:T(8,128)(2,1)S(1)} %collective-permute-done.10, bf16[4,8,4096]{2,1,0:T(8,128)(2,1)S(1)} %fusion.1), kind=kLoop, calls=%fused_computation.9 | loop fusion | flops 262144 | bytes 327680 | tf_op jit(solution)/shard_map/convert_element_type | solution.py:19
  (11 shorter events, 0.2 us)
Async XLA Ops:
  0.9 7.4 %collective-permute-start = (bf16[8,4224]{1,0:T(8,128)(2,1)S(1)}, bf16[8,4224]{1,0:T(8,128)(2,1)S(1)}, u32[]{:S(2)}, u32[]{:S(2)}) collective-permute-start(bf16[8,4224]{1,0:T(8,128)(2,1)S(1)} %message.1), channel_id=1, source_target_pairs={{0,4},{1,5},{2,6},{3,7},{4,0},{5,1},{6,2},{7,3},{8,12},{9,13},{10,... | collective-permute-start | bytes 202760 | tf_op jit(solution)/shard_map/ppermute | solution.py:27
  4.0 7.4 %collective-permute-start.1 = (bf16[8,4224]{1,0:T(8,128)(2,1)S(1)}, bf16[8,4224]{1,0:T(8,128)(2,1)S(1)}, u32[]{:S(2)}, u32[]{:S(2)}) collective-permute-start(bf16[8,4224]{1,0:T(8,128)(2,1)S(1)} %message.1), channel_id=1, source_target_pairs={{0,8},{1,9},{2,10},{3,11},{4,12},{5,13},{6,14},{7,15},{8,0},{9,1},... | collective-permute-start | bytes 202760 | tf_op jit(solution)/shard_map/ppermute | solution.py:27
  6.6 6.3 %collective-permute-start.2 = (bf16[8,4224]{1,0:T(8,128)(2,1)S(1)}, bf16[8,4224]{1,0:T(8,128)(2,1)S(1)}, u32[]{:S(2)}, u32[]{:S(2)}) collective-permute-start(bf16[8,4224]{1,0:T(8,128)(2,1)S(1)} %message.1), channel_id=1, source_target_pairs={{0,12},{1,13},{2,14},{3,15},{4,8},{5,9},{6,10},{7,11},{8,4},{9,5},... | collective-permute-start | bytes 202760 | tf_op jit(solution)/shard_map/ppermute | solution.py:27
  6.6 7.7 %collective-permute-start.3 = (bf16[8,4224]{1,0:T(8,128)(2,1)S(1)}, bf16[8,4224]{1,0:T(8,128)(2,1)S(1)}, u32[]{:S(2)}, u32[]{:S(2)}) collective-permute-start(bf16[8,4224]{1,0:T(8,128)(2,1)S(1)} %message.1), channel_id=1, source_target_pairs={{0,2},{1,3},{2,0},{3,1},{4,6},{5,7},{6,4},{7,5},{8,10},{9,11},{10,... | collective-permute-start | bytes 202760 | tf_op jit(solution)/shard_map/ppermute | solution.py:27
  8.3 6.0 %collective-permute-start.4 = (bf16[8,4224]{1,0:T(8,128)(2,1)S(1)}, bf16[8,4224]{1,0:T(8,128)(2,1)S(1)}, u32[]{:S(2)}, u32[]{:S(2)}) collective-permute-start(bf16[8,4224]{1,0:T(8,128)(2,1)S(1)} %collective-permute-done), channel_id=1, source_target_pairs={{0,2},{1,3},{2,0},{3,1},{4,6},{5,7},{6,4},{7,5},{8,10},{9,11},{10,... | collective-permute-start | bytes 202760 | tf_op jit(solution)/shard_map/ppermute | solution.py:27
  11.4 4.3 %collective-permute-start.5 = (bf16[8,4224]{1,0:T(8,128)(2,1)S(1)}, bf16[8,4224]{1,0:T(8,128)(2,1)S(1)}, u32[]{:S(2)}, u32[]{:S(2)}) collective-permute-start(bf16[8,4224]{1,0:T(8,128)(2,1)S(1)} %collective-permute-done.1), channel_id=1, source_target_pairs={{0,2},{1,3},{2,0},{3,1},{4,6},{5,7},{6,4},{7,5},{8,10},{9,11},{10,... | collective-permute-start | bytes 202760 | tf_op jit(solution)/shard_map/ppermute | solution.py:27
  12.9 4.3 %collective-permute-start.6 = (bf16[8,4224]{1,0:T(8,128)(2,1)S(1)}, bf16[8,4224]{1,0:T(8,128)(2,1)S(1)}, u32[]{:S(2)}, u32[]{:S(2)}) collective-permute-start(bf16[8,4224]{1,0:T(8,128)(2,1)S(1)} %collective-permute-done.2), channel_id=1, source_target_pairs={{0,2},{1,3},{2,0},{3,1},{4,6},{5,7},{6,4},{7,5},{8,10},{9,11},{10,... | collective-permute-start | bytes 202760 | tf_op jit(solution)/shard_map/ppermute | solution.py:27
  17.2 2.0 %collective-permute-start.7 = (bf16[64,4224]{1,0:T(8,128)(2,1)S(1)}, bf16[64,4224]{1,0:T(8,128)(2,1)S(1)}, u32[]{:S(2)}, u32[]{:S(2)}) collective-permute-start(bf16[64,4224]{1,0:T(8,128)(2,1)S(1)} %get-tuple-element.10), channel_id=1, source_target_pairs={{0,1},{1,0},{2,3},{3,2},{4,5},{5,4},{6,7},{7,6},{8,9},{9,8},{10,11... | collective-permute-start | bytes 1622024 | tf_op jit(solution)/shard_map/ppermute | solution.py:27
  44.6 2.0 %collective-permute-start.8 = (bf16[2,4,8,4096]{3,2,1,0:T(8,128)(2,1)S(1)}, bf16[2,4,8,4096]{3,2,1,0:T(8,128)(2,1)S(1)}, u32[]{:S(2)}, u32[]{:S(2)}) collective-permute-start(bf16[2,4,8,4096]{3,2,1,0:T(8,128)(2,1)S(1)} %bitcast.33), channel_id=1, source_target_pairs={{0,1},{1,0},{2,3},{3,2},{4,5},{5,4},{6,7},{7,6},{8,9},{9,8},{10,11... | collective-permute-start | bytes 1572872 | tf_op jit(solution)/shard_map/ppermute | solution.py:27
  46.7 8.4 %collective-permute-start.9 = (bf16[4,8,4096]{2,1,0:T(8,128)(2,1)S(1)}, bf16[4,8,4096]{2,1,0:T(8,128)(2,1)S(1)}, u32[]{:S(2)}, u32[]{:S(2)}) collective-permute-start(bf16[4,8,4096]{2,1,0:T(8,128)(2,1)S(1)} %slice_bitcast_fusion), channel_id=1, source_target_pairs={{0,2},{1,3},{2,0},{3,1},{4,6},{5,7},{6,4},{7,5},{8,10},{9,11},{10,... | collective-permute-start | bytes 786440 | tf_op jit(solution)/shard_map/ppermute | solution.py:27
  55.2 7.8 %collective-permute-start.10 = (bf16[8,4096]{1,0:T(8,128)(2,1)S(1)}, bf16[8,4096]{1,0:T(8,128)(2,1)S(1)}, u32[]{:S(2)}, u32[]{:S(2)}) collective-permute-start(bf16[8,4096]{1,0:T(8,128)(2,1)S(1)} %get-tuple-element.7), channel_id=1, source_target_pairs={{0,8},{1,9},{2,10},{3,11},{4,12},{5,13},{6,14},{7,15},{8,0},{9,1},... | collective-permute-start | bytes 196616 | tf_op jit(solution)/shard_map/ppermute | solution.py:27
  56.8 6.2 %collective-permute-start.11 = (bf16[8,4096]{1,0:T(8,128)(2,1)S(1)}, bf16[8,4096]{1,0:T(8,128)(2,1)S(1)}, u32[]{:S(2)}, u32[]{:S(2)}) collective-permute-start(bf16[8,4096]{1,0:T(8,128)(2,1)S(1)} %get-tuple-element.9), channel_id=1, source_target_pairs={{0,12},{1,13},{2,14},{3,15},{4,8},{5,9},{6,10},{7,11},{8,4},{9,5},... | collective-permute-start | bytes 196616 | tf_op jit(solution)/shard_map/ppermute | solution.py:27
  58.6 5.1 %collective-permute-start.12 = (bf16[8,4096]{1,0:T(8,128)(2,1)S(1)}, bf16[8,4096]{1,0:T(8,128)(2,1)S(1)}, u32[]{:S(2)}, u32[]{:S(2)}) collective-permute-start(bf16[8,4096]{1,0:T(8,128)(2,1)S(1)} %get-tuple-element.8), channel_id=1, source_target_pairs={{0,4},{1,5},{2,6},{3,7},{4,0},{5,1},{6,2},{7,3},{8,12},{9,13},{10,... | collective-permute-start | bytes 196616 | tf_op jit(solution)/shard_map/ppermute | solution.py:27

commit v7 on v6

--- a/solution.py
+++ b/solution.py
@@ -50,8 +50,13 @@
     rows = y.shape[0]
     y = y.reshape(2, dp_count // 2, ep_count, rows // (ep_count * dp_count), y.shape[1])
     y = add_up(y[0], send(y[1], ep_mask=0, dp_mask=1))
-    y = add_up(y[0], *[send(y[d // 2], ep_mask=0, dp_mask=d) for d in range(2, dp_count, 2)])
-    return add_up(y[0], *[send(y[m], ep_mask=m, dp_mask=0) for m in ep_order(ep_count)])
+    order = ep_order(ep_count)
+    far = []
+    for d in range(2, dp_count, 2):
+        block = y[d // 2]
+        block = add_up(block[0], *[send(block[m], ep_mask=m, dp_mask=0) for m in order])
+        far.append(send(block, ep_mask=0, dp_mask=d))
+    return add_up(y[0, 0], *[send(y[0, m], ep_mask=m, dp_mask=0) for m in order], *far)
 
 
 def message_kernel(expert_total, tokens_ref, ids_ref, scores_ref, out_ref, ids_buf, scores_buf, sem):

time: 64.5 us -> 62.5 us (0.969)
  waiting for transfers between devices: 20.7 us -> 16.1 us
  starting transfers between devices: 16.2 us -> 18.9 us
    ppermute x13 -> x16, waiting for transfers between devices: 20.7 us -> 16.1 us  [hop(): return lax.ppermute(x, ('ep', 'dp'), pairs)]
    ppermute x13 -> x16, starting transfers between devices: 16.2 us -> 18.9 us  [hop(): return lax.ppermute(x, ('ep', 'dp'), pairs)]
  transfers between devices with their start and end apart: 13 -> 16, of which waited for: 8 -> 9; matrix products, arithmetic and copies ran while one was open for 0% -> 0% of each run, Pallas kernels for 0% -> 0%
where the time goes in v7:
time: 62.5 us; the launch traced here: 62.4 us
  Pallas kernels  26.2 us (42%)
  starting transfers between devices  18.9 us (30%)
  waiting for transfers between devices  16.1 us (26%)
  other arithmetic  0.84 us (1%)
    pallas_call x1, Pallas kernels, experts(): pl.pallas_call(functools.partial(experts_kernel, width, expert_total, ste...  25.2 us
    ppermute x16, starting transfers between devices, hop(): return lax.ppermute(x, ('ep', 'dp'), pairs)  18.9 us
    ppermute x16, waiting for transfers between devices, hop(): return lax.ppermute(x, ('ep', 'dp'), pairs)  16.1 us
  transfers between devices with their start and end apart: 16, of which 9 were waited for; matrix products, arithmetic and copies ran while one was open for 0% of the time, Pallas kernels for 0%

profile of v7, /device:TPU:0, one launch (start us, length us, event | category | flops | bytes accessed | tf_op | source)
XLA Modules:
  0.0 62.4 jit_solution(9392203384164113173)
XLA Ops:
  0.0 0.9 %message.1 = bf16[8,4224]{1,0:T(8,128)(2,1)S(1)} custom-call(bf16[8,4096]{1,0:T(8,128)(2,1)} %tokens_ref.1, s32[8,8]{1,0:T(8,128)} %ids_ref.1, f32[8,8]{1,0:T(8,128)} %scores_ref.1), custom_call_target="tpu_custom_call" | custom-call | tf_op jit(solution)/shard_map/message/pallas_call | solution.py:88
  0.9 3.1 %collective-permute-start = (bf16[8,4224]{1,0:T(8,128)(2,1)S(1)}, bf16[8,4224]{1,0:T(8,128)(2,1)S(1)}, u32[]{:S(2)}, u32[]{:S(2)}) collective-permute-start(bf16[8,4224]{1,0:T(8,128)(2,1)S(1)} %message.1), channel_id=1, source_target_pairs={{0,4},{1,5},{2,6},{3,7},{4,0},{5,1},{6,2},{7,3},{8,12},{9,13},{10,... | collective-permute-start | bytes 202760 | tf_op jit(solution)/shard_map/ppermute | solution.py:27
  4.0 2.6 %collective-permute-start.1 = (bf16[8,4224]{1,0:T(8,128)(2,1)S(1)}, bf16[8,4224]{1,0:T(8,128)(2,1)S(1)}, u32[]{:S(2)}, u32[]{:S(2)}) collective-permute-start(bf16[8,4224]{1,0:T(8,128)(2,1)S(1)} %message.1), channel_id=1, source_target_pairs={{0,8},{1,9},{2,10},{3,11},{4,12},{5,13},{6,14},{7,15},{8,0},{9,1},... | collective-permute-start | bytes 202760 | tf_op jit(solution)/shard_map/ppermute | solution.py:27
  6.6 0.0 collective-permute-start.2
  6.6 1.7 %collective-permute-start.3 = (bf16[8,4224]{1,0:T(8,128)(2,1)S(1)}, bf16[8,4224]{1,0:T(8,128)(2,1)S(1)}, u32[]{:S(2)}, u32[]{:S(2)}) collective-permute-start(bf16[8,4224]{1,0:T(8,128)(2,1)S(1)} %message.1), channel_id=1, source_target_pairs={{0,2},{1,3},{2,0},{3,1},{4,6},{5,7},{6,4},{7,5},{8,10},{9,11},{10,... | collective-permute-start | bytes 202760 | tf_op jit(solution)/shard_map/ppermute | solution.py:27
  8.3 0.0 collective-permute-done
  8.3 0.4 collective-permute-start.4
  8.7 2.7 %collective-permute-done.1 = bf16[8,4224]{1,0:T(8,128)(2,1)S(1)} collective-permute-done((bf16[8,4224]{1,0:T(8,128)(2,1)S(1)}, bf16[8,4224]{1,0:T(8,128)(2,1)S(1)}, u32[]{:S(2)}, u32[]{:S(2)}) %collective-permute-start.1) | collective-permute-done | bytes 67616 | tf_op jit(solution)/shard_map/ppermute | solution.py:27
  11.4 1.5 %collective-permute-start.5 = (bf16[8,4224]{1,0:T(8,128)(2,1)S(1)}, bf16[8,4224]{1,0:T(8,128)(2,1)S(1)}, u32[]{:S(2)}, u32[]{:S(2)}) collective-permute-start(bf16[8,4224]{1,0:T(8,128)(2,1)S(1)} %collective-permute-done.1), channel_id=1, source_target_pairs={{0,2},{1,3},{2,0},{3,1},{4,6},{5,7},{6,4},{7,5},{8,10},{9,11},{10,... | collective-permute-start | bytes 202760 | tf_op jit(solution)/shard_map/ppermute | solution.py:27
  12.9 0.0 collective-permute-done.2
  12.9 1.4 %collective-permute-start.6 = (bf16[8,4224]{1,0:T(8,128)(2,1)S(1)}, bf16[8,4224]{1,0:T(8,128)(2,1)S(1)}, u32[]{:S(2)}, u32[]{:S(2)}) collective-permute-start(bf16[8,4224]{1,0:T(8,128)(2,1)S(1)} %collective-permute-done.2), channel_id=1, source_target_pairs={{0,2},{1,3},{2,0},{3,1},{4,6},{5,7},{6,4},{7,5},{8,10},{9,11},{10,... | collective-permute-start | bytes 202760 | tf_op jit(solution)/shard_map/ppermute | solution.py:27
  14.3 0.0 collective-permute-done.3
  14.4 0.0 collective-permute-done.4
  14.4 1.3 %collective-permute-done.5 = bf16[8,4224]{1,0:T(8,128)(2,1)S(1)} collective-permute-done((bf16[8,4224]{1,0:T(8,128)(2,1)S(1)}, bf16[8,4224]{1,0:T(8,128)(2,1)S(1)}, u32[]{:S(2)}, u32[]{:S(2)}) %collective-permute-start.5) | collective-permute-done | bytes 67616 | tf_op jit(solution)/shard_map/ppermute | solution.py:27
  15.7 1.5 %collective-permute-done.6 = bf16[8,4224]{1,0:T(8,128)(2,1)S(1)} collective-permute-done((bf16[8,4224]{1,0:T(8,128)(2,1)S(1)}, bf16[8,4224]{1,0:T(8,128)(2,1)S(1)}, u32[]{:S(2)}, u32[]{:S(2)}) %collective-permute-start.6) | collective-permute-done | bytes 67616 | tf_op jit(solution)/shard_map/ppermute | solution.py:27
  17.2 0.1 collective-permute-start.7
  17.3 1.9 %collective-permute-done.7 = bf16[64,4224]{1,0:T(8,128)(2,1)S(1)} collective-permute-done((bf16[64,4224]{1,0:T(8,128)(2,1)S(1)}, bf16[64,4224]{1,0:T(8,128)(2,1)S(1)}, u32[]{:S(2)}, u32[]{:S(2)}) %collective-permute-start.7) | collective-permute-done | bytes 540704 | tf_op jit(solution)/shard_map/ppermute | solution.py:27
  19.3 25.2 %experts.1 = bf16[128,4096]{1,0:T(8,128)(2,1)S(1)} custom-call(s32[1]{0:T(128)} %bitcast.first_ref, bf16[128,4224]{1,0:T(8,128)(2,1)S(1)} %constant_dynamic-update-slice_fusion.8.x_ref, bf16[3072,4096]{1,0:T(8,128)(2,1)} %bitcast.33, bf16[3072,4096]{1,0:T(8,128)(2,1)} %bitcast.34, bf16[3072,4096]{1,0:T(8,128)(2,1)} %bitcast.35), custom_call_target="tpu_custom_call" | custom-call | tf_op jit(solution)/shard_map/experts/pallas_call | solution.py:184
  44.5 0.1 fusion.8
  44.6 0.2 collective-permute-start.8
  44.8 1.8 %collective-permute-done.8 = bf16[2,4,8,4096]{3,2,1,0:T(8,128)(2,1)S(1)} collective-permute-done((bf16[2,4,8,4096]{3,2,1,0:T(8,128)(2,1)S(1)}, bf16[2,4,8,4096]{3,2,1,0:T(8,128)(2,1)S(1)}, u32[]{:S(2)}, u32[]{:S(2)}) %collective-permute-start.8) | collective-permute-done | bytes 524320 | tf_op jit(solution)/shard_map/ppermute | solution.py:27
  46.6 0.1 fusion
  46.7 1.6 %collective-permute-start.12 = (bf16[8,4096]{1,0:T(8,128)(2,1)S(1)}, bf16[8,4096]{1,0:T(8,128)(2,1)S(1)}, u32[]{:S(2)}, u32[]{:S(2)}) collective-permute-start(bf16[8,4096]{1,0:T(8,128)(2,1)S(1)} %get-tuple-element.10), channel_id=1, source_target_pairs={{0,8},{1,9},{2,10},{3,11},{4,12},{5,13},{6,14},{7,15},{8,0},{9,1},... | collective-permute-start | bytes 196616 | tf_op jit(solution)/shard_map/ppermute | solution.py:27
  48.3 1.7 %collective-permute-start.13 = (bf16[8,4096]{1,0:T(8,128)(2,1)S(1)}, bf16[8,4096]{1,0:T(8,128)(2,1)S(1)}, u32[]{:S(2)}, u32[]{:S(2)}) collective-permute-start(bf16[8,4096]{1,0:T(8,128)(2,1)S(1)} %get-tuple-element.9), channel_id=1, source_target_pairs={{0,12},{1,13},{2,14},{3,15},{4,8},{5,9},{6,10},{7,11},{8,4},{9,5},... | collective-permute-start | bytes 196616 | tf_op jit(solution)/shard_map/ppermute | solution.py:27
  50.1 0.5 collective-permute-start.14
  50.6 2.9 %collective-permute-start.10 = (bf16[8,4096]{1,0:T(8,128)(2,1)S(1)}, bf16[8,4096]{1,0:T(8,128)(2,1)S(1)}, u32[]{:S(2)}, u32[]{:S(2)}) collective-permute-start(bf16[8,4096]{1,0:T(8,128)(2,1)S(1)} %get-tuple-element.12), channel_id=1, source_target_pairs={{0,12},{1,13},{2,14},{3,15},{4,8},{5,9},{6,10},{7,11},{8,4},{9,5},... | collective-permute-start | bytes 196616 | tf_op jit(solution)/shard_map/ppermute | solution.py:27
  53.5 0.0 collective-permute-start.11
  53.5 2.1 %collective-permute-done.12 = bf16[8,4096]{1,0:T(8,128)(2,1)S(1)} collective-permute-done((bf16[8,4096]{1,0:T(8,128)(2,1)S(1)}, bf16[8,4096]{1,0:T(8,128)(2,1)S(1)}, u32[]{:S(2)}, u32[]{:S(2)}) %collective-permute-start.12) | collective-permute-done | bytes 65568 | tf_op jit(solution)/shard_map/ppermute | solution.py:27
  55.5 0.0 collective-permute-start.9
  55.5 0.0 collective-permute-done.13
  55.6 1.8 %collective-permute-done.14 = bf16[8,4096]{1,0:T(8,128)(2,1)S(1)} collective-permute-done((bf16[8,4096]{1,0:T(8,128)(2,1)S(1)}, bf16[8,4096]{1,0:T(8,128)(2,1)S(1)}, u32[]{:S(2)}, u32[]{:S(2)}) %collective-permute-start.14) | collective-permute-done | bytes 65568 | tf_op jit(solution)/shard_map/ppermute | solution.py:27
  57.4 1.2 %collective-permute-start.15 = (bf16[8,4096]{1,0:T(8,128)(2,1)S(1)}, bf16[8,4096]{1,0:T(8,128)(2,1)S(1)}, u32[]{:S(2)}, u32[]{:S(2)}) collective-permute-start(bf16[8,4096]{1,0:T(8,128)(2,1)S(1)} %fusion.3), channel_id=1, source_target_pairs={{0,2},{1,3},{2,0},{3,1},{4,6},{5,7},{6,4},{7,5},{8,10},{9,11},{10,... | collective-permute-start | bytes 196616 | tf_op jit(solution)/shard_map/ppermute | solution.py:27
  58.6 0.0 collective-permute-done.10
  58.6 0.5 collective-permute-done.11
  59.0 2.6 %collective-permute-done.9 = bf16[8,4096]{1,0:T(8,128)(2,1)S(1)} collective-permute-done((bf16[8,4096]{1,0:T(8,128)(2,1)S(1)}, bf16[8,4096]{1,0:T(8,128)(2,1)S(1)}, u32[]{:S(2)}, u32[]{:S(2)}) %collective-permute-start.9) | collective-permute-done | bytes 65568 | tf_op jit(solution)/shard_map/ppermute | solution.py:27
  61.7 0.0 collective-permute-done.15
  61.7 0.7 %fusion.7 = bf16[8,4096]{1,0:T(8,128)(2,1)} fusion(bf16[8,4096]{1,0:T(8,128)(2,1)S(1)} %collective-permute-done.15, bf16[8,4096]{1,0:T(8,128)(2,1)S(1)} %collective-permute-done.11, bf16[8,4096]{1,0:T(8,128)(2,1)S(1)} %collective-permute-done.10, bf16[8,4096]{1,0:T(8,128)(2,1)S(1)} %collective-permute-done.9, bf16[2,4,8,4096]{3,2,1,0:T(8,128)(2,1)S(1)} %fusion), kind=kLoop, calls=%fused_computation.10 | loop fusion | flops 327680 | bytes 393216 | tf_op jit(solution)/shard_map/convert_element_type | solution.py:19
  (11 shorter events, 0.2 us)
Async XLA Ops:
  0.9 7.4 %collective-permute-start = (bf16[8,4224]{1,0:T(8,128)(2,1)S(1)}, bf16[8,4224]{1,0:T(8,128)(2,1)S(1)}, u32[]{:S(2)}, u32[]{:S(2)}) collective-permute-start(bf16[8,4224]{1,0:T(8,128)(2,1)S(1)} %message.1), channel_id=1, source_target_pairs={{0,4},{1,5},{2,6},{3,7},{4,0},{5,1},{6,2},{7,3},{8,12},{9,13},{10,... | collective-permute-start | bytes 202760 | tf_op jit(solution)/shard_map/ppermute | solution.py:27
  4.0 7.4 %collective-permute-start.1 = (bf16[8,4224]{1,0:T(8,128)(2,1)S(1)}, bf16[8,4224]{1,0:T(8,128)(2,1)S(1)}, u32[]{:S(2)}, u32[]{:S(2)}) collective-permute-start(bf16[8,4224]{1,0:T(8,128)(2,1)S(1)} %message.1), channel_id=1, source_target_pairs={{0,8},{1,9},{2,10},{3,11},{4,12},{5,13},{6,14},{7,15},{8,0},{9,1},... | collective-permute-start | bytes 202760 | tf_op jit(solution)/shard_map/ppermute | solution.py:27
  6.6 6.3 %collective-permute-start.2 = (bf16[8,4224]{1,0:T(8,128)(2,1)S(1)}, bf16[8,4224]{1,0:T(8,128)(2,1)S(1)}, u32[]{:S(2)}, u32[]{:S(2)}) collective-permute-start(bf16[8,4224]{1,0:T(8,128)(2,1)S(1)} %message.1), channel_id=1, source_target_pairs={{0,12},{1,13},{2,14},{3,15},{4,8},{5,9},{6,10},{7,11},{8,4},{9,5},... | collective-permute-start | bytes 202760 | tf_op jit(solution)/shard_map/ppermute | solution.py:27
  6.6 7.7 %collective-permute-start.3 = (bf16[8,4224]{1,0:T(8,128)(2,1)S(1)}, bf16[8,4224]{1,0:T(8,128)(2,1)S(1)}, u32[]{:S(2)}, u32[]{:S(2)}) collective-permute-start(bf16[8,4224]{1,0:T(8,128)(2,1)S(1)} %message.1), channel_id=1, source_target_pairs={{0,2},{1,3},{2,0},{3,1},{4,6},{5,7},{6,4},{7,5},{8,10},{9,11},{10,... | collective-permute-start | bytes 202760 | tf_op jit(solution)/shard_map/ppermute | solution.py:27
  8.3 6.0 %collective-permute-start.4 = (bf16[8,4224]{1,0:T(8,128)(2,1)S(1)}, bf16[8,4224]{1,0:T(8,128)(2,1)S(1)}, u32[]{:S(2)}, u32[]{:S(2)}) collective-permute-start(bf16[8,4224]{1,0:T(8,128)(2,1)S(1)} %collective-permute-done), channel_id=1, source_target_pairs={{0,2},{1,3},{2,0},{3,1},{4,6},{5,7},{6,4},{7,5},{8,10},{9,11},{10,... | collective-permute-start | bytes 202760 | tf_op jit(solution)/shard_map/ppermute | solution.py:27
  11.4 4.3 %collective-permute-start.5 = (bf16[8,4224]{1,0:T(8,128)(2,1)S(1)}, bf16[8,4224]{1,0:T(8,128)(2,1)S(1)}, u32[]{:S(2)}, u32[]{:S(2)}) collective-permute-start(bf16[8,4224]{1,0:T(8,128)(2,1)S(1)} %collective-permute-done.1), channel_id=1, source_target_pairs={{0,2},{1,3},{2,0},{3,1},{4,6},{5,7},{6,4},{7,5},{8,10},{9,11},{10,... | collective-permute-start | bytes 202760 | tf_op jit(solution)/shard_map/ppermute | solution.py:27
  12.9 4.3 %collective-permute-start.6 = (bf16[8,4224]{1,0:T(8,128)(2,1)S(1)}, bf16[8,4224]{1,0:T(8,128)(2,1)S(1)}, u32[]{:S(2)}, u32[]{:S(2)}) collective-permute-start(bf16[8,4224]{1,0:T(8,128)(2,1)S(1)} %collective-permute-done.2), channel_id=1, source_target_pairs={{0,2},{1,3},{2,0},{3,1},{4,6},{5,7},{6,4},{7,5},{8,10},{9,11},{10,... | collective-permute-start | bytes 202760 | tf_op jit(solution)/shard_map/ppermute | solution.py:27
  17.2 2.0 %collective-permute-start.7 = (bf16[64,4224]{1,0:T(8,128)(2,1)S(1)}, bf16[64,4224]{1,0:T(8,128)(2,1)S(1)}, u32[]{:S(2)}, u32[]{:S(2)}) collective-permute-start(bf16[64,4224]{1,0:T(8,128)(2,1)S(1)} %get-tuple-element.13), channel_id=1, source_target_pairs={{0,1},{1,0},{2,3},{3,2},{4,5},{5,4},{6,7},{7,6},{8,9},{9,8},{10,11... | collective-permute-start | bytes 1622024 | tf_op jit(solution)/shard_map/ppermute | solution.py:27
  44.6 2.0 %collective-permute-start.8 = (bf16[2,4,8,4096]{3,2,1,0:T(8,128)(2,1)S(1)}, bf16[2,4,8,4096]{3,2,1,0:T(8,128)(2,1)S(1)}, u32[]{:S(2)}, u32[]{:S(2)}) collective-permute-start(bf16[2,4,8,4096]{3,2,1,0:T(8,128)(2,1)S(1)} %bitcast.37), channel_id=1, source_target_pairs={{0,1},{1,0},{2,3},{3,2},{4,5},{5,4},{6,7},{7,6},{8,9},{9,8},{10,11... | collective-permute-start | bytes 1572872 | tf_op jit(solution)/shard_map/ppermute | solution.py:27
  46.7 8.8 %collective-permute-start.12 = (bf16[8,4096]{1,0:T(8,128)(2,1)S(1)}, bf16[8,4096]{1,0:T(8,128)(2,1)S(1)}, u32[]{:S(2)}, u32[]{:S(2)}) collective-permute-start(bf16[8,4096]{1,0:T(8,128)(2,1)S(1)} %get-tuple-element.10), channel_id=1, source_target_pairs={{0,8},{1,9},{2,10},{3,11},{4,12},{5,13},{6,14},{7,15},{8,0},{9,1},... | collective-permute-start | bytes 196616 | tf_op jit(solution)/shard_map/ppermute | solution.py:27
  48.3 7.2 %collective-permute-start.13 = (bf16[8,4096]{1,0:T(8,128)(2,1)S(1)}, bf16[8,4096]{1,0:T(8,128)(2,1)S(1)}, u32[]{:S(2)}, u32[]{:S(2)}) collective-permute-start(bf16[8,4096]{1,0:T(8,128)(2,1)S(1)} %get-tuple-element.9), channel_id=1, source_target_pairs={{0,12},{1,13},{2,14},{3,15},{4,8},{5,9},{6,10},{7,11},{8,4},{9,5},... | collective-permute-start | bytes 196616 | tf_op jit(solution)/shard_map/ppermute | solution.py:27
  50.1 7.2 %collective-permute-start.14 = (bf16[8,4096]{1,0:T(8,128)(2,1)S(1)}, bf16[8,4096]{1,0:T(8,128)(2,1)S(1)}, u32[]{:S(2)}, u32[]{:S(2)}) collective-permute-start(bf16[8,4096]{1,0:T(8,128)(2,1)S(1)} %get-tuple-element.8), channel_id=1, source_target_pairs={{0,4},{1,5},{2,6},{3,7},{4,0},{5,1},{6,2},{7,3},{8,12},{9,13},{10,... | collective-permute-start | bytes 196616 | tf_op jit(solution)/shard_map/ppermute | solution.py:27
  50.6 8.0 %collective-permute-start.10 = (bf16[8,4096]{1,0:T(8,128)(2,1)S(1)}, bf16[8,4096]{1,0:T(8,128)(2,1)S(1)}, u32[]{:S(2)}, u32[]{:S(2)}) collective-permute-start(bf16[8,4096]{1,0:T(8,128)(2,1)S(1)} %get-tuple-element.12), channel_id=1, source_target_pairs={{0,12},{1,13},{2,14},{3,15},{4,8},{5,9},{6,10},{7,11},{8,4},{9,5},... | collective-permute-start | bytes 196616 | tf_op jit(solution)/shard_map/ppermute | solution.py:27
  53.5 5.5 %collective-permute-start.11 = (bf16[8,4096]{1,0:T(8,128)(2,1)S(1)}, bf16[8,4096]{1,0:T(8,128)(2,1)S(1)}, u32[]{:S(2)}, u32[]{:S(2)}) collective-permute-start(bf16[8,4096]{1,0:T(8,128)(2,1)S(1)} %get-tuple-element.11), channel_id=1, source_target_pairs={{0,4},{1,5},{2,6},{3,7},{4,0},{5,1},{6,2},{7,3},{8,12},{9,13},{10,... | collective-permute-start | bytes 196616 | tf_op jit(solution)/shard_map/ppermute | solution.py:27
  55.5 6.1 %collective-permute-start.9 = (bf16[8,4096]{1,0:T(8,128)(2,1)S(1)}, bf16[8,4096]{1,0:T(8,128)(2,1)S(1)}, u32[]{:S(2)}, u32[]{:S(2)}) collective-permute-start(bf16[8,4096]{1,0:T(8,128)(2,1)S(1)} %get-tuple-element.7), channel_id=1, source_target_pairs={{0,8},{1,9},{2,10},{3,11},{4,12},{5,13},{6,14},{7,15},{8,0},{9,1},... | collective-permute-start | bytes 196616 | tf_op jit(solution)/shard_map/ppermute | solution.py:27
  57.4 4.3 %collective-permute-start.15 = (bf16[8,4096]{1,0:T(8,128)(2,1)S(1)}, bf16[8,4096]{1,0:T(8,128)(2,1)S(1)}, u32[]{:S(2)}, u32[]{:S(2)}) collective-permute-start(bf16[8,4096]{1,0:T(8,128)(2,1)S(1)} %fusion.3), channel_id=1, source_target_pairs={{0,2},{1,3},{2,0},{3,1},{4,6},{5,7},{6,4},{7,5},{8,10},{9,11},{10,... | collective-permute-start | bytes 196616 | tf_op jit(solution)/shard_map/ppermute | solution.py:27

commit v8 on v7

--- a/solution.py
+++ b/solution.py
@@ -50,7 +50,7 @@
     rows = y.shape[0]
     y = y.reshape(2, dp_count // 2, ep_count, rows // (ep_count * dp_count), y.shape[1])
     y = add_up(y[0], send(y[1], ep_mask=0, dp_mask=1))
-    order = ep_order(ep_count)
+    order = list(range(ep_count - 1, 0, -1))
     far = []
     for d in range(2, dp_count, 2):
         block = y[d // 2]

time: 62.5 us -> 62 us (level)
  waiting for transfers between devices: 16.1 us -> 12.4 us
  starting transfers between devices: 18.9 us -> 22 us
    ppermute x16, waiting for transfers between devices: 16.1 us -> 12.4 us  [hop(): return lax.ppermute(x, ('ep', 'dp'), pairs)]
    ppermute x16, starting transfers between devices: 18.9 us -> 22 us  [hop(): return lax.ppermute(x, ('ep', 'dp'), pairs)]
  transfers between devices with their start and end apart: 16 -> 16, of which waited for: 9 -> 7; matrix products, arithmetic and copies ran while one was open for 0% -> 0% of each run, Pallas kernels for 0% -> 0%
where the time goes in v8:
time: 62 us; the launch traced here: 61.8 us
  Pallas kernels  26.2 us (42%)
  starting transfers between devices  22 us (35%)
  waiting for transfers between devices  12.4 us (20%)
  other arithmetic  0.84 us (1%)
    pallas_call x1, Pallas kernels, experts(): pl.pallas_call(functools.partial(experts_kernel, width, expert_total, ste...  25.2 us
    ppermute x16, starting transfers between devices, hop(): return lax.ppermute(x, ('ep', 'dp'), pairs)  22 us
    ppermute x16, waiting for transfers between devices, hop(): return lax.ppermute(x, ('ep', 'dp'), pairs)  12.4 us
  transfers between devices with their start and end apart: 16, of which 7 were waited for; matrix products, arithmetic and copies ran while one was open for 0% of the time, Pallas kernels for 0%

profile of v8, /device:TPU:0, one launch (start us, length us, event | category | flops | bytes accessed | tf_op | source)
XLA Modules:
  0.0 61.8 jit_solution(9173416390715387993)
XLA Ops:
  0.0 0.9 %message.1 = bf16[8,4224]{1,0:T(8,128)(2,1)S(1)} custom-call(bf16[8,4096]{1,0:T(8,128)(2,1)} %tokens_ref.1, s32[8,8]{1,0:T(8,128)} %ids_ref.1, f32[8,8]{1,0:T(8,128)} %scores_ref.1), custom_call_target="tpu_custom_call" | custom-call | tf_op jit(solution)/shard_map/message/pallas_call | solution.py:88
  0.9 3.1 %collective-permute-start = (bf16[8,4224]{1,0:T(8,128)(2,1)S(1)}, bf16[8,4224]{1,0:T(8,128)(2,1)S(1)}, u32[]{:S(2)}, u32[]{:S(2)}) collective-permute-start(bf16[8,4224]{1,0:T(8,128)(2,1)S(1)} %message.1), channel_id=1, source_target_pairs={{0,4},{1,5},{2,6},{3,7},{4,0},{5,1},{6,2},{7,3},{8,12},{9,13},{10,... | collective-permute-start | bytes 202760 | tf_op jit(solution)/shard_map/ppermute | solution.py:27
  4.0 2.6 %collective-permute-start.1 = (bf16[8,4224]{1,0:T(8,128)(2,1)S(1)}, bf16[8,4224]{1,0:T(8,128)(2,1)S(1)}, u32[]{:S(2)}, u32[]{:S(2)}) collective-permute-start(bf16[8,4224]{1,0:T(8,128)(2,1)S(1)} %message.1), channel_id=1, source_target_pairs={{0,8},{1,9},{2,10},{3,11},{4,12},{5,13},{6,14},{7,15},{8,0},{9,1},... | collective-permute-start | bytes 202760 | tf_op jit(solution)/shard_map/ppermute | solution.py:27
  6.6 0.0 collective-permute-start.2
  6.6 1.7 %collective-permute-start.3 = (bf16[8,4224]{1,0:T(8,128)(2,1)S(1)}, bf16[8,4224]{1,0:T(8,128)(2,1)S(1)}, u32[]{:S(2)}, u32[]{:S(2)}) collective-permute-start(bf16[8,4224]{1,0:T(8,128)(2,1)S(1)} %message.1), channel_id=1, source_target_pairs={{0,2},{1,3},{2,0},{3,1},{4,6},{5,7},{6,4},{7,5},{8,10},{9,11},{10,... | collective-permute-start | bytes 202760 | tf_op jit(solution)/shard_map/ppermute | solution.py:27
  8.3 0.0 collective-permute-done
  8.3 0.4 collective-permute-start.4
  8.7 2.7 %collective-permute-done.1 = bf16[8,4224]{1,0:T(8,128)(2,1)S(1)} collective-permute-done((bf16[8,4224]{1,0:T(8,128)(2,1)S(1)}, bf16[8,4224]{1,0:T(8,128)(2,1)S(1)}, u32[]{:S(2)}, u32[]{:S(2)}) %collective-permute-start.1) | collective-permute-done | bytes 67616 | tf_op jit(solution)/shard_map/ppermute | solution.py:27
  11.4 1.5 %collective-permute-start.5 = (bf16[8,4224]{1,0:T(8,128)(2,1)S(1)}, bf16[8,4224]{1,0:T(8,128)(2,1)S(1)}, u32[]{:S(2)}, u32[]{:S(2)}) collective-permute-start(bf16[8,4224]{1,0:T(8,128)(2,1)S(1)} %collective-permute-done.1), channel_id=1, source_target_pairs={{0,2},{1,3},{2,0},{3,1},{4,6},{5,7},{6,4},{7,5},{8,10},{9,11},{10,... | collective-permute-start | bytes 202760 | tf_op jit(solution)/shard_map/ppermute | solution.py:27
  12.9 0.0 collective-permute-done.2
  12.9 1.4 %collective-permute-start.6 = (bf16[8,4224]{1,0:T(8,128)(2,1)S(1)}, bf16[8,4224]{1,0:T(8,128)(2,1)S(1)}, u32[]{:S(2)}, u32[]{:S(2)}) collective-permute-start(bf16[8,4224]{1,0:T(8,128)(2,1)S(1)} %collective-permute-done.2), channel_id=1, source_target_pairs={{0,2},{1,3},{2,0},{3,1},{4,6},{5,7},{6,4},{7,5},{8,10},{9,11},{10,... | collective-permute-start | bytes 202760 | tf_op jit(solution)/shard_map/ppermute | solution.py:27
  14.3 0.0 collective-permute-done.3
  14.4 0.0 collective-permute-done.4
  14.4 1.3 %collective-permute-done.5 = bf16[8,4224]{1,0:T(8,128)(2,1)S(1)} collective-permute-done((bf16[8,4224]{1,0:T(8,128)(2,1)S(1)}, bf16[8,4224]{1,0:T(8,128)(2,1)S(1)}, u32[]{:S(2)}, u32[]{:S(2)}) %collective-permute-start.5) | collective-permute-done | bytes 67616 | tf_op jit(solution)/shard_map/ppermute | solution.py:27
  15.7 1.5 %collective-permute-done.6 = bf16[8,4224]{1,0:T(8,128)(2,1)S(1)} collective-permute-done((bf16[8,4224]{1,0:T(8,128)(2,1)S(1)}, bf16[8,4224]{1,0:T(8,128)(2,1)S(1)}, u32[]{:S(2)}, u32[]{:S(2)}) %collective-permute-start.6) | collective-permute-done | bytes 67616 | tf_op jit(solution)/shard_map/ppermute | solution.py:27
  17.2 0.1 collective-permute-start.7
  17.3 1.9 %collective-permute-done.7 = bf16[64,4224]{1,0:T(8,128)(2,1)S(1)} collective-permute-done((bf16[64,4224]{1,0:T(8,128)(2,1)S(1)}, bf16[64,4224]{1,0:T(8,128)(2,1)S(1)}, u32[]{:S(2)}, u32[]{:S(2)}) %collective-permute-start.7) | collective-permute-done | bytes 540704 | tf_op jit(solution)/shard_map/ppermute | solution.py:27
  19.3 25.2 %experts.1 = bf16[128,4096]{1,0:T(8,128)(2,1)S(1)} custom-call(s32[1]{0:T(128)} %bitcast.first_ref, bf16[128,4224]{1,0:T(8,128)(2,1)S(1)} %constant_dynamic-update-slice_fusion.8.x_ref, bf16[3072,4096]{1,0:T(8,128)(2,1)} %bitcast.33, bf16[3072,4096]{1,0:T(8,128)(2,1)} %bitcast.34, bf16[3072,4096]{1,0:T(8,128)(2,1)} %bitcast.35), custom_call_target="tpu_custom_call" | custom-call | tf_op jit(solution)/shard_map/experts/pallas_call | solution.py:184
  44.5 0.1 fusion.8
  44.6 0.2 collective-permute-start.8
  44.8 1.8 %collective-permute-done.8 = bf16[2,4,8,4096]{3,2,1,0:T(8,128)(2,1)S(1)} collective-permute-done((bf16[2,4,8,4096]{3,2,1,0:T(8,128)(2,1)S(1)}, bf16[2,4,8,4096]{3,2,1,0:T(8,128)(2,1)S(1)}, u32[]{:S(2)}, u32[]{:S(2)}) %collective-permute-start.8) | collective-permute-done | bytes 524320 | tf_op jit(solution)/shard_map/ppermute | solution.py:27
  46.6 0.1 fusion
  46.7 3.3 %collective-permute-start.12 = (bf16[8,4096]{1,0:T(8,128)(2,1)S(1)}, bf16[8,4096]{1,0:T(8,128)(2,1)S(1)}, u32[]{:S(2)}, u32[]{:S(2)}) collective-permute-start(bf16[8,4096]{1,0:T(8,128)(2,1)S(1)} %get-tuple-element.10), channel_id=1, source_target_pairs={{0,12},{1,13},{2,14},{3,15},{4,8},{5,9},{6,10},{7,11},{8,4},{9,5},... | collective-permute-start | bytes 196616 | tf_op jit(solution)/shard_map/ppermute | solution.py:27
  50.0 0.0 collective-permute-start.13
  50.0 1.2 %collective-permute-start.14 = (bf16[8,4096]{1,0:T(8,128)(2,1)S(1)}, bf16[8,4096]{1,0:T(8,128)(2,1)S(1)}, u32[]{:S(2)}, u32[]{:S(2)}) collective-permute-start(bf16[8,4096]{1,0:T(8,128)(2,1)S(1)} %get-tuple-element.8), channel_id=1, source_target_pairs={{0,4},{1,5},{2,6},{3,7},{4,0},{5,1},{6,2},{7,3},{8,12},{9,13},{10,... | collective-permute-start | bytes 196616 | tf_op jit(solution)/shard_map/ppermute | solution.py:27
  51.2 1.7 %collective-permute-start.10 = (bf16[8,4096]{1,0:T(8,128)(2,1)S(1)}, bf16[8,4096]{1,0:T(8,128)(2,1)S(1)}, u32[]{:S(2)}, u32[]{:S(2)}) collective-permute-start(bf16[8,4096]{1,0:T(8,128)(2,1)S(1)} %get-tuple-element.12), channel_id=1, source_target_pairs={{0,8},{1,9},{2,10},{3,11},{4,12},{5,13},{6,14},{7,15},{8,0},{9,1},... | collective-permute-start | bytes 196616 | tf_op jit(solution)/shard_map/ppermute | solution.py:27
  52.9 2.0 %collective-permute-start.11 = (bf16[8,4096]{1,0:T(8,128)(2,1)S(1)}, bf16[8,4096]{1,0:T(8,128)(2,1)S(1)}, u32[]{:S(2)}, u32[]{:S(2)}) collective-permute-start(bf16[8,4096]{1,0:T(8,128)(2,1)S(1)} %get-tuple-element.11), channel_id=1, source_target_pairs={{0,4},{1,5},{2,6},{3,7},{4,0},{5,1},{6,2},{7,3},{8,12},{9,13},{10,... | collective-permute-start | bytes 196616 | tf_op jit(solution)/shard_map/ppermute | solution.py:27
  54.9 0.0 collective-permute-done.12
  54.9 1.8 %collective-permute-start.9 = (bf16[8,4096]{1,0:T(8,128)(2,1)S(1)}, bf16[8,4096]{1,0:T(8,128)(2,1)S(1)}, u32[]{:S(2)}, u32[]{:S(2)}) collective-permute-start(bf16[8,4096]{1,0:T(8,128)(2,1)S(1)} %get-tuple-element.7), channel_id=1, source_target_pairs={{0,12},{1,13},{2,14},{3,15},{4,8},{5,9},{6,10},{7,11},{8,4},{9,5},... | collective-permute-start | bytes 196616 | tf_op jit(solution)/shard_map/ppermute | solution.py:27
  56.8 0.0 collective-permute-done.13
  56.8 0.0 collective-permute-done.14
  56.8 1.0 %collective-permute-start.15 = (bf16[8,4096]{1,0:T(8,128)(2,1)S(1)}, bf16[8,4096]{1,0:T(8,128)(2,1)S(1)}, u32[]{:S(2)}, u32[]{:S(2)}) collective-permute-start(bf16[8,4096]{1,0:T(8,128)(2,1)S(1)} %fusion.3), channel_id=1, source_target_pairs={{0,2},{1,3},{2,0},{3,1},{4,6},{5,7},{6,4},{7,5},{8,10},{9,11},{10,... | collective-permute-start | bytes 196616 | tf_op jit(solution)/shard_map/ppermute | solution.py:27
  57.9 1.4 %collective-permute-done.10 = bf16[8,4096]{1,0:T(8,128)(2,1)S(1)} collective-permute-done((bf16[8,4096]{1,0:T(8,128)(2,1)S(1)}, bf16[8,4096]{1,0:T(8,128)(2,1)S(1)}, u32[]{:S(2)}, u32[]{:S(2)}) %collective-permute-start.10) | collective-permute-done | bytes 65568 | tf_op jit(solution)/shard_map/ppermute | solution.py:27
  59.3 0.0 collective-permute-done.11
  59.3 1.9 %collective-permute-done.9 = bf16[8,4096]{1,0:T(8,128)(2,1)S(1)} collective-permute-done((bf16[8,4096]{1,0:T(8,128)(2,1)S(1)}, bf16[8,4096]{1,0:T(8,128)(2,1)S(1)}, u32[]{:S(2)}, u32[]{:S(2)}) %collective-permute-start.9) | collective-permute-done | bytes 65568 | tf_op jit(solution)/shard_map/ppermute | solution.py:27
  61.1 0.0 collective-permute-done.15
  61.2 0.7 %fusion.7 = bf16[8,4096]{1,0:T(8,128)(2,1)} fusion(bf16[8,4096]{1,0:T(8,128)(2,1)S(1)} %collective-permute-done.15, bf16[8,4096]{1,0:T(8,128)(2,1)S(1)} %collective-permute-done.11, bf16[8,4096]{1,0:T(8,128)(2,1)S(1)} %collective-permute-done.10, bf16[8,4096]{1,0:T(8,128)(2,1)S(1)} %collective-permute-done.9, bf16[2,4,8,4096]{3,2,1,0:T(8,128)(2,1)S(1)} %fusion), kind=kLoop, calls=%fused_computation.10 | loop fusion | flops 327680 | bytes 393216 | tf_op jit(solution)/shard_map/convert_element_type | solution.py:19
  (11 shorter events, 0.2 us)
Async XLA Ops:
  0.9 7.4 %collective-permute-start = (bf16[8,4224]{1,0:T(8,128)(2,1)S(1)}, bf16[8,4224]{1,0:T(8,128)(2,1)S(1)}, u32[]{:S(2)}, u32[]{:S(2)}) collective-permute-start(bf16[8,4224]{1,0:T(8,128)(2,1)S(1)} %message.1), channel_id=1, source_target_pairs={{0,4},{1,5},{2,6},{3,7},{4,0},{5,1},{6,2},{7,3},{8,12},{9,13},{10,... | collective-permute-start | bytes 202760 | tf_op jit(solution)/shard_map/ppermute | solution.py:27
  4.0 7.4 %collective-permute-start.1 = (bf16[8,4224]{1,0:T(8,128)(2,1)S(1)}, bf16[8,4224]{1,0:T(8,128)(2,1)S(1)}, u32[]{:S(2)}, u32[]{:S(2)}) collective-permute-start(bf16[8,4224]{1,0:T(8,128)(2,1)S(1)} %message.1), channel_id=1, source_target_pairs={{0,8},{1,9},{2,10},{3,11},{4,12},{5,13},{6,14},{7,15},{8,0},{9,1},... | collective-permute-start | bytes 202760 | tf_op jit(solution)/shard_map/ppermute | solution.py:27
  6.6 6.3 %collective-permute-start.2 = (bf16[8,4224]{1,0:T(8,128)(2,1)S(1)}, bf16[8,4224]{1,0:T(8,128)(2,1)S(1)}, u32[]{:S(2)}, u32[]{:S(2)}) collective-permute-start(bf16[8,4224]{1,0:T(8,128)(2,1)S(1)} %message.1), channel_id=1, source_target_pairs={{0,12},{1,13},{2,14},{3,15},{4,8},{5,9},{6,10},{7,11},{8,4},{9,5},... | collective-permute-start | bytes 202760 | tf_op jit(solution)/shard_map/ppermute | solution.py:27
  6.6 7.7 %collective-permute-start.3 = (bf16[8,4224]{1,0:T(8,128)(2,1)S(1)}, bf16[8,4224]{1,0:T(8,128)(2,1)S(1)}, u32[]{:S(2)}, u32[]{:S(2)}) collective-permute-start(bf16[8,4224]{1,0:T(8,128)(2,1)S(1)} %message.1), channel_id=1, source_target_pairs={{0,2},{1,3},{2,0},{3,1},{4,6},{5,7},{6,4},{7,5},{8,10},{9,11},{10,... | collective-permute-start | bytes 202760 | tf_op jit(solution)/shard_map/ppermute | solution.py:27
  8.3 6.0 %collective-permute-start.4 = (bf16[8,4224]{1,0:T(8,128)(2,1)S(1)}, bf16[8,4224]{1,0:T(8,128)(2,1)S(1)}, u32[]{:S(2)}, u32[]{:S(2)}) collective-permute-start(bf16[8,4224]{1,0:T(8,128)(2,1)S(1)} %collective-permute-done), channel_id=1, source_target_pairs={{0,2},{1,3},{2,0},{3,1},{4,6},{5,7},{6,4},{7,5},{8,10},{9,11},{10,... | collective-permute-start | bytes 202760 | tf_op jit(solution)/shard_map/ppermute | solution.py:27
  11.4 4.3 %collective-permute-start.5 = (bf16[8,4224]{1,0:T(8,128)(2,1)S(1)}, bf16[8,4224]{1,0:T(8,128)(2,1)S(1)}, u32[]{:S(2)}, u32[]{:S(2)}) collective-permute-start(bf16[8,4224]{1,0:T(8,128)(2,1)S(1)} %collective-permute-done.1), channel_id=1, source_target_pairs={{0,2},{1,3},{2,0},{3,1},{4,6},{5,7},{6,4},{7,5},{8,10},{9,11},{10,... | collective-permute-start | bytes 202760 | tf_op jit(solution)/shard_map/ppermute | solution.py:27
  12.9 4.3 %collective-permute-start.6 = (bf16[8,4224]{1,0:T(8,128)(2,1)S(1)}, bf16[8,4224]{1,0:T(8,128)(2,1)S(1)}, u32[]{:S(2)}, u32[]{:S(2)}) collective-permute-start(bf16[8,4224]{1,0:T(8,128)(2,1)S(1)} %collective-permute-done.2), channel_id=1, source_target_pairs={{0,2},{1,3},{2,0},{3,1},{4,6},{5,7},{6,4},{7,5},{8,10},{9,11},{10,... | collective-permute-start | bytes 202760 | tf_op jit(solution)/shard_map/ppermute | solution.py:27
  17.2 2.0 %collective-permute-start.7 = (bf16[64,4224]{1,0:T(8,128)(2,1)S(1)}, bf16[64,4224]{1,0:T(8,128)(2,1)S(1)}, u32[]{:S(2)}, u32[]{:S(2)}) collective-permute-start(bf16[64,4224]{1,0:T(8,128)(2,1)S(1)} %get-tuple-element.13), channel_id=1, source_target_pairs={{0,1},{1,0},{2,3},{3,2},{4,5},{5,4},{6,7},{7,6},{8,9},{9,8},{10,11... | collective-permute-start | bytes 1622024 | tf_op jit(solution)/shard_map/ppermute | solution.py:27
  44.6 2.0 %collective-permute-start.8 = (bf16[2,4,8,4096]{3,2,1,0:T(8,128)(2,1)S(1)}, bf16[2,4,8,4096]{3,2,1,0:T(8,128)(2,1)S(1)}, u32[]{:S(2)}, u32[]{:S(2)}) collective-permute-start(bf16[2,4,8,4096]{3,2,1,0:T(8,128)(2,1)S(1)} %bitcast.37), channel_id=1, source_target_pairs={{0,1},{1,0},{2,3},{3,2},{4,5},{5,4},{6,7},{7,6},{8,9},{9,8},{10,11... | collective-permute-start | bytes 1572872 | tf_op jit(solution)/shard_map/ppermute | solution.py:27
  46.7 8.2 %collective-permute-start.12 = (bf16[8,4096]{1,0:T(8,128)(2,1)S(1)}, bf16[8,4096]{1,0:T(8,128)(2,1)S(1)}, u32[]{:S(2)}, u32[]{:S(2)}) collective-permute-start(bf16[8,4096]{1,0:T(8,128)(2,1)S(1)} %get-tuple-element.10), channel_id=1, source_target_pairs={{0,12},{1,13},{2,14},{3,15},{4,8},{5,9},{6,10},{7,11},{8,4},{9,5},... | collective-permute-start | bytes 196616 | tf_op jit(solution)/shard_map/ppermute | solution.py:27
  50.0 6.8 %collective-permute-start.13 = (bf16[8,4096]{1,0:T(8,128)(2,1)S(1)}, bf16[8,4096]{1,0:T(8,128)(2,1)S(1)}, u32[]{:S(2)}, u32[]{:S(2)}) collective-permute-start(bf16[8,4096]{1,0:T(8,128)(2,1)S(1)} %get-tuple-element.9), channel_id=1, source_target_pairs={{0,8},{1,9},{2,10},{3,11},{4,12},{5,13},{6,14},{7,15},{8,0},{9,1},... | collective-permute-start | bytes 196616 | tf_op jit(solution)/shard_map/ppermute | solution.py:27
  50.0 6.8 %collective-permute-start.14 = (bf16[8,4096]{1,0:T(8,128)(2,1)S(1)}, bf16[8,4096]{1,0:T(8,128)(2,1)S(1)}, u32[]{:S(2)}, u32[]{:S(2)}) collective-permute-start(bf16[8,4096]{1,0:T(8,128)(2,1)S(1)} %get-tuple-element.8), channel_id=1, source_target_pairs={{0,4},{1,5},{2,6},{3,7},{4,0},{5,1},{6,2},{7,3},{8,12},{9,13},{10,... | collective-permute-start | bytes 196616 | tf_op jit(solution)/shard_map/ppermute | solution.py:27
  51.2 8.1 %collective-permute-start.10 = (bf16[8,4096]{1,0:T(8,128)(2,1)S(1)}, bf16[8,4096]{1,0:T(8,128)(2,1)S(1)}, u32[]{:S(2)}, u32[]{:S(2)}) collective-permute-start(bf16[8,4096]{1,0:T(8,128)(2,1)S(1)} %get-tuple-element.12), channel_id=1, source_target_pairs={{0,8},{1,9},{2,10},{3,11},{4,12},{5,13},{6,14},{7,15},{8,0},{9,1},... | collective-permute-start | bytes 196616 | tf_op jit(solution)/shard_map/ppermute | solution.py:27
  52.9 6.3 %collective-permute-start.11 = (bf16[8,4096]{1,0:T(8,128)(2,1)S(1)}, bf16[8,4096]{1,0:T(8,128)(2,1)S(1)}, u32[]{:S(2)}, u32[]{:S(2)}) collective-permute-start(bf16[8,4096]{1,0:T(8,128)(2,1)S(1)} %get-tuple-element.11), channel_id=1, source_target_pairs={{0,4},{1,5},{2,6},{3,7},{4,0},{5,1},{6,2},{7,3},{8,12},{9,13},{10,... | collective-permute-start | bytes 196616 | tf_op jit(solution)/shard_map/ppermute | solution.py:27
  54.9 6.2 %collective-permute-start.9 = (bf16[8,4096]{1,0:T(8,128)(2,1)S(1)}, bf16[8,4096]{1,0:T(8,128)(2,1)S(1)}, u32[]{:S(2)}, u32[]{:S(2)}) collective-permute-start(bf16[8,4096]{1,0:T(8,128)(2,1)S(1)} %get-tuple-element.7), channel_id=1, source_target_pairs={{0,12},{1,13},{2,14},{3,15},{4,8},{5,9},{6,10},{7,11},{8,4},{9,5},... | collective-permute-start | bytes 196616 | tf_op jit(solution)/shard_map/ppermute | solution.py:27
  56.8 4.3 %collective-permute-start.15 = (bf16[8,4096]{1,0:T(8,128)(2,1)S(1)}, bf16[8,4096]{1,0:T(8,128)(2,1)S(1)}, u32[]{:S(2)}, u32[]{:S(2)}) collective-permute-start(bf16[8,4096]{1,0:T(8,128)(2,1)S(1)} %fusion.3), channel_id=1, source_target_pairs={{0,2},{1,3},{2,0},{3,1},{4,6},{5,7},{6,4},{7,5},{8,10},{9,11},{10,... | collective-permute-start | bytes 196616 | tf_op jit(solution)/shard_map/ppermute | solution.py:27
